TPU v7x, 512 devices: a whole 4x8x8 slice. The times are simulated.
512 devices in a mesh: row: 16 (over x, y_hi), col: 16 (over z, core), depth: 2 (over y_lo).
Axes of the slice: x: 4, y: 8 (y_hi: 4, y_lo: 2; y = y_hi * 2 + y_lo), z: 8, core: 2. Of those that a mesh axis runs over, the one named last changes fastest.
Arguments:
- embeddings: bfloat16 [64, 32768], P(None, ('row', 'col', 'depth')), may hold values from -6 to 6
- coords: float32 [16, 32768], P(None, ('row', 'col', 'depth')), may hold values from -4 to 4
- pair_weight: bfloat16 [32768, 32768], P('row', ('col', 'depth')), may hold values from 0.0125 to 28.8, as said below
Outputs:
- new_coords: float32 [16, 32768], P(None, ('row', 'col', 'depth'))
- stress: float32 [], replicated
Inputs may be any that keep to these rules, and one draw needn't show every extreme that they name: `pair_weight`: every weight is positive.
All inputs are finite; a program needn't handle non-finite values.
Results may differ from a plain program's by a relative error of at most 0.00035.
Values may be sent and summed in bfloat16 or wider, within the bound.
No kernel may reach another device: no remote copies, remote signals or barrier semaphores. Data moves between devices by JAX's collectives and lax.ppermute only.
A program may use at most 64 MiB of HBM per device.

v0:
```python
import jax
import jax.numpy as jnp
from jax import lax
from jax.sharding import PartitionSpec as P


def broadcast(array, axis, root):
    mine = lax.axis_index(axis) == root
    return lax.psum(jnp.where(mine, array, jnp.zeros_like(array)), axis)


def block_terms(f_rows, x_rows, f_cols, x_cols, weights):
    hi = lax.Precision.HIGHEST
    fr = f_rows.astype(jnp.float32)
    fc = f_cols.astype(jnp.float32)
    fs_rows = jnp.sum(fr * fr, axis=0)
    fs_cols = jnp.sum(fc * fc, axis=0)
    xs_rows = jnp.sum(x_rows * x_rows, axis=0)
    xs_cols = jnp.sum(x_cols * x_cols, axis=0)
    gram_f = lax.dot_general(
        f_rows, f_cols, (((0,), (0,)), ((), ())), preferred_element_type=jnp.float32
    )
    dissim = jnp.sqrt(jnp.maximum(fs_rows[:, None] + fs_cols[None, :] - 2.0 * gram_f, 0.0)) / 8.0
    gram_x = lax.dot_general(
        x_rows, x_cols, (((0,), (0,)), ((), ())), precision=hi, preferred_element_type=jnp.float32
    )
    dist = jnp.sqrt(jnp.maximum(xs_rows[:, None] + xs_cols[None, :] - 2.0 * gram_x, 0.0))
    wfloat = weights.astype(jnp.float32)
    cmat = wfloat * dissim / jnp.maximum(dist, 1.0) - wfloat
    pull = lax.dot_general(
        x_cols, cmat, (((1,), (1,)), ((), ())), precision=hi, preferred_element_type=jnp.float32
    )
    rate = jnp.sum(cmat, axis=1)
    wsum = jnp.sum(wfloat, axis=1)
    misfit = jnp.sum(wfloat * (dissim - dist) ** 2, axis=1)
    scale = jnp.sum(wfloat * dissim * dissim, axis=1)
    return jnp.concatenate([pull, jnp.stack([rate, wsum, misfit, scale], axis=0)], axis=0)


def shards(embeddings, coords, pair_weight):
    f_rows = lax.all_gather(embeddings, ("col", "depth"), axis=1, tiled=True)
    x_rows = lax.all_gather(coords, ("col", "depth"), axis=1, tiled=True)
    rows = pair_weight.shape[0]
    cols = pair_weight.shape[1]
    depth_pos = lax.axis_index("depth")
    f_half = lax.dynamic_slice_in_dim(f_rows, depth_pos * cols, cols, 1)
    x_half = lax.dynamic_slice_in_dim(x_rows, depth_pos * cols, cols, 1)
    source = lax.axis_index("col")
    f_cols = broadcast(f_half, "row", source)
    x_cols = broadcast(x_half.astype(jnp.bfloat16), "row", source).astype(x_half.dtype)
    blk = min(512, rows)
    pieces = []
    for start in range(0, rows, blk):
        pieces.append(
            block_terms(
                f_rows[:, start : start + blk],
                x_rows[:, start : start + blk],
                f_cols,
                x_cols,
                pair_weight[start : start + blk],
            )
        )
    partial_value = jnp.concatenate(pieces, axis=1)
    shares = lax.psum_scatter(partial_value, ("col", "depth"), scatter_dimension=1, tiled=True)
    dims = coords.shape[0]
    pull = shares[:dims]
    rate = shares[dims]
    wsum = shares[dims + 1]
    new_coords = coords + (rate[None, :] * coords - pull) / wsum[None, :]
    misfit_all, scale_all = lax.psum(
        (jnp.sum(shares[dims + 2]), jnp.sum(shares[dims + 3])), ("row", "col", "depth")
    )
    return (new_coords, misfit_all / scale_all)


def solution(mesh):
    placed = (
        P(None, ("row", "col", "depth")),
        P(None, ("row", "col", "depth")),
        P("row", ("col", "depth")),
    )
    return jax.shard_map(
        shards,
        mesh=mesh,
        in_specs=placed,
        out_specs=(P(None, ("row", "col", "depth")), P()),
        check_vma=False,
    )
```

profile of v0, /device:TPU:1, one launch (start us, length us, event | category | flops | bytes accessed | tf_op | source)
XLA Modules:
  0.0 488.0 jit_solution(13569575596550404733)
XLA Ops:
  7.2 0.0 all-reduce.3.cloned.1.call-start
  7.2 0.8 copy.16
  8.0 64.6 %all_gather.7 = bf16[64,2048]{0,1:T(8,128)(2,1)S(1)} all-gather(bf16[64,64]{0,1:T(8,128)(2,1)S(1)} %copy.16), channel_id=1, replica_groups=mesh['row'=16,'col'=16,'depth'=2] {'col','depth'}, dimensions={1}, use_global_device_ids=true | all-gather | bytes 270336 | tf_op jit(solution)/shard_map/all_gather | solution.py:41
  72.6 0.8 dynamic-slice_select_fusion
  73.5 0.0 all-reduce.3.cloned.1.call-update
  73.5 0.0 reduce-scatter.4.cloned.1.call-start
  73.6 55.5 %all-gather = f32[32,64,16]{1,2,0:T(8,128)S(1)} all-gather(f32[1,64,16]{1,2,0:T(8,128)} %bitcast.109), channel_id=1, replica_groups=mesh['row'=16,'col'=16,'depth'=2] {'col','depth'}, dimensions={0}, use_global_device_ids=true | all-gather | bytes 135168 | tf_op jit(solution)/shard_map/all_gather | solution.py:42
  129.1 0.1 copy.14
  129.2 0.1 reshape.15
  129.3 0.0 copy-done
  129.3 70.1 %psum.28 = bf16[16,1024]{1,0:T(8,128)(2,1)S(1)} all-reduce(bf16[16,1024]{1,0:T(8,128)(2,1)S(1)} %fusion.41), channel_id=1, replica_groups=mesh['row'=16,'col'=16,'depth'=2] {'row'}, use_global_device_ids=true, to_apply=%region_0.1 | all-reduce | flops 16384 | bytes 65536 | tf_op jit(solution)/shard_map/psum | solution.py:9
  199.4 3.6 fusion.50
  203.0 2.3 copy.25
  205.4 1.4 copy.24
  206.8 3.0 fusion.17
  209.8 3.0 fusion.22
  212.8 1.3 copy.23
  214.2 3.0 fusion.27
  217.2 0.7 copy.22
  217.9 0.0 copy-start.4
  217.9 3.1 fusion.32
  220.9 0.0 copy-done.1
  220.9 0.4 multiply_reduce_fusion.4
  221.3 11.2 %all-reduce.3.cloned.1.call-done = bf16[64,1024]{0,1:T(8,128)(2,1)} async-done(((bf16[64,1024]{0,1:T(8,128)(2,1)}), bf16[64,1024]{0,1:T(8,128)(2,1)}) %all-reduce.3.cloned.1.call-update) | async-done | bytes 131088 | tf_op jit(solution)/shard_map/psum | solution.py:9
  232.5 1.2 multiply_reduce_fusion
  233.7 0.0 copy-done.4
  233.7 0.0 copy-start.9
  233.7 3.8 fusion.8
  237.5 0.8 fusion.54
  238.3 0.4 copy-done.3
  238.7 0.0 copy-done.5
  238.8 2.0 fusion.9
  240.7 0.8 fusion.53
  241.5 0.4 copy-done.2
  242.0 2.0 fusion.10
  243.9 0.8 fusion.52
  244.7 0.8 copy-done.7
  245.5 2.0 fusion.11
  247.5 0.8 fusion.51
  248.4 1.4 copy.20
  249.8 0.0 reduce-scatter.4.cloned.1.call-update
  249.8 127.9 %reduce-scatter.4.cloned.1.call-done = f32[64,20]{1,0:T(8,128)} async-done(((f32[2048,20]{1,0:T(8,128)}), f32[64,20]{1,0:T(8,128)}) %reduce-scatter.4.cloned.1.call-update) | async-done | bytes 5136
  377.7 1.6 slice_reduce_fusion
  379.4 0.8 copy.27
  380.2 0.1 copy.28
  380.2 0.1 copy.26
  380.3 97.8 %all-reduce = (f32[]{:T(128)}, f32[]{:T(128)}) all-reduce(f32[]{:T(128)} %get-tuple-element.23, f32[]{:T(128)} %get-tuple-element.22), channel_id=1, replica_groups=mesh['row'=16,'col'=16,'depth'=2] {'row','col','depth'}, use_global_device_ids=true, to_apply=%region_30.31 | all-reduce | flops 2 | bytes 16 | tf_op jit(solution)/shard_map/psum | solution.py:70
  479.4 0.6 divide_add_fusion
  (19 shorter events, 0.2 us)
Async XLA Ops:
  7.2 225.4 %all-reduce.3.cloned.1.call-start = ((), (), s32[]{:S(2)}) async-start(), calls=%async_computation.1 | async-start | bytes 524288 | tf_op jit(solution)/shard_map/psum | solution.py:9
  72.6 56.7 %copy-start = (bf16[64,2048]{0,1:T(8,128)(2,1)}, bf16[64,2048]{0,1:T(8,128)(2,1)S(1)}, u32[]{:S(2)}) copy-start(bf16[64,2048]{0,1:T(8,128)(2,1)S(1)} %all_gather.7) | copy-start | bytes 786436
  73.5 304.2 %reduce-scatter.4.cloned.1.call-start = ((), (), s32[]{:S(2)}) async-start(), calls=%async_computation.2 | async-start | bytes 1081344
  217.2 3.8 copy-start.1
  217.9 15.8 %copy-start.4 = (bf16[512,1024]{0,1:T(8,128)(2,1)S(1)}, bf16[512,1024]{0,1:T(8,128)(2,1)}, u32[]{:S(2)}) copy-start(bf16[512,1024]{0,1:T(8,128)(2,1)} %copy.25) | copy-start | bytes 3145732
  233.7 4.6 copy-start.9
  237.5 1.2 copy-start.3
  237.5 1.3 copy-start.5
  238.8 2.8 copy-start.8
  240.7 1.2 copy-start.2
  243.9 1.6 copy-start.7
  248.3 231.2 %copy-start.6 = (f32[16,64]{1,0:T(8,128)S(1)}, f32[16,64]{1,0:T(8,128)}, u32[]{:S(2)}) copy-start(f32[16,64]{1,0:T(8,128)} %param.4) | copy-start | bytes 12292
Sparse Core Ops, SparseCore 0:
  73.6 158.8 all-reduce.2
  249.9 127.7 reduce-scatter.3
where the time goes:
time: 489 us; the launch traced here: 488 us
  blocking collectives  288 us (59%)
  waiting for transfers between devices  139 us (28%)
  matrix products  25 us (5%)
  between operations  16.7 us (3%)
  local copies, waits for them, and re-layouts  14.5 us (3%)
    unnamed x3, waiting for transfers between devices  128 us
    psum x1, blocking collectives, shards(): lax.psum((jnp.sum(shares[dims + 2]), jnp.sum(shares[dims + 3])), ('row',...  97.8 us
    psum x1, blocking collectives, broadcast(): return lax.psum(jnp.where(mine, array, jnp.zeros_like(array)), axis)  70.1 us
    all_gather x1, blocking collectives, shards(): f_rows = lax.all_gather(embeddings, ('col', 'depth'), axis=1, tiled=True)  64.6 us
    all_gather x1, blocking collectives, shards(): x_rows = lax.all_gather(coords, ('col', 'depth'), axis=1, tiled=True)  55.5 us
    dot_general x4, matrix products, block_terms(): lax.dot_general(x_rows, x_cols, (((0,), (0,)), ((), ())), precision=hi, p...  12.1 us
    psum x1, waiting for transfers between devices, broadcast(): return lax.psum(jnp.where(mine, array, jnp.zeros_like(array)), axis)  11.2 us
    unnamed x30, local copies, waits for them, and re-layouts  10.6 us
  transfers between devices with their start and end apart: 2, of which 2 were waited for; matrix products, arithmetic and copies ran while one was open for 5% of the time, Pallas kernels for 0%

commit v1 on v0

v1 whole, which is shorter than its diff:
```python
import jax
import jax.numpy as jnp
from jax import lax
from jax.experimental import pallas as pl
from jax.experimental.pallas import tpu as pltpu
from jax.sharding import PartitionSpec as P

F32 = jnp.float32
BF16 = jnp.bfloat16

EMB, XH, XL, XH2, QF, QX, ONE, LANES = 0, 64, 80, 96, 112, 115, 118, 128
TINY = 1e-30


def bilinear_form(kind):
    a = lax.broadcasted_iota(jnp.int32, (LANES, LANES), 0)
    b = lax.broadcasted_iota(jnp.int32, (LANES, LANES), 1)

    def band(first, count, shift):
        return (a >= first) & (a < first + count) & (b == a + shift)

    if kind == 0:
        cross = band(EMB, 64, 0)
        square, unit = QF, 1.0 / 64.0
    else:
        cross = band(XH, 16, 0) | band(XL, 16, XH2 - XL) | band(XH2, 16, XL - XH2)
        square, unit = QX, 1.0
    norms = band(square, 3, ONE - square) | band(ONE, 3, square - ONE)
    return jnp.where(cross, -2.0 * unit, jnp.where(norms, unit, 0.0)).astype(BF16)


def split3(value):
    hi = value.astype(BF16).astype(F32)
    mid = (value - hi).astype(BF16).astype(F32)
    low = (value - hi - mid).astype(BF16).astype(F32)
    return hi, mid, low


def pack_kernel(emb_ref, crd_ref, own_ref, out_ref):
    emb = emb_ref[...].astype(F32)
    crd = crd_ref[...]
    points = emb.shape[1]
    hi = crd.astype(BF16).astype(F32)
    low = (crd - hi).astype(BF16).astype(F32)
    squares = split3(jnp.sum(emb * emb, axis=0, keepdims=True))
    squares += split3(jnp.sum(crd * crd, axis=0, keepdims=True))
    lane = lax.broadcasted_iota(jnp.int32, (16, points), 0)
    tail = jnp.where((lane >= ONE - QF) & (lane < ONE - QF + 3), 1.0, 0.0)
    for k, sq in enumerate(squares):
        tail = jnp.where(lane == k, sq, tail)
    rows = jnp.concatenate([emb, hi, low, hi, tail], axis=0)
    mine = rows.T.astype(BF16)
    own_ref[...] = mine
    for k in range(out_ref.shape[0]):
        out_ref[k] = mine


def pairs_kernel(row_ref, col_ref, w_hbm, out_ref, w_ref, f_scr, x_scr, sems):
    total_rows = row_ref.shape[0]
    total = col_ref.shape[0]
    tm = min(256, total_rows)
    tn = min(256, total)
    per = tm // 64
    steps = total_rows // tm

    def fetch(i):
        at = pl.ds(i * tm, tm)
        return pltpu.make_async_copy(w_hbm.at[at, :], w_ref.at[at, :], sems.at[i])

    for i in range(steps):
        fetch(i).start()
    all_cols = col_ref[...]
    dims = (((1,), (1,)), ((), ()))
    form_f = bilinear_form(0)
    f_scr[...] = lax.dot_general(form_f, all_cols, dims, preferred_element_type=F32).astype(BF16)
    x_scr[...] = lax.dot_general(bilinear_form(1), all_cols, dims, preferred_element_type=F32).astype(BF16)
    lane = lax.broadcasted_iota(jnp.int32, (tm, LANES), 1)

    def block(i, carry):
        mis, scl = carry
        fetch(i).wait()
        at = pl.ds(pl.multiple_of(i * tm, tm), tm)
        rows = row_ref[at, :]
        acc = jnp.zeros((tm, LANES), F32)
        wacc = jnp.zeros((tm, LANES), F32)
        for start in range(0, total, tn):
            cut = slice(start, start + tn)
            f2 = jnp.dot(rows, f_scr[:, cut], preferred_element_type=F32)
            x2 = jnp.dot(rows, x_scr[:, cut], preferred_element_type=F32)
            wb = w_ref[at, cut]
            w = wb.astype(F32)
            f2 = jnp.maximum(f2, TINY)
            x2 = jnp.maximum(x2, TINY)
            dissim = f2 * lax.rsqrt(f2)
            inv = lax.rsqrt(x2)
            diff = dissim - x2 * inv
            cmat = w * (dissim * jnp.minimum(inv, 1.0) - 1.0)
            mis += jnp.sum((w * (diff * diff)).reshape(tm // 8, 8, tn), axis=0)
            cols = col_ref[cut, :]
            acc += jnp.dot(cmat.astype(BF16), cols, preferred_element_type=F32)
            wacc += jnp.dot(wb, cols, preferred_element_type=F32)
        bent = jnp.dot(rows, form_f, preferred_element_type=F32)
        scl += jnp.sum((bent * wacc).reshape(tm // 8, 8, LANES), axis=0)
        sums = jnp.where(lane == ONE + 1, wacc, acc).T
        pull = sums[XH : XH + 16] + sums[XL : XL + 16]
        rate = sums[ONE : ONE + 1]
        wsum = sums[ONE + 1 : ONE + 2]
        for k in range(per):
            cut = slice(64 * k, 64 * k + 64)
            out_ref[i * per + k, 0:8, :] = jnp.concatenate([pull[0:8, cut], pull[8:16, cut]], axis=1)
            out_ref[i * per + k, 8:9, :] = jnp.concatenate([rate[:, cut], wsum[:, cut]], axis=1)
        return mis, scl

    mis, scl = lax.fori_loop(
        0, steps, block, (jnp.zeros((8, tn), F32), jnp.zeros((8, LANES), F32))
    )
    mis = jnp.sum(mis, axis=0, keepdims=True)
    mis = sum(mis[:, k : k + 128] for k in range(0, tn, 128))
    scl = jnp.sum(scl, axis=0, keepdims=True)
    count = out_ref.shape[0]
    out_ref[:, 9:10, :] = jnp.broadcast_to(mis[None], (count, 1, 128))
    out_ref[:, 10:11, :] = jnp.broadcast_to(scl[None], (count, 1, 128))
    out_ref[:, 11:16, :] = jnp.zeros((count, 5, 128), F32)


def finish_kernel(part_ref, crd_ref, new_ref, share_ref):
    sums = jnp.sum(part_ref[...], axis=0)
    rate = sums[8:9, 0:64]
    wsum = sums[8:9, 64:128]
    pull = jnp.concatenate([sums[0:8, 0:64], sums[0:8, 64:128]], axis=0)
    crd = crd_ref[...]
    new_ref[...] = crd + (rate * crd - pull) / wsum
    share_ref[...] = jnp.broadcast_to(sums[8:16][None], share_ref.shape)


def stress_kernel(part_ref, out_ref):
    sums = jnp.sum(part_ref[...], axis=0)
    out_ref[...] = jnp.sum(sums[1:2], axis=1, keepdims=True) / jnp.sum(sums[2:3], axis=1, keepdims=True)


def column_moves(n_row, n_col, n_depth):
    moves = []
    for row in range(n_row):
        for at in range(n_col * n_depth):
            moves.append((row * n_col * n_depth + at, (at % n_row * n_col + row) * n_depth + at // n_row))
    return moves


def shards(embeddings, coords, pair_weight):
    rows, cols = pair_weight.shape
    points = embeddings.shape[1]
    group = rows // points
    n_row, n_col, n_depth = (lax.axis_size(a) for a in ("row", "col", "depth"))

    packed = pl.pallas_call(
        pack_kernel,
        out_shape=(
            jax.ShapeDtypeStruct((points, LANES), BF16),
            jax.ShapeDtypeStruct((group, points, LANES), BF16),
        ),
        name="pack",
    )(embeddings, coords)
    moved = lax.ppermute(packed[0], ("row", "col", "depth"), column_moves(n_row, n_col, n_depth))
    t_rows = lax.all_to_all(packed[1], ("col", "depth"), 0, 0, tiled=True).reshape(rows, LANES)
    moved = jnp.broadcast_to(moved[None], (n_row, points, LANES))
    t_cols = lax.all_to_all(moved, "row", 0, 0, tiled=True).reshape(cols, LANES)

    vmem = pl.BlockSpec(memory_space=pltpu.VMEM)
    parts = pl.pallas_call(
        pairs_kernel,
        in_specs=[vmem, vmem, pl.BlockSpec(memory_space=pltpu.HBM)],
        out_specs=vmem,
        out_shape=jax.ShapeDtypeStruct((group, 16, 128), F32),
        scratch_shapes=[
            pltpu.VMEM((rows, cols), BF16),
            pltpu.VMEM((LANES, cols), BF16),
            pltpu.VMEM((LANES, cols), BF16),
            pltpu.SemaphoreType.DMA((max(1, rows // 256),)),
        ],
        compiler_params=pltpu.CompilerParams(vmem_limit_bytes=60 * 1024 * 1024),
        name="pairs",
    )(t_rows, t_cols, pair_weight)
    parts = lax.all_to_all(parts, ("col", "depth"), 0, 0, tiled=True)
    new_coords, shares = pl.pallas_call(
        finish_kernel,
        out_shape=(
            jax.ShapeDtypeStruct(coords.shape, F32),
            jax.ShapeDtypeStruct((n_row, 8, 128), F32),
        ),
        name="finish",
    )(parts, coords)
    shares = lax.all_to_all(shares, "row", 0, 0, tiled=True)
    stress = pl.pallas_call(
        stress_kernel,
        out_shape=jax.ShapeDtypeStruct((1, 1), F32),
        name="stress",
    )(shares)
    return (new_coords, stress[0, 0])


def solution(mesh):
    placed = (
        P(None, ("row", "col", "depth")),
        P(None, ("row", "col", "depth")),
        P("row", ("col", "depth")),
    )
    return jax.shard_map(
        shards,
        mesh=mesh,
        in_specs=placed,
        out_specs=(P(None, ("row", "col", "depth")), P()),
        check_vma=False,
    )
```

time: 489 us -> 116 us (0.24)
  blocking collectives: 288 us -> 85.7 us
  waiting for transfers between devices: 139 us -> 1.06 us
  matrix products: 25 us -> 0 us
  Pallas kernels: 0 us -> 18.1 us
  between operations: 16.7 us -> 0.66 us
  local copies, waits for them, and re-layouts: 14.5 us -> 0.04 us
  starting transfers between devices: 0.08 us -> 8.83 us
    psum x2 -> x0, blocking collectives: 168 us -> none  [the longest x1 97.8 us: shards(): lax.psum((jnp.sum(shares[dims + 2]), jnp.sum(shares[dims + 3])), ('row',...]
    unnamed x3 -> x0, waiting for transfers between devices: 128 us -> none
    all_gather x2 -> x0, blocking collectives: 120 us -> none  [the longest x1 64.6 us: shards(): f_rows = lax.all_gather(embeddings, ('col', 'depth'), axis=1, tiled=True)]
    all_to_all x0 -> x4, blocking collectives: none -> 85.7 us  [the longest x1 30.5 us: shards(): lax.all_to_all(packed[1], ('col', 'depth'), 0, 0, tiled=True)]
    dot_general x12 -> x0, matrix products: 25 us -> none  [the longest x4 12.1 us: block_terms(): lax.dot_general(x_rows, x_cols, (((0,), (0,)), ((), ())), precision=hi, p...]
    pallas_call x0 -> x4, Pallas kernels: none -> 18.1 us  [the longest x1 13.3 us: shards(): pl.pallas_call(pairs_kernel, in_specs=[vmem, vmem, pl.BlockSpec(memory_sp...]
    psum x1 -> x0, waiting for transfers between devices: 11.2 us -> none  [broadcast(): return lax.psum(jnp.where(mine, array, jnp.zeros_like(array)), axis)]
    unnamed x30 -> x0, local copies, waits for them, and re-layouts: 10.6 us -> none
  transfers between devices with their start and end apart: 2 -> 1, of which waited for: 2 -> 1; matrix products, arithmetic and copies ran while one was open for 5% -> 0% of each run, Pallas kernels for 0% -> 0%
where the time goes in v1:
time: 116 us; the launch traced here: 114 us
  blocking collectives  85.7 us (74%)
  Pallas kernels  18.1 us (16%)
  starting transfers between devices  8.83 us (8%)
    all_to_all x1, blocking collectives, shards(): lax.all_to_all(packed[1], ('col', 'depth'), 0, 0, tiled=True)  30.5 us
    all_to_all x1, blocking collectives, shards(): t_cols = lax.all_to_all(moved, 'row', 0, 0, tiled=True).reshape(cols, LANES)  24.5 us
    all_to_all x1, blocking collectives, shards(): parts = lax.all_to_all(parts, ('col', 'depth'), 0, 0, tiled=True)  17.2 us
    all_to_all x1, blocking collectives, shards(): shares = lax.all_to_all(shares, 'row', 0, 0, tiled=True)  13.4 us
    pallas_call x1, Pallas kernels, shards(): pl.pallas_call(pairs_kernel, in_specs=[vmem, vmem, pl.BlockSpec(memory_sp...  13.3 us
    ppermute x1, starting transfers between devices, shards(): lax.ppermute(packed[0], ('row', 'col', 'depth'), column_moves(n_row, n_co...  8.83 us
  transfers between devices with their start and end apart: 1, of which 1 were waited for; matrix products, arithmetic and copies ran while one was open for 0% of the time, Pallas kernels for 0%

profile of v1, /device:TPU:1, one launch (start us, length us, event | category | flops | bytes accessed | tf_op | source)
XLA Modules:
  0.0 114.4 jit_solution(13611599926805985513)
XLA Ops:
  0.6 1.6 %pack.1 = (bf16[64,128]{1,0:T(8,128)(2,1)}, bf16[32,64,128]{2,1,0:T(8,128)(2,1)}) custom-call(bf16[64,64]{1,0:T(8,128)(2,1)} %emb_ref.1, f32[16,64]{1,0:T(8,128)} %crd_ref.3), custom_call_target="tpu_custom_call" | custom-call | tf_op jit(solution)/shard_map/pack/pallas_call | solution.py:155
  2.3 8.8 %collective-permute-start = (bf16[64,128]{1,0:T(8,128)(2,1)}, bf16[64,128]{1,0:T(8,128)(2,1)S(1)}, u32[]{:S(2)}, u32[]{:S(2)}) collective-permute-start(bf16[64,128]{1,0:T(8,128)(2,1)} %get-tuple-element.7), channel_id=1, source_target_pairs={{0,0},{1,32},{2,64},{3,96},{4,128},{5,160},{6,192},{7,224},{8,256}... | collective-permute-start | bytes 49160 | tf_op jit(solution)/shard_map/ppermute | solution.py:163
  11.1 1.1 collective-permute-done
  12.2 24.5 %all_to_all.20 = bf16[16,64,128]{2,1,0:T(8,128)(2,1)} all-to-all(bf16[16,64,128]{2,1,0:T(8,128)(2,1)S(1)} %broadcast_in_dim.2), channel_id=1, replica_groups=mesh['row'=16,'col'=16,'depth'=2] {'row'}, dimensions={0} | all-to-all | bytes 524288 | tf_op jit(solution)/shard_map/all_to_all | solution.py:166
  36.7 30.5 %all_to_all.21 = bf16[32,64,128]{2,1,0:T(8,128)(2,1)} all-to-all(bf16[32,64,128]{2,1,0:T(8,128)(2,1)} %get-tuple-element.6), channel_id=1, replica_groups=mesh['row'=16,'col'=16,'depth'=2] {'col','depth'}, dimensions={0} | all-to-all | bytes 1048576 | tf_op jit(solution)/shard_map/all_to_all | solution.py:164
  67.3 13.3 %pairs.1 = f32[32,16,128]{2,1,0:T(8,128)} custom-call(bf16[2048,128]{1,0:T(8,128)(2,1)} %bitcast.3, bf16[1024,128]{1,0:T(8,128)(2,1)} %bitcast.4, bf16[2048,1024]{1,0:T(8,128)(2,1)} %w_hbm.1), custom_call_target="tpu_custom_call" | custom-call | tf_op jit(solution)/shard_map/pairs/pallas_call | solution.py:169
  80.6 17.2 %all_to_all.22.part_ref = f32[32,16,128]{2,1,0:T(8,128)} all-to-all(f32[32,16,128]{2,1,0:T(8,128)} %pairs.1), channel_id=1, replica_groups=mesh['row'=16,'col'=16,'depth'=2] {'col','depth'}, dimensions={0} | all-to-all | bytes 524288 | tf_op jit(solution)/shard_map/all_to_all | solution.py:183
  97.9 1.7 %finish.1 = (f32[16,64]{1,0:T(8,128)}, f32[16,8,128]{2,1,0:T(8,128)}) custom-call(f32[32,16,128]{2,1,0:T(8,128)} %all_to_all.22.part_ref, f32[16,64]{1,0:T(8,128)} %crd_ref.3), custom_call_target="tpu_custom_call" | custom-call | tf_op jit(solution)/shard_map/finish/pallas_call | solution.py:184
  99.5 13.4 %all_to_all.23.part_ref = f32[16,8,128]{2,1,0:T(8,128)} all-to-all(f32[16,8,128]{2,1,0:T(8,128)} %get-tuple-element.9), channel_id=1, replica_groups=mesh['row'=16,'col'=16,'depth'=2] {'row'}, dimensions={0} | all-to-all | bytes 131072 | tf_op jit(solution)/shard_map/all_to_all | solution.py:192
  112.9 1.4 %stress.1 = f32[1,1]{1,0:T(1,128)} custom-call(f32[16,8,128]{2,1,0:T(8,128)} %all_to_all.23.part_ref), custom_call_target="tpu_custom_call" | custom-call | tf_op jit(solution)/shard_map/stress/pallas_call | solution.py:193
  (1 shorter events, 0.0 us)
Async XLA Ops:
  2.3 9.9 %collective-permute-start = (bf16[64,128]{1,0:T(8,128)(2,1)}, bf16[64,128]{1,0:T(8,128)(2,1)S(1)}, u32[]{:S(2)}, u32[]{:S(2)}) collective-permute-start(bf16[64,128]{1,0:T(8,128)(2,1)} %get-tuple-element.7), channel_id=1, source_target_pairs={{0,0},{1,32},{2,64},{3,96},{4,128},{5,160},{6,192},{7,224},{8,256}... | collective-permute-start | bytes 49160 | tf_op jit(solution)/shard_map/ppermute | solution.py:163

commit v2 on v1

--- a/solution.py
+++ b/solution.py
@@ -58,7 +58,7 @@
 def pairs_kernel(row_ref, col_ref, w_hbm, out_ref, w_ref, f_scr, x_scr, sems):
     total_rows = row_ref.shape[0]
     total = col_ref.shape[0]
-    tm = min(256, total_rows)
+    tm = min(512, total_rows)
     tn = min(256, total)
     per = tm // 64
     steps = total_rows // tm
@@ -162,6 +162,7 @@
     )(embeddings, coords)
     moved = lax.ppermute(packed[0], ("row", "col", "depth"), column_moves(n_row, n_col, n_depth))
     t_rows = lax.all_to_all(packed[1], ("col", "depth"), 0, 0, tiled=True).reshape(rows, LANES)
+    moved, t_rows = lax.optimization_barrier((moved, t_rows))
     moved = jnp.broadcast_to(moved[None], (n_row, points, LANES))
     t_cols = lax.all_to_all(moved, "row", 0, 0, tiled=True).reshape(cols, LANES)
 
@@ -175,9 +176,9 @@
             pltpu.VMEM((rows, cols), BF16),
             pltpu.VMEM((LANES, cols), BF16),
             pltpu.VMEM((LANES, cols), BF16),
-            pltpu.SemaphoreType.DMA((max(1, rows // 256),)),
+            pltpu.SemaphoreType.DMA((max(1, rows // 512),)),
         ],
-        compiler_params=pltpu.CompilerParams(vmem_limit_bytes=60 * 1024 * 1024),
+        compiler_params=pltpu.CompilerParams(vmem_limit_bytes=57 * 1024 * 1024),
         name="pairs",
     )(t_rows, t_cols, pair_weight)
     parts = lax.all_to_all(parts, ("col", "depth"), 0, 0, tiled=True)

time: 116 us -> 100 us (0.86)
  blocking collectives: 85.7 us -> 52.6 us
  starting transfers between devices: 8.83 us -> 19.7 us
  waiting for transfers between devices: 1.06 us -> 10.2 us
  Pallas kernels: 18.1 us -> 15.9 us
    all_to_all x1 -> x0, blocking collectives: 30.5 us -> none  [shards(): lax.all_to_all(packed[1], ('col', 'depth'), 0, 0, tiled=True)]
    all_to_all x0 -> x1, starting transfers between devices: none -> 13 us  [shards(): lax.all_to_all(packed[1], ('col', 'depth'), 0, 0, tiled=True)]
    all_to_all x0 -> x1, waiting for transfers between devices: none -> 9.09 us  [shards(): lax.all_to_all(packed[1], ('col', 'depth'), 0, 0, tiled=True)]
    all_to_all x1, blocking collectives: 24.5 us -> 20 us  [shards(): t_cols = lax.all_to_all(moved, 'row', 0, 0, tiled=True).reshape(cols, LANES)]
    ppermute x1, starting transfers between devices: 8.83 us -> 6.67 us  [shards(): lax.ppermute(packed[0], ('row', 'col', 'depth'), column_moves(n_row, n_co...]
    pallas_call x1, Pallas kernels: 13.3 us -> 11.2 us  [shards(): pl.pallas_call(pairs_kernel, in_specs=[vmem, vmem, pl.BlockSpec(memory_sp...]
    all_to_all x1, blocking collectives: 17.2 us -> 19.3 us  [shards(): parts = lax.all_to_all(parts, ('col', 'depth'), 0, 0, tiled=True)]
  transfers between devices with their start and end apart: 1 -> 2, of which waited for: 1 -> 2; matrix products, arithmetic and copies ran while one was open for 0% -> 0% of each run, Pallas kernels for 0% -> 0%
where the time goes in v2:
time: 100 us; the launch traced here: 99 us
  blocking collectives  52.6 us (53%)
  starting transfers between devices  19.7 us (20%)
  Pallas kernels  15.9 us (16%)
  waiting for transfers between devices  10.2 us (10%)
    all_to_all x1, blocking collectives, shards(): t_cols = lax.all_to_all(moved, 'row', 0, 0, tiled=True).reshape(cols, LANES)  20 us
    all_to_all x1, blocking collectives, shards(): parts = lax.all_to_all(parts, ('col', 'depth'), 0, 0, tiled=True)  19.3 us
    all_to_all x1, blocking collectives, shards(): shares = lax.all_to_all(shares, 'row', 0, 0, tiled=True)  13.2 us
    all_to_all x1, starting transfers between devices, shards(): lax.all_to_all(packed[1], ('col', 'depth'), 0, 0, tiled=True)  13 us
    pallas_call x1, Pallas kernels, shards(): pl.pallas_call(pairs_kernel, in_specs=[vmem, vmem, pl.BlockSpec(memory_sp...  11.2 us
    all_to_all x1, waiting for transfers between devices, shards(): lax.all_to_all(packed[1], ('col', 'depth'), 0, 0, tiled=True)  9.09 us
    ppermute x1, starting transfers between devices, shards(): lax.ppermute(packed[0], ('row', 'col', 'depth'), column_moves(n_row, n_co...  6.67 us
  transfers between devices with their start and end apart: 2, of which 2 were waited for; matrix products, arithmetic and copies ran while one was open for 0% of the time, Pallas kernels for 0%

profile of v2, /device:TPU:1, one launch (start us, length us, event | category | flops | bytes accessed | tf_op | source)
XLA Modules:
  0.0 99.0 jit_solution(12429058651917425259)
XLA Ops:
  0.6 1.6 %pack.1 = (bf16[64,128]{1,0:T(8,128)(2,1)}, bf16[32,64,128]{2,1,0:T(8,128)(2,1)}) custom-call(bf16[64,64]{1,0:T(8,128)(2,1)} %emb_ref.1, f32[16,64]{1,0:T(8,128)} %crd_ref.3), custom_call_target="tpu_custom_call" | custom-call | tf_op jit(solution)/shard_map/pack/pallas_call | solution.py:155
  2.3 13.0 %all-to-all-start = ((bf16[32,64,128]{2,1,0:T(8,128)(2,1)}), bf16[32,64,128]{2,1,0:T(8,128)(2,1)S(1)}, u32[]{:S(2)}, u32[]{:S(2)}) async-start(bf16[32,64,128]{2,1,0:T(8,128)(2,1)} %get-tuple-element.9), calls=%async_computation | async-start | bytes 1048576 | tf_op jit(solution)/shard_map/all_to_all | solution.py:164
  15.3 6.7 %collective-permute-start = (bf16[64,128]{1,0:T(8,128)(2,1)}, bf16[64,128]{1,0:T(8,128)(2,1)S(1)}, u32[]{:S(2)}, u32[]{:S(2)}) collective-permute-start(bf16[64,128]{1,0:T(8,128)(2,1)} %get-tuple-element.8), channel_id=1, source_target_pairs={{0,0},{1,32},{2,64},{3,96},{4,128},{5,160},{6,192},{7,224},{8,256}... | collective-permute-start | bytes 49160 | tf_op jit(solution)/shard_map/ppermute | solution.py:163
  21.9 1.1 %collective-permute-done = bf16[64,128]{1,0:T(8,128)(2,1)S(1)} collective-permute-done((bf16[64,128]{1,0:T(8,128)(2,1)}, bf16[64,128]{1,0:T(8,128)(2,1)S(1)}, u32[]{:S(2)}, u32[]{:S(2)}) %collective-permute-start) | collective-permute-done | bytes 16416 | tf_op jit(solution)/shard_map/ppermute | solution.py:163
  23.0 9.1 %all-to-all-done = bf16[32,64,128]{2,1,0:T(8,128)(2,1)S(1)} async-done(((bf16[32,64,128]{2,1,0:T(8,128)(2,1)}), bf16[32,64,128]{2,1,0:T(8,128)(2,1)S(1)}, u32[]{:S(2)}, u32[]{:S(2)}) %all-to-all-start) | async-done | bytes 524320 | tf_op jit(solution)/shard_map/all_to_all | solution.py:164
  32.1 0.0 copy-start
  32.2 20.0 %all_to_all.20 = bf16[16,64,128]{2,1,0:T(8,128)(2,1)} all-to-all(bf16[16,64,128]{2,1,0:T(8,128)(2,1)S(1)} %broadcast_in_dim.2), channel_id=1, replica_groups=mesh['row'=16,'col'=16,'depth'=2] {'row'}, dimensions={0} | all-to-all | bytes 524288 | tf_op jit(solution)/shard_map/all_to_all | solution.py:167
  52.1 0.0 copy-done
  52.2 11.2 %pairs.1 = f32[32,16,128]{2,1,0:T(8,128)} custom-call(bf16[2048,128]{1,0:T(8,128)(2,1)} %bitcast.3, bf16[1024,128]{1,0:T(8,128)(2,1)} %bitcast.4, bf16[2048,1024]{1,0:T(8,128)(2,1)} %w_hbm.1), custom_call_target="tpu_custom_call" | custom-call | tf_op jit(solution)/shard_map/pairs/pallas_call | solution.py:170
  63.3 19.3 %all_to_all.21.part_ref = f32[32,16,128]{2,1,0:T(8,128)} all-to-all(f32[32,16,128]{2,1,0:T(8,128)} %pairs.1), channel_id=1, replica_groups=mesh['row'=16,'col'=16,'depth'=2] {'col','depth'}, dimensions={0} | all-to-all | bytes 524288 | tf_op jit(solution)/shard_map/all_to_all | solution.py:184
  82.7 1.7 %finish.1 = (f32[16,64]{1,0:T(8,128)}, f32[16,8,128]{2,1,0:T(8,128)}) custom-call(f32[32,16,128]{2,1,0:T(8,128)} %all_to_all.21.part_ref, f32[16,64]{1,0:T(8,128)} %crd_ref.3), custom_call_target="tpu_custom_call" | custom-call | tf_op jit(solution)/shard_map/finish/pallas_call | solution.py:185
  84.3 13.2 %all_to_all.22.part_ref = f32[16,8,128]{2,1,0:T(8,128)} all-to-all(f32[16,8,128]{2,1,0:T(8,128)} %get-tuple-element.13), channel_id=1, replica_groups=mesh['row'=16,'col'=16,'depth'=2] {'row'}, dimensions={0} | all-to-all | bytes 131072 | tf_op jit(solution)/shard_map/all_to_all | solution.py:193
  97.6 1.4 %stress.1 = f32[1,1]{1,0:T(1,128)} custom-call(f32[16,8,128]{2,1,0:T(8,128)} %all_to_all.22.part_ref), custom_call_target="tpu_custom_call" | custom-call | tf_op jit(solution)/shard_map/stress/pallas_call | solution.py:194
  (1 shorter events, 0.0 us)
Async XLA Ops:
  2.3 29.8 %all-to-all-start = ((bf16[32,64,128]{2,1,0:T(8,128)(2,1)}), bf16[32,64,128]{2,1,0:T(8,128)(2,1)S(1)}, u32[]{:S(2)}, u32[]{:S(2)}) async-start(bf16[32,64,128]{2,1,0:T(8,128)(2,1)} %get-tuple-element.9), calls=%async_computation | async-start | bytes 1048576 | tf_op jit(solution)/shard_map/all_to_all | solution.py:164
  15.3 7.7 %collective-permute-start = (bf16[64,128]{1,0:T(8,128)(2,1)}, bf16[64,128]{1,0:T(8,128)(2,1)S(1)}, u32[]{:S(2)}, u32[]{:S(2)}) collective-permute-start(bf16[64,128]{1,0:T(8,128)(2,1)} %get-tuple-element.8), channel_id=1, source_target_pairs={{0,0},{1,32},{2,64},{3,96},{4,128},{5,160},{6,192},{7,224},{8,256}... | collective-permute-start | bytes 49160 | tf_op jit(solution)/shard_map/ppermute | solution.py:163
  32.1 20.1 %copy-start = (bf16[32,64,128]{2,1,0:T(8,128)(2,1)}, bf16[32,64,128]{2,1,0:T(8,128)(2,1)S(1)}, u32[]{:S(2)}) copy-start(bf16[32,64,128]{2,1,0:T(8,128)(2,1)S(1)} %all-to-all-done) | copy-start | bytes 1572868

commit v3 on v1

--- a/solution.py
+++ b/solution.py
@@ -55,13 +55,12 @@
         out_ref[k] = mine
 
 
-def pairs_kernel(row_ref, col_ref, w_hbm, out_ref, w_ref, f_scr, x_scr, sems):
-    total_rows = row_ref.shape[0]
-    total = col_ref.shape[0]
-    tm = min(256, total_rows)
+def pairs_kernel(core_ref, own_ref, oth_ref, col_ref, w_hbm, out_ref, w_ref, f_scr, x_scr, sems):
+    total_rows, total = w_ref.shape
+    tm = min(1024, total_rows)
     tn = min(256, total)
-    per = tm // 64
     steps = total_rows // tm
+    first = core_ref[0] == 0
 
     def fetch(i):
         at = pl.ds(i * tm, tm)
@@ -80,9 +79,13 @@
         mis, scl = carry
         fetch(i).wait()
         at = pl.ds(pl.multiple_of(i * tm, tm), tm)
-        rows = row_ref[at, :]
-        acc = jnp.zeros((tm, LANES), F32)
-        wacc = jnp.zeros((tm, LANES), F32)
+        pieces = []
+        for k in range(tm // 256):
+            cut = pl.ds(pl.multiple_of(i * (tm // 2) + k * 128, 128), 128)
+            own, oth = own_ref[cut, :], oth_ref[cut, :]
+            pieces += [jnp.where(first, own, oth), jnp.where(first, oth, own)]
+        rows = jnp.concatenate(pieces, axis=0)
+        acc = jnp.zeros((2 * tm, LANES), F32)
         for start in range(0, total, tn):
             cut = slice(start, start + tn)
             f2 = jnp.dot(rows, f_scr[:, cut], preferred_element_type=F32)
@@ -96,46 +99,48 @@
             diff = dissim - x2 * inv
             cmat = w * (dissim * jnp.minimum(inv, 1.0) - 1.0)
             mis += jnp.sum((w * (diff * diff)).reshape(tm // 8, 8, tn), axis=0)
-            cols = col_ref[cut, :]
-            acc += jnp.dot(cmat.astype(BF16), cols, preferred_element_type=F32)
-            wacc += jnp.dot(wb, cols, preferred_element_type=F32)
+            both = jnp.concatenate([cmat.astype(BF16), wb], axis=0)
+            acc += jnp.dot(both, col_ref[cut, :], preferred_element_type=F32)
         bent = jnp.dot(rows, form_f, preferred_element_type=F32)
-        scl += jnp.sum((bent * wacc).reshape(tm // 8, 8, LANES), axis=0)
-        sums = jnp.where(lane == ONE + 1, wacc, acc).T
+        scl += jnp.sum((bent * acc[tm:]).reshape(tm // 8, 8, LANES), axis=0)
+        sums = jnp.where(lane == ONE + 1, acc[tm:], acc[:tm]).T
         pull = sums[XH : XH + 16] + sums[XL : XL + 16]
         rate = sums[ONE : ONE + 1]
         wsum = sums[ONE + 1 : ONE + 2]
-        for k in range(per):
+        for k in range(tm // 64):
             cut = slice(64 * k, 64 * k + 64)
-            out_ref[i * per + k, 0:8, :] = jnp.concatenate([pull[0:8, cut], pull[8:16, cut]], axis=1)
-            out_ref[i * per + k, 8:9, :] = jnp.concatenate([rate[:, cut], wsum[:, cut]], axis=1)
+            to = i * (tm // 64) + k
+            for j in range(8):
+                line = jnp.concatenate([pull[j : j + 1, cut], pull[j + 8 : j + 9, cut]], axis=1)
+                out_ref[to, :, 128 * j : 128 * j + 128] = line
+            out_ref[to, :, 1024:1152] = jnp.concatenate([rate[:, cut], wsum[:, cut]], axis=1)
         return mis, scl
 
     mis, scl = lax.fori_loop(
         0, steps, block, (jnp.zeros((8, tn), F32), jnp.zeros((8, LANES), F32))
     )
-    mis = jnp.sum(mis, axis=0, keepdims=True)
-    mis = sum(mis[:, k : k + 128] for k in range(0, tn, 128))
-    scl = jnp.sum(scl, axis=0, keepdims=True)
-    count = out_ref.shape[0]
-    out_ref[:, 9:10, :] = jnp.broadcast_to(mis[None], (count, 1, 128))
-    out_ref[:, 10:11, :] = jnp.broadcast_to(scl[None], (count, 1, 128))
-    out_ref[:, 11:16, :] = jnp.zeros((count, 5, 128), F32)
+    mis = jnp.sum(jnp.sum(mis, axis=0, keepdims=True), axis=1, keepdims=True)
+    scl = jnp.sum(jnp.sum(scl, axis=0, keepdims=True), axis=1, keepdims=True)
+    at = lax.broadcasted_iota(jnp.int32, (1, 128), 1)
+    line = jnp.where(at == 0, mis, jnp.where(at == 1, scl, 0.0))
+    out_ref[:, :, 1152:1280] = jnp.broadcast_to(line[None], (out_ref.shape[0], 1, 128))
 
 
 def finish_kernel(part_ref, crd_ref, new_ref, share_ref):
     sums = jnp.sum(part_ref[...], axis=0)
-    rate = sums[8:9, 0:64]
-    wsum = sums[8:9, 64:128]
-    pull = jnp.concatenate([sums[0:8, 0:64], sums[0:8, 64:128]], axis=0)
+    lines = [sums[:, 128 * k : 128 * k + 128] for k in range(10)]
+    share_ref[...] = jnp.broadcast_to(lines[9][None], share_ref.shape)
+    half = jnp.concatenate(lines[:8], axis=0)
+    pull = jnp.concatenate([half[:, 0:64], half[:, 64:128]], axis=0)
+    rate = lines[8][:, 0:64]
+    wsum = lines[8][:, 64:128]
     crd = crd_ref[...]
     new_ref[...] = crd + (rate * crd - pull) / wsum
-    share_ref[...] = jnp.broadcast_to(sums[8:16][None], share_ref.shape)
 
 
 def stress_kernel(part_ref, out_ref):
     sums = jnp.sum(part_ref[...], axis=0)
-    out_ref[...] = jnp.sum(sums[1:2], axis=1, keepdims=True) / jnp.sum(sums[2:3], axis=1, keepdims=True)
+    out_ref[...] = sums[:, 0:1] / sums[:, 1:2]
 
 
 def column_moves(n_row, n_col, n_depth):
@@ -150,42 +155,52 @@
     rows, cols = pair_weight.shape
     points = embeddings.shape[1]
     group = rows // points
-    n_row, n_col, n_depth = (lax.axis_size(a) for a in ("row", "col", "depth"))
+    n_row, n_z, n_core, n_depth = (lax.axis_size(a) for a in ("row", "z", "core", "depth"))
+    likes = n_z * n_depth
 
     packed = pl.pallas_call(
         pack_kernel,
         out_shape=(
             jax.ShapeDtypeStruct((points, LANES), BF16),
-            jax.ShapeDtypeStruct((group, points, LANES), BF16),
+            jax.ShapeDtypeStruct((likes, points, LANES), BF16),
         ),
         name="pack",
     )(embeddings, coords)
-    moved = lax.ppermute(packed[0], ("row", "col", "depth"), column_moves(n_row, n_col, n_depth))
-    t_rows = lax.all_to_all(packed[1], ("col", "depth"), 0, 0, tiled=True).reshape(rows, LANES)
+    moves = column_moves(n_row, n_z * n_core, n_depth)
+    moved = lax.ppermute(packed[0], ("row", "z", "core", "depth"), moves)
+    own = lax.all_to_all(packed[1], ("z", "depth"), 0, 0, tiled=True).reshape(rows // n_core, LANES)
+    moved, own = lax.optimization_barrier((moved, own))
+    oth = lax.ppermute(own, "core", [(0, 1), (1, 0)])
     moved = jnp.broadcast_to(moved[None], (n_row, points, LANES))
     t_cols = lax.all_to_all(moved, "row", 0, 0, tiled=True).reshape(cols, LANES)
 
     vmem = pl.BlockSpec(memory_space=pltpu.VMEM)
     parts = pl.pallas_call(
         pairs_kernel,
-        in_specs=[vmem, vmem, pl.BlockSpec(memory_space=pltpu.HBM)],
+        in_specs=[
+            pl.BlockSpec(memory_space=pltpu.SMEM),
+            vmem,
+            vmem,
+            vmem,
+            pl.BlockSpec(memory_space=pltpu.HBM),
+        ],
         out_specs=vmem,
-        out_shape=jax.ShapeDtypeStruct((group, 16, 128), F32),
+        out_shape=jax.ShapeDtypeStruct((group, 1, 1280), F32),
         scratch_shapes=[
             pltpu.VMEM((rows, cols), BF16),
             pltpu.VMEM((LANES, cols), BF16),
             pltpu.VMEM((LANES, cols), BF16),
-            pltpu.SemaphoreType.DMA((max(1, rows // 256),)),
+            pltpu.SemaphoreType.DMA((max(1, rows // 1024),)),
         ],
-        compiler_params=pltpu.CompilerParams(vmem_limit_bytes=60 * 1024 * 1024),
+        compiler_params=pltpu.CompilerParams(vmem_limit_bytes=52 * 1024 * 1024),
         name="pairs",
-    )(t_rows, t_cols, pair_weight)
-    parts = lax.all_to_all(parts, ("col", "depth"), 0, 0, tiled=True)
+    )(lax.axis_index("core").reshape(1).astype(jnp.int32), own, oth, t_cols, pair_weight)
+    parts = lax.all_to_all(parts, ("z", "core", "depth"), 0, 0, tiled=True)
     new_coords, shares = pl.pallas_call(
         finish_kernel,
         out_shape=(
             jax.ShapeDtypeStruct(coords.shape, F32),
-            jax.ShapeDtypeStruct((n_row, 8, 128), F32),
+            jax.ShapeDtypeStruct((n_row, 1, 128), F32),
         ),
         name="finish",
     )(parts, coords)
@@ -199,15 +214,15 @@
 
 
 def solution(mesh):
-    placed = (
-        P(None, ("row", "col", "depth")),
-        P(None, ("row", "col", "depth")),
-        P("row", ("col", "depth")),
+    n_row, n_col, n_depth = (mesh.shape[a] for a in ("row", "col", "depth"))
+    fine = jax.sharding.Mesh(
+        mesh.devices.reshape(n_row, n_col // 2, 2, n_depth), ("row", "z", "core", "depth")
     )
+    points = P(None, ("row", "z", "core", "depth"))
     return jax.shard_map(
         shards,
-        mesh=mesh,
-        in_specs=placed,
-        out_specs=(P(None, ("row", "col", "depth")), P()),
+        mesh=fine,
+        in_specs=(points, points, P("row", ("z", "core", "depth"))),
+        out_specs=(points, P()),
         check_vma=False,
     )

time: 116 us -> 93.8 us (0.81)
  blocking collectives: 85.7 us -> 34.1 us
  starting transfers between devices: 8.83 us -> 35.8 us
  waiting for transfers between devices: 1.06 us -> 6.77 us
  Pallas kernels: 18.1 us -> 14.3 us
    all_to_all x3 -> x1, blocking collectives: 72.3 us -> 21.6 us  [shards(): parts = lax.all_to_all(parts, ('z', 'core', 'depth'), 0, 0, tiled=True)]
    all_to_all x0 -> x2, starting transfers between devices: none -> 23.1 us  [the longest x1 12 us: shards(): lax.all_to_all(packed[1], ('z', 'depth'), 0, 0, tiled=True)]
    all_to_all x0 -> x2, waiting for transfers between devices: none -> 4.58 us  [the longest x1 4.11 us: shards(): t_cols = lax.all_to_all(moved, 'row', 0, 0, tiled=True).reshape(cols, LANES)]
    ppermute x1 -> x2, starting transfers between devices: 8.83 us -> 12.7 us  [the longest x1 7.39 us: shards(): moved = lax.ppermute(packed[0], ('row', 'z', 'core', 'depth'), moves)]
    pallas_call x1, Pallas kernels: 13.3 us -> 9.81 us  [shards(): pl.pallas_call(pairs_kernel, in_specs=[pl.BlockSpec(memory_space=pltpu.SM...]
  transfers between devices with their start and end apart: 1 -> 4, of which waited for: 1 -> 4; matrix products, arithmetic and copies ran while one was open for 0% -> 0% of each run, Pallas kernels for 0% -> 0%
where the time goes in v3:
time: 93.8 us; the launch traced here: 92.4 us
  starting transfers between devices  35.8 us (38%)
  blocking collectives  34.1 us (36%)
  Pallas kernels  14.3 us (15%)
  waiting for transfers between devices  6.77 us (7%)
    all_to_all x1, blocking collectives, shards(): parts = lax.all_to_all(parts, ('z', 'core', 'depth'), 0, 0, tiled=True)  21.6 us
    all_to_all x1, blocking collectives, shards(): shares = lax.all_to_all(shares, 'row', 0, 0, tiled=True)  12.5 us
    all_to_all x1, starting transfers between devices, shards(): lax.all_to_all(packed[1], ('z', 'depth'), 0, 0, tiled=True)  12 us
    all_to_all x1, starting transfers between devices, shards(): t_cols = lax.all_to_all(moved, 'row', 0, 0, tiled=True).reshape(cols, LANES)  11.1 us
    pallas_call x1, Pallas kernels, shards(): pl.pallas_call(pairs_kernel, in_specs=[pl.BlockSpec(memory_space=pltpu.SM...  9.81 us
    ppermute x1, starting transfers between devices, shards(): moved = lax.ppermute(packed[0], ('row', 'z', 'core', 'depth'), moves)  7.39 us
    ppermute x1, starting transfers between devices, shards(): oth = lax.ppermute(own, 'core', [(0, 1), (1, 0)])  5.34 us
    all_to_all x1, waiting for transfers between devices, shards(): t_cols = lax.all_to_all(moved, 'row', 0, 0, tiled=True).reshape(cols, LANES)  4.11 us
  transfers between devices with their start and end apart: 4, of which 4 were waited for; matrix products, arithmetic and copies ran while one was open for 0% of the time, Pallas kernels for 0%

profile of v3, /device:TPU:1, one launch (start us, length us, event | category | flops | bytes accessed | tf_op | source)
XLA Modules:
  0.0 92.4 jit_solution(361055317750900976)
XLA Ops:
  0.6 1.5 %pack.1 = (bf16[64,128]{1,0:T(8,128)(2,1)}, bf16[16,64,128]{2,1,0:T(8,128)(2,1)}) custom-call(bf16[64,64]{1,0:T(8,128)(2,1)} %emb_ref.1, f32[16,64]{1,0:T(8,128)} %crd_ref.3), custom_call_target="tpu_custom_call" | custom-call | tf_op jit(solution)/shard_map/pack/pallas_call | solution.py:161
  2.2 12.0 %all-to-all-start = ((bf16[16,64,128]{2,1,0:T(8,128)(2,1)}), bf16[16,64,128]{2,1,0:T(8,128)(2,1)S(1)}, u32[]{:S(2)}, u32[]{:S(2)}) async-start(bf16[16,64,128]{2,1,0:T(8,128)(2,1)} %get-tuple-element.9), calls=%async_computation | async-start | bytes 524288 | tf_op jit(solution)/shard_map/all_to_all | solution.py:171
  14.1 7.4 %collective-permute-start = (bf16[64,128]{1,0:T(8,128)(2,1)}, bf16[64,128]{1,0:T(8,128)(2,1)S(1)}, u32[]{:S(2)}, u32[]{:S(2)}) collective-permute-start(bf16[64,128]{1,0:T(8,128)(2,1)} %get-tuple-element.8), channel_id=1, source_target_pairs={{0,0},{1,32},{2,64},{3,96},{4,128},{5,160},{6,192},{7,224},{8,256}... | collective-permute-start | bytes 49160 | tf_op jit(solution)/shard_map/ppermute | solution.py:170
  21.5 1.1 %collective-permute-done = bf16[64,128]{1,0:T(8,128)(2,1)S(1)} collective-permute-done((bf16[64,128]{1,0:T(8,128)(2,1)}, bf16[64,128]{1,0:T(8,128)(2,1)S(1)}, u32[]{:S(2)}, u32[]{:S(2)}) %collective-permute-start) | collective-permute-done | bytes 16416 | tf_op jit(solution)/shard_map/ppermute | solution.py:170
  22.6 0.5 all-to-all-done
  23.1 0.7 broadcast_in_dim.2
  23.8 11.1 %all-to-all-start.1 = ((bf16[16,64,128]{2,1,0:T(8,128)(2,1)}), bf16[16,64,128]{2,1,0:T(8,128)(2,1)S(1)}, u32[]{:S(2)}, u32[]{:S(2)}) async-start(bf16[16,64,128]{2,1,0:T(8,128)(2,1)} %broadcast_in_dim.2), calls=%async_computation.1 | async-start | bytes 524288 | tf_op jit(solution)/shard_map/all_to_all | solution.py:175
  34.9 5.3 %collective-permute-start.1 = (bf16[1024,128]{1,0:T(8,128)(2,1)S(1)}, bf16[1024,128]{1,0:T(8,128)(2,1)S(1)}, u32[]{:S(2)}, u32[]{:S(2)}) collective-permute-start(bf16[1024,128]{1,0:T(8,128)(2,1)S(1)} %bitcast.4), channel_id=1, source_target_pairs={{0,2},{2,0},{1,3},{3,1},{4,6},{6,4},{5,7},{7,5},{8,10},{10,8},{9,1... | collective-permute-start | bytes 786440 | tf_op jit(solution)/shard_map/ppermute | solution.py:173
  40.3 1.1 %collective-permute-done.1.oth_ref = bf16[1024,128]{1,0:T(8,128)(2,1)S(1)} collective-permute-done((bf16[1024,128]{1,0:T(8,128)(2,1)S(1)}, bf16[1024,128]{1,0:T(8,128)(2,1)S(1)}, u32[]{:S(2)}, u32[]{:S(2)}) %collective-permute-start.1) | collective-permute-done | bytes 262176 | tf_op jit(solution)/shard_map/ppermute | solution.py:173
  41.4 4.1 %all-to-all-done.1 = bf16[16,64,128]{2,1,0:T(8,128)(2,1)S(1)} async-done(((bf16[16,64,128]{2,1,0:T(8,128)(2,1)}), bf16[16,64,128]{2,1,0:T(8,128)(2,1)S(1)}, u32[]{:S(2)}, u32[]{:S(2)}) %all-to-all-start.1) | async-done | bytes 262176 | tf_op jit(solution)/shard_map/all_to_all | solution.py:175
  45.5 9.8 %pairs.1 = f32[32,1,1280]{2,1,0:T(1,128)S(1)} custom-call(s32[1]{0:T(128)} %bitcast.core_ref, bf16[1024,128]{1,0:T(8,128)(2,1)S(1)} %bitcast.5, bf16[1024,128]{1,0:T(8,128)(2,1)S(1)} %collective-permute-done.1.oth_ref, bf16[1024,128]{1,0:T(8,128)(2,1)S(1)} %bitcast.6, bf16[2048,1024]{1,0:T(8,128)(2,1)} %w_hbm.1), custom_call_target="tpu_custom_call" | custom-call | tf_op jit(solution)/shard_map/pairs/pallas_call | solution.py:178
  55.3 21.6 %all_to_all.20.part_ref = f32[32,1,1280]{2,1,0:T(1,128)} all-to-all(f32[32,1,1280]{2,1,0:T(1,128)S(1)} %pairs.1), channel_id=1, replica_groups=mesh['row'=16,'z'=8,'core'=2,'depth'=2] {'z','core','depth'}, dimensions={0} | all-to-all | bytes 327680 | tf_op jit(solution)/shard_map/all_to_all | solution.py:198
  76.9 1.7 %finish.1 = (f32[16,64]{1,0:T(8,128)}, f32[16,1,128]{2,1,0:T(1,128)}) custom-call(f32[32,1,1280]{2,1,0:T(1,128)} %all_to_all.20.part_ref, f32[16,64]{1,0:T(8,128)} %crd_ref.3), custom_call_target="tpu_custom_call" | custom-call | tf_op jit(solution)/shard_map/finish/pallas_call | solution.py:199
  78.6 12.5 %all_to_all.21.part_ref = f32[16,1,128]{2,1,0:T(1,128)} all-to-all(f32[16,1,128]{2,1,0:T(1,128)} %get-tuple-element.13), channel_id=1, replica_groups=mesh['row'=16,'z'=8,'core'=2,'depth'=2] {'row'}, dimensions={0} | all-to-all | bytes 16384 | tf_op jit(solution)/shard_map/all_to_all | solution.py:207
  91.1 1.3 %stress.1 = f32[1,1]{1,0:T(1,128)} custom-call(f32[16,1,128]{2,1,0:T(1,128)} %all_to_all.21.part_ref), custom_call_target="tpu_custom_call" | custom-call | tf_op jit(solution)/shard_map/stress/pallas_call | solution.py:208
Async XLA Ops:
  2.2 20.9 %all-to-all-start = ((bf16[16,64,128]{2,1,0:T(8,128)(2,1)}), bf16[16,64,128]{2,1,0:T(8,128)(2,1)S(1)}, u32[]{:S(2)}, u32[]{:S(2)}) async-start(bf16[16,64,128]{2,1,0:T(8,128)(2,1)} %get-tuple-element.9), calls=%async_computation | async-start | bytes 524288 | tf_op jit(solution)/shard_map/all_to_all | solution.py:171
  14.1 8.5 %collective-permute-start = (bf16[64,128]{1,0:T(8,128)(2,1)}, bf16[64,128]{1,0:T(8,128)(2,1)S(1)}, u32[]{:S(2)}, u32[]{:S(2)}) collective-permute-start(bf16[64,128]{1,0:T(8,128)(2,1)} %get-tuple-element.8), channel_id=1, source_target_pairs={{0,0},{1,32},{2,64},{3,96},{4,128},{5,160},{6,192},{7,224},{8,256}... | collective-permute-start | bytes 49160 | tf_op jit(solution)/shard_map/ppermute | solution.py:170
  23.8 21.7 %all-to-all-start.1 = ((bf16[16,64,128]{2,1,0:T(8,128)(2,1)}), bf16[16,64,128]{2,1,0:T(8,128)(2,1)S(1)}, u32[]{:S(2)}, u32[]{:S(2)}) async-start(bf16[16,64,128]{2,1,0:T(8,128)(2,1)} %broadcast_in_dim.2), calls=%async_computation.1 | async-start | bytes 524288 | tf_op jit(solution)/shard_map/all_to_all | solution.py:175
  34.9 6.5 %collective-permute-start.1 = (bf16[1024,128]{1,0:T(8,128)(2,1)S(1)}, bf16[1024,128]{1,0:T(8,128)(2,1)S(1)}, u32[]{:S(2)}, u32[]{:S(2)}) collective-permute-start(bf16[1024,128]{1,0:T(8,128)(2,1)S(1)} %bitcast.4), channel_id=1, source_target_pairs={{0,2},{2,0},{1,3},{3,1},{4,6},{6,4},{5,7},{7,5},{8,10},{10,8},{9,1... | collective-permute-start | bytes 786440 | tf_op jit(solution)/shard_map/ppermute | solution.py:173

commit v4 on v3

--- a/solution.py
+++ b/solution.py
@@ -55,6 +55,13 @@
         out_ref[k] = mine
 
 
+def pick_sums():
+    a = lax.broadcasted_iota(jnp.int32, (48, LANES), 0)
+    b = lax.broadcasted_iota(jnp.int32, (48, LANES), 1)
+    keep = ((a < 32) & (b == a + XH)) | ((a >= 32) & (b == ONE))
+    return jnp.where(keep, 1.0, 0.0).astype(BF16)
+
+
 def pairs_kernel(core_ref, own_ref, oth_ref, col_ref, w_hbm, out_ref, w_ref, f_scr, x_scr, sems):
     total_rows, total = w_ref.shape
     tm = min(1024, total_rows)
@@ -69,11 +76,10 @@
     for i in range(steps):
         fetch(i).start()
     all_cols = col_ref[...]
-    dims = (((1,), (1,)), ((), ()))
-    form_f = bilinear_form(0)
-    f_scr[...] = lax.dot_general(form_f, all_cols, dims, preferred_element_type=F32).astype(BF16)
-    x_scr[...] = lax.dot_general(bilinear_form(1), all_cols, dims, preferred_element_type=F32).astype(BF16)
-    lane = lax.broadcasted_iota(jnp.int32, (tm, LANES), 1)
+    last = (((1,), (1,)), ((), ()))
+    f_scr[...] = lax.dot_general(bilinear_form(0), all_cols, last, preferred_element_type=F32).astype(BF16)
+    x_scr[...] = lax.dot_general(bilinear_form(1), all_cols, last, preferred_element_type=F32).astype(BF16)
+    flat = lax.dot_general(pick_sums(), all_cols, last, preferred_element_type=F32).astype(BF16)
 
     def block(i, carry):
         mis, scl = carry
@@ -85,7 +91,8 @@
             own, oth = own_ref[cut, :], oth_ref[cut, :]
             pieces += [jnp.where(first, own, oth), jnp.where(first, oth, own)]
         rows = jnp.concatenate(pieces, axis=0)
-        acc = jnp.zeros((2 * tm, LANES), F32)
+        acc = jnp.zeros((48, tm), F32)
+        wacc = jnp.zeros((16, tm), F32)
         for start in range(0, total, tn):
             cut = slice(start, start + tn)
             f2 = jnp.dot(rows, f_scr[:, cut], preferred_element_type=F32)
@@ -99,14 +106,12 @@
             diff = dissim - x2 * inv
             cmat = w * (dissim * jnp.minimum(inv, 1.0) - 1.0)
             mis += jnp.sum((w * (diff * diff)).reshape(tm // 8, 8, tn), axis=0)
-            both = jnp.concatenate([cmat.astype(BF16), wb], axis=0)
-            acc += jnp.dot(both, col_ref[cut, :], preferred_element_type=F32)
-        bent = jnp.dot(rows, form_f, preferred_element_type=F32)
-        scl += jnp.sum((bent * acc[tm:]).reshape(tm // 8, 8, LANES), axis=0)
-        sums = jnp.where(lane == ONE + 1, acc[tm:], acc[:tm]).T
-        pull = sums[XH : XH + 16] + sums[XL : XL + 16]
-        rate = sums[ONE : ONE + 1]
-        wsum = sums[ONE + 1 : ONE + 2]
+            scl += jnp.sum((w * f2).reshape(tm // 8, 8, tn), axis=0)
+            acc += lax.dot_general(flat[:, cut], cmat.astype(BF16), last, preferred_element_type=F32)
+            wacc += lax.dot_general(flat[32:, cut], wb, last, preferred_element_type=F32)
+        pull = acc[0:16] + acc[16:32]
+        rate = acc[32:33]
+        wsum = wacc[0:1]
         for k in range(tm // 64):
             cut = slice(64 * k, 64 * k + 64)
             to = i * (tm // 64) + k
@@ -116,9 +121,8 @@
             out_ref[to, :, 1024:1152] = jnp.concatenate([rate[:, cut], wsum[:, cut]], axis=1)
         return mis, scl
 
-    mis, scl = lax.fori_loop(
-        0, steps, block, (jnp.zeros((8, tn), F32), jnp.zeros((8, LANES), F32))
-    )
+    zero = jnp.zeros((8, tn), F32)
+    mis, scl = lax.fori_loop(0, steps, block, (zero, zero))
     mis = jnp.sum(jnp.sum(mis, axis=0, keepdims=True), axis=1, keepdims=True)
     scl = jnp.sum(jnp.sum(scl, axis=0, keepdims=True), axis=1, keepdims=True)
     at = lax.broadcasted_iota(jnp.int32, (1, 128), 1)
@@ -126,10 +130,9 @@
     out_ref[:, :, 1152:1280] = jnp.broadcast_to(line[None], (out_ref.shape[0], 1, 128))
 
 
-def finish_kernel(part_ref, crd_ref, new_ref, share_ref):
+def finish_kernel(part_ref, crd_ref, new_ref):
     sums = jnp.sum(part_ref[...], axis=0)
-    lines = [sums[:, 128 * k : 128 * k + 128] for k in range(10)]
-    share_ref[...] = jnp.broadcast_to(lines[9][None], share_ref.shape)
+    lines = [sums[:, 128 * k : 128 * k + 128] for k in range(9)]
     half = jnp.concatenate(lines[:8], axis=0)
     pull = jnp.concatenate([half[:, 0:64], half[:, 64:128]], axis=0)
     rate = lines[8][:, 0:64]
@@ -196,15 +199,14 @@
         name="pairs",
     )(lax.axis_index("core").reshape(1).astype(jnp.int32), own, oth, t_cols, pair_weight)
     parts = lax.all_to_all(parts, ("z", "core", "depth"), 0, 0, tiled=True)
-    new_coords, shares = pl.pallas_call(
+    shares = jnp.sum(parts[:, :, 1152:], axis=0, keepdims=True)
+    shares = lax.all_to_all(jnp.broadcast_to(shares, (n_row, 1, 128)), "row", 0, 0, tiled=True)
+    new_coords = pl.pallas_call(
         finish_kernel,
-        out_shape=(
-            jax.ShapeDtypeStruct(coords.shape, F32),
-            jax.ShapeDtypeStruct((n_row, 1, 128), F32),
-        ),
+        out_shape=jax.ShapeDtypeStruct(coords.shape, F32),
+        cost_estimate=pl.CostEstimate(flops=100000, bytes_accessed=200000, transcendentals=0),
         name="finish",
     )(parts, coords)
-    shares = lax.all_to_all(shares, "row", 0, 0, tiled=True)
     stress = pl.pallas_call(
         stress_kernel,
         out_shape=jax.ShapeDtypeStruct((1, 1), F32),

time: 93.8 us -> 91.8 us (0.979)
  blocking collectives: 34.1 us -> 21.5 us
  waiting for transfers between devices: 6.77 us -> 13.8 us
  starting transfers between devices: 35.8 us -> 39.3 us
  local copies, waits for them, and re-layouts: 0.75 us -> 1.94 us
    all_to_all x1 -> x0, blocking collectives: 12.5 us -> none  [shards(): shares = lax.all_to_all(shares, 'row', 0, 0, tiled=True)]
    all_to_all x0 -> x1, waiting for transfers between devices: none -> 7.06 us  [shards(): lax.all_to_all(jnp.broadcast_to(shares, (n_row, 1, 128)), 'row', 0, 0, ti...]
    all_to_all x0 -> x1, starting transfers between devices: none -> 3.49 us  [shards(): lax.all_to_all(jnp.broadcast_to(shares, (n_row, 1, 128)), 'row', 0, 0, ti...]
  transfers between devices with their start and end apart: 4 -> 5, of which waited for: 4 -> 5; matrix products, arithmetic and copies ran while one was open for 0% -> 0% of each run, Pallas kernels for 0% -> 2%
where the time goes in v4:
time: 91.8 us; the launch traced here: 90.9 us
  starting transfers between devices  39.3 us (43%)
  blocking collectives  21.5 us (23%)
  waiting for transfers between devices  13.8 us (15%)
  Pallas kernels  13.6 us (15%)
  local copies, waits for them, and re-layouts  1.94 us (2%)
    all_to_all x1, blocking collectives, shards(): parts = lax.all_to_all(parts, ('z', 'core', 'depth'), 0, 0, tiled=True)  21.5 us
    all_to_all x1, starting transfers between devices, shards(): lax.all_to_all(packed[1], ('z', 'depth'), 0, 0, tiled=True)  12 us
    all_to_all x1, starting transfers between devices, shards(): t_cols = lax.all_to_all(moved, 'row', 0, 0, tiled=True).reshape(cols, LANES)  11.1 us
    pallas_call x1, Pallas kernels, shards(): pl.pallas_call(pairs_kernel, in_specs=[pl.BlockSpec(memory_space=pltpu.SM...  9.11 us
    ppermute x1, starting transfers between devices, shards(): moved = lax.ppermute(packed[0], ('row', 'z', 'core', 'depth'), moves)  7.39 us
    all_to_all x1, waiting for transfers between devices, shards(): lax.all_to_all(jnp.broadcast_to(shares, (n_row, 1, 128)), 'row', 0, 0, ti...  7.06 us
    ppermute x1, starting transfers between devices, shards(): oth = lax.ppermute(own, 'core', [(0, 1), (1, 0)])  5.34 us
    all_to_all x1, waiting for transfers between devices, shards(): t_cols = lax.all_to_all(moved, 'row', 0, 0, tiled=True).reshape(cols, LANES)  4.11 us
  transfers between devices with their start and end apart: 5, of which 5 were waited for; matrix products, arithmetic and copies ran while one was open for 0% of the time, Pallas kernels for 2%

profile of v4, /device:TPU:1, one launch (start us, length us, event | category | flops | bytes accessed | tf_op | source)
XLA Modules:
  0.0 90.9 jit_solution(6364391319833135021)
XLA Ops:
  0.6 1.5 %pack.1 = (bf16[64,128]{1,0:T(8,128)(2,1)}, bf16[16,64,128]{2,1,0:T(8,128)(2,1)}) custom-call(bf16[64,64]{1,0:T(8,128)(2,1)} %emb_ref.1, f32[16,64]{1,0:T(8,128)} %crd_ref.3), custom_call_target="tpu_custom_call" | custom-call | tf_op jit(solution)/shard_map/pack/pallas_call | solution.py:164
  2.1 12.0 %all-to-all-start = ((bf16[16,64,128]{2,1,0:T(8,128)(2,1)}), bf16[16,64,128]{2,1,0:T(8,128)(2,1)S(1)}, u32[]{:S(2)}, u32[]{:S(2)}) async-start(bf16[16,64,128]{2,1,0:T(8,128)(2,1)} %get-tuple-element.7), calls=%async_computation | async-start | bytes 524288 | tf_op jit(solution)/shard_map/all_to_all | solution.py:174
  14.1 7.4 %collective-permute-start = (bf16[64,128]{1,0:T(8,128)(2,1)}, bf16[64,128]{1,0:T(8,128)(2,1)S(1)}, u32[]{:S(2)}, u32[]{:S(2)}) collective-permute-start(bf16[64,128]{1,0:T(8,128)(2,1)} %get-tuple-element.6), channel_id=1, source_target_pairs={{0,0},{1,32},{2,64},{3,96},{4,128},{5,160},{6,192},{7,224},{8,256}... | collective-permute-start | bytes 49160 | tf_op jit(solution)/shard_map/ppermute | solution.py:173
  21.5 1.1 %collective-permute-done = bf16[64,128]{1,0:T(8,128)(2,1)S(1)} collective-permute-done((bf16[64,128]{1,0:T(8,128)(2,1)}, bf16[64,128]{1,0:T(8,128)(2,1)S(1)}, u32[]{:S(2)}, u32[]{:S(2)}) %collective-permute-start) | collective-permute-done | bytes 16416 | tf_op jit(solution)/shard_map/ppermute | solution.py:173
  22.6 0.5 all-to-all-done
  23.1 0.7 broadcast_in_dim.4
  23.8 11.1 %all-to-all-start.1 = ((bf16[16,64,128]{2,1,0:T(8,128)(2,1)}), bf16[16,64,128]{2,1,0:T(8,128)(2,1)S(1)}, u32[]{:S(2)}, u32[]{:S(2)}) async-start(bf16[16,64,128]{2,1,0:T(8,128)(2,1)} %broadcast_in_dim.4), calls=%async_computation.1 | async-start | bytes 524288 | tf_op jit(solution)/shard_map/all_to_all | solution.py:178
  34.9 5.3 %collective-permute-start.1 = (bf16[1024,128]{1,0:T(8,128)(2,1)S(1)}, bf16[1024,128]{1,0:T(8,128)(2,1)S(1)}, u32[]{:S(2)}, u32[]{:S(2)}) collective-permute-start(bf16[1024,128]{1,0:T(8,128)(2,1)S(1)} %bitcast.4), channel_id=1, source_target_pairs={{0,2},{2,0},{1,3},{3,1},{4,6},{6,4},{5,7},{7,5},{8,10},{10,8},{9,1... | collective-permute-start | bytes 786440 | tf_op jit(solution)/shard_map/ppermute | solution.py:176
  40.3 1.1 %collective-permute-done.1.oth_ref = bf16[1024,128]{1,0:T(8,128)(2,1)S(1)} collective-permute-done((bf16[1024,128]{1,0:T(8,128)(2,1)S(1)}, bf16[1024,128]{1,0:T(8,128)(2,1)S(1)}, u32[]{:S(2)}, u32[]{:S(2)}) %collective-permute-start.1) | collective-permute-done | bytes 262176 | tf_op jit(solution)/shard_map/ppermute | solution.py:176
  41.4 4.1 %all-to-all-done.1 = bf16[16,64,128]{2,1,0:T(8,128)(2,1)S(1)} async-done(((bf16[16,64,128]{2,1,0:T(8,128)(2,1)}), bf16[16,64,128]{2,1,0:T(8,128)(2,1)S(1)}, u32[]{:S(2)}, u32[]{:S(2)}) %all-to-all-start.1) | async-done | bytes 262176 | tf_op jit(solution)/shard_map/all_to_all | solution.py:178
  45.5 9.1 %pairs.1 = f32[32,1,1280]{2,1,0:T(1,128)S(1)} custom-call(s32[1]{0:T(128)} %bitcast.core_ref, bf16[1024,128]{1,0:T(8,128)(2,1)S(1)} %bitcast.5, bf16[1024,128]{1,0:T(8,128)(2,1)S(1)} %collective-permute-done.1.oth_ref, bf16[1024,128]{1,0:T(8,128)(2,1)S(1)} %bitcast.6, bf16[2048,1024]{1,0:T(8,128)(2,1)} %w_hbm.1), custom_call_target="tpu_custom_call" | custom-call | tf_op jit(solution)/shard_map/pairs/pallas_call | solution.py:181
  54.6 21.5 %all_to_all.20.part_ref = f32[32,1,1280]{2,1,0:T(1,128)S(1)} all-to-all(f32[32,1,1280]{2,1,0:T(1,128)S(1)} %pairs.1), channel_id=1, replica_groups=mesh['row'=16,'z'=8,'core'=2,'depth'=2] {'z','core','depth'}, dimensions={0} | all-to-all | bytes 327680 | tf_op jit(solution)/shard_map/all_to_all | solution.py:201
  76.1 0.0 copy-start
  76.2 0.6 broadcast_in_dim.5
  76.8 3.5 %all-to-all-start.3 = ((f32[16,1,128]{2,1,0:T(1,128)}), f32[16,1,128]{2,1,0:T(1,128)S(1)}, u32[]{:S(2)}, u32[]{:S(2)}) async-start(f32[16,1,128]{2,1,0:T(1,128)} %broadcast_in_dim.5), calls=%async_computation.3 | async-start | bytes 16384 | tf_op jit(solution)/shard_map/all_to_all | solution.py:203
  80.3 0.0 copy-done
  80.3 1.7 %finish.1 = f32[16,64]{1,0:T(8,128)} custom-call(f32[32,1,1280]{2,1,0:T(1,128)} %copy-done, f32[16,64]{1,0:T(8,128)} %crd_ref.3), custom_call_target="tpu_custom_call" | custom-call | flops 100000 | bytes 200000 | tf_op jit(solution)/shard_map/finish/pallas_call | solution.py:204
  82.0 7.1 %all-to-all-done.3.part_ref = f32[16,1,128]{2,1,0:T(1,128)S(1)} async-done(((f32[16,1,128]{2,1,0:T(1,128)}), f32[16,1,128]{2,1,0:T(1,128)S(1)}, u32[]{:S(2)}, u32[]{:S(2)}) %all-to-all-start.3) | async-done | bytes 8224 | tf_op jit(solution)/shard_map/all_to_all | solution.py:203
  89.0 0.0 copy-start.1
  89.0 0.6 copy-done.1
  89.6 1.3 %stress.1 = f32[1,1]{1,0:T(1,128)} custom-call(f32[16,1,128]{2,1,0:T(1,128)} %copy-done.1), custom_call_target="tpu_custom_call" | custom-call | tf_op jit(solution)/shard_map/stress/pallas_call | solution.py:210
  (1 shorter events, 0.0 us)
Async XLA Ops:
  2.1 20.9 %all-to-all-start = ((bf16[16,64,128]{2,1,0:T(8,128)(2,1)}), bf16[16,64,128]{2,1,0:T(8,128)(2,1)S(1)}, u32[]{:S(2)}, u32[]{:S(2)}) async-start(bf16[16,64,128]{2,1,0:T(8,128)(2,1)} %get-tuple-element.7), calls=%async_computation | async-start | bytes 524288 | tf_op jit(solution)/shard_map/all_to_all | solution.py:174
  14.1 8.5 %collective-permute-start = (bf16[64,128]{1,0:T(8,128)(2,1)}, bf16[64,128]{1,0:T(8,128)(2,1)S(1)}, u32[]{:S(2)}, u32[]{:S(2)}) collective-permute-start(bf16[64,128]{1,0:T(8,128)(2,1)} %get-tuple-element.6), channel_id=1, source_target_pairs={{0,0},{1,32},{2,64},{3,96},{4,128},{5,160},{6,192},{7,224},{8,256}... | collective-permute-start | bytes 49160 | tf_op jit(solution)/shard_map/ppermute | solution.py:173
  23.8 21.7 %all-to-all-start.1 = ((bf16[16,64,128]{2,1,0:T(8,128)(2,1)}), bf16[16,64,128]{2,1,0:T(8,128)(2,1)S(1)}, u32[]{:S(2)}, u32[]{:S(2)}) async-start(bf16[16,64,128]{2,1,0:T(8,128)(2,1)} %broadcast_in_dim.4), calls=%async_computation.1 | async-start | bytes 524288 | tf_op jit(solution)/shard_map/all_to_all | solution.py:178
  34.9 6.5 %collective-permute-start.1 = (bf16[1024,128]{1,0:T(8,128)(2,1)S(1)}, bf16[1024,128]{1,0:T(8,128)(2,1)S(1)}, u32[]{:S(2)}, u32[]{:S(2)}) collective-permute-start(bf16[1024,128]{1,0:T(8,128)(2,1)S(1)} %bitcast.4), channel_id=1, source_target_pairs={{0,2},{2,0},{1,3},{3,1},{4,6},{6,4},{5,7},{7,5},{8,10},{10,8},{9,1... | collective-permute-start | bytes 786440 | tf_op jit(solution)/shard_map/ppermute | solution.py:176
  76.1 4.1 %copy-start = (f32[32,1,1280]{2,1,0:T(1,128)}, f32[32,1,1280]{2,1,0:T(1,128)S(1)}, u32[]{:S(2)}) copy-start(f32[32,1,1280]{2,1,0:T(1,128)S(1)} %all_to_all.20.part_ref) | copy-start | bytes 491524
  76.8 12.3 %all-to-all-start.3 = ((f32[16,1,128]{2,1,0:T(1,128)}), f32[16,1,128]{2,1,0:T(1,128)S(1)}, u32[]{:S(2)}, u32[]{:S(2)}) async-start(f32[16,1,128]{2,1,0:T(1,128)} %broadcast_in_dim.5), calls=%async_computation.3 | async-start | bytes 16384 | tf_op jit(solution)/shard_map/all_to_all | solution.py:203
  89.0 0.6 copy-start.1

commit v5 on v4

--- a/solution.py
+++ b/solution.py
@@ -62,12 +62,12 @@
     return jnp.where(keep, 1.0, 0.0).astype(BF16)
 
 
-def pairs_kernel(core_ref, own_ref, oth_ref, col_ref, w_hbm, out_ref, w_ref, f_scr, x_scr, sems):
+def pairs_kernel(own_ref, oth_ref, col_ref, w_hbm, out_ref, w_ref, f_scr, x_scr, flat_scr, c_scr, f_tiles, x_tiles, sems):
     total_rows, total = w_ref.shape
-    tm = min(1024, total_rows)
+    tm = c_scr.shape[0]
     tn = min(256, total)
     steps = total_rows // tm
-    first = core_ref[0] == 0
+    first = lax.axis_index("core") == 0
 
     def fetch(i):
         at = pl.ds(i * tm, tm)
@@ -79,36 +79,42 @@
     last = (((1,), (1,)), ((), ()))
     f_scr[...] = lax.dot_general(bilinear_form(0), all_cols, last, preferred_element_type=F32).astype(BF16)
     x_scr[...] = lax.dot_general(bilinear_form(1), all_cols, last, preferred_element_type=F32).astype(BF16)
-    flat = lax.dot_general(pick_sums(), all_cols, last, preferred_element_type=F32).astype(BF16)
-
-    def block(i, carry):
-        mis, scl = carry
-        fetch(i).wait()
-        at = pl.ds(pl.multiple_of(i * tm, tm), tm)
+    flat_scr[...] = lax.dot_general(pick_sums(), all_cols, last, preferred_element_type=F32).astype(BF16)
+
+    def squares(i, slot):
         pieces = []
         for k in range(tm // 256):
             cut = pl.ds(pl.multiple_of(i * (tm // 2) + k * 128, 128), 128)
             own, oth = own_ref[cut, :], oth_ref[cut, :]
             pieces += [jnp.where(first, own, oth), jnp.where(first, oth, own)]
         rows = jnp.concatenate(pieces, axis=0)
+        f_tiles[slot] = jnp.dot(rows, f_scr[...], preferred_element_type=F32)
+        x_tiles[slot] = jnp.dot(rows, x_scr[...], preferred_element_type=F32)
+
+    def block(i, slot, mis, scl):
+        fetch(i).wait()
+        squares(jnp.minimum(i + 1, steps - 1), 1 - slot)
+        base = i * tm
         acc = jnp.zeros((48, tm), F32)
         wacc = jnp.zeros((16, tm), F32)
         for start in range(0, total, tn):
             cut = slice(start, start + tn)
-            f2 = jnp.dot(rows, f_scr[:, cut], preferred_element_type=F32)
-            x2 = jnp.dot(rows, x_scr[:, cut], preferred_element_type=F32)
-            wb = w_ref[at, cut]
-            w = wb.astype(F32)
-            f2 = jnp.maximum(f2, TINY)
-            x2 = jnp.maximum(x2, TINY)
-            dissim = f2 * lax.rsqrt(f2)
-            inv = lax.rsqrt(x2)
-            diff = dissim - x2 * inv
-            cmat = w * (dissim * jnp.minimum(inv, 1.0) - 1.0)
-            mis += jnp.sum((w * (diff * diff)).reshape(tm // 8, 8, tn), axis=0)
-            scl += jnp.sum((w * f2).reshape(tm // 8, 8, tn), axis=0)
-            acc += lax.dot_general(flat[:, cut], cmat.astype(BF16), last, preferred_element_type=F32)
-            wacc += lax.dot_general(flat[32:, cut], wb, last, preferred_element_type=F32)
+            for r in range(0, tm, 16):
+                f2 = jnp.maximum(f_tiles[slot, r : r + 16, cut], TINY)
+                x2 = jnp.maximum(x_tiles[slot, r : r + 16, cut], TINY)
+                w = w_ref[pl.ds(pl.multiple_of(base + r, 16), 16), cut].astype(F32)
+                dissim = f2 * lax.rsqrt(f2)
+                inv = lax.rsqrt(x2)
+                diff = dissim - x2 * inv
+                cmat = w * (dissim * jnp.minimum(inv, 1.0) - 1.0)
+                c_scr[r : r + 16, cut] = cmat.astype(BF16)
+                miss = w * (diff * diff)
+                size = w * f2
+                mis += miss[0:8] + miss[8:16]
+                scl += size[0:8] + size[8:16]
+            wb = w_ref[pl.ds(pl.multiple_of(base, tm), tm), cut]
+            acc += lax.dot_general(flat_scr[:, cut], c_scr[:, cut], last, preferred_element_type=F32)
+            wacc += lax.dot_general(flat_scr[32:, cut], wb, last, preferred_element_type=F32)
         pull = acc[0:16] + acc[16:32]
         rate = acc[32:33]
         wsum = wacc[0:1]
@@ -121,8 +127,15 @@
             out_ref[to, :, 1024:1152] = jnp.concatenate([rate[:, cut], wsum[:, cut]], axis=1)
         return mis, scl
 
+    def two(k, carry):
+        carry = block(2 * k, 0, *carry)
+        return block(2 * k + 1, 1, *carry)
+
+    squares(0, 0)
     zero = jnp.zeros((8, tn), F32)
-    mis, scl = lax.fori_loop(0, steps, block, (zero, zero))
+    mis, scl = lax.fori_loop(0, steps // 2, two, (zero, zero))
+    if steps % 2:
+        mis, scl = block(steps - 1, 0, mis, scl)
     mis = jnp.sum(jnp.sum(mis, axis=0, keepdims=True), axis=1, keepdims=True)
     scl = jnp.sum(jnp.sum(scl, axis=0, keepdims=True), axis=1, keepdims=True)
     at = lax.broadcasted_iota(jnp.int32, (1, 128), 1)
@@ -139,11 +152,6 @@
     wsum = lines[8][:, 64:128]
     crd = crd_ref[...]
     new_ref[...] = crd + (rate * crd - pull) / wsum
-
-
-def stress_kernel(part_ref, out_ref):
-    sums = jnp.sum(part_ref[...], axis=0)
-    out_ref[...] = sums[:, 0:1] / sums[:, 1:2]
 
 
 def column_moves(n_row, n_col, n_depth):
@@ -178,10 +186,10 @@
     t_cols = lax.all_to_all(moved, "row", 0, 0, tiled=True).reshape(cols, LANES)
 
     vmem = pl.BlockSpec(memory_space=pltpu.VMEM)
+    tm = 256
     parts = pl.pallas_call(
         pairs_kernel,
         in_specs=[
-            pl.BlockSpec(memory_space=pltpu.SMEM),
             vmem,
             vmem,
             vmem,
@@ -193,11 +201,15 @@
             pltpu.VMEM((rows, cols), BF16),
             pltpu.VMEM((LANES, cols), BF16),
             pltpu.VMEM((LANES, cols), BF16),
-            pltpu.SemaphoreType.DMA((max(1, rows // 1024),)),
+            pltpu.VMEM((48, cols), BF16),
+            pltpu.VMEM((tm, cols), BF16),
+            pltpu.VMEM((2, tm, cols), F32),
+            pltpu.VMEM((2, tm, cols), F32),
+            pltpu.SemaphoreType.DMA((rows // tm,)),
         ],
         compiler_params=pltpu.CompilerParams(vmem_limit_bytes=52 * 1024 * 1024),
         name="pairs",
-    )(lax.axis_index("core").reshape(1).astype(jnp.int32), own, oth, t_cols, pair_weight)
+    )(own, oth, t_cols, pair_weight)
     parts = lax.all_to_all(parts, ("z", "core", "depth"), 0, 0, tiled=True)
     shares = jnp.sum(parts[:, :, 1152:], axis=0, keepdims=True)
     shares = lax.all_to_all(jnp.broadcast_to(shares, (n_row, 1, 128)), "row", 0, 0, tiled=True)
@@ -207,12 +219,8 @@
         cost_estimate=pl.CostEstimate(flops=100000, bytes_accessed=200000, transcendentals=0),
         name="finish",
     )(parts, coords)
-    stress = pl.pallas_call(
-        stress_kernel,
-        out_shape=jax.ShapeDtypeStruct((1, 1), F32),
-        name="stress",
-    )(shares)
-    return (new_coords, stress[0, 0])
+    totals = jnp.sum(shares, axis=(0, 1))
+    return (new_coords, totals[0] / totals[1])
 
 
 def solution(mesh):

time: 91.8 us -> 92.9 us (1.012)
  between operations: 0.7 us -> 3.07 us
  Pallas kernels: 13.6 us -> 12.4 us
    pallas_call x2 -> x1, Pallas kernels: 10.4 us -> 9.16 us  [shards(): pl.pallas_call(pairs_kernel, in_specs=[vmem, vmem, vmem, pl.BlockSpec(mem...]
where the time goes in v5:
time: 92.9 us; the launch traced here: 92.1 us
  starting transfers between devices  39.3 us (42%)
  blocking collectives  21.5 us (23%)
  waiting for transfers between devices  13.8 us (15%)
  Pallas kernels  12.4 us (13%)
  between operations  3.07 us (3%)
  local copies, waits for them, and re-layouts  1.96 us (2%)
    all_to_all x1, blocking collectives, shards(): parts = lax.all_to_all(parts, ('z', 'core', 'depth'), 0, 0, tiled=True)  21.5 us
    all_to_all x1, starting transfers between devices, shards(): lax.all_to_all(packed[1], ('z', 'depth'), 0, 0, tiled=True)  12 us
    all_to_all x1, starting transfers between devices, shards(): t_cols = lax.all_to_all(moved, 'row', 0, 0, tiled=True).reshape(cols, LANES)  11.1 us
    pallas_call x1, Pallas kernels, shards(): pl.pallas_call(pairs_kernel, in_specs=[vmem, vmem, vmem, pl.BlockSpec(mem...  9.16 us
    ppermute x1, starting transfers between devices, shards(): moved = lax.ppermute(packed[0], ('row', 'z', 'core', 'depth'), moves)  7.39 us
    all_to_all x1, waiting for transfers between devices, shards(): lax.all_to_all(jnp.broadcast_to(shares, (n_row, 1, 128)), 'row', 0, 0, ti...  7.06 us
    ppermute x1, starting transfers between devices, shards(): oth = lax.ppermute(own, 'core', [(0, 1), (1, 0)])  5.34 us
    all_to_all x1, waiting for transfers between devices, shards(): t_cols = lax.all_to_all(moved, 'row', 0, 0, tiled=True).reshape(cols, LANES)  4.11 us
  transfers between devices with their start and end apart: 5, of which 5 were waited for; matrix products, arithmetic and copies ran while one was open for 0% of the time, Pallas kernels for 2%

profile of v5, /device:TPU:1, one launch (start us, length us, event | category | flops | bytes accessed | tf_op | source)
XLA Modules:
  0.0 92.1 jit_solution(9556415216739324111)
XLA Ops:
  0.6 1.5 %pack.1 = (bf16[64,128]{1,0:T(8,128)(2,1)}, bf16[16,64,128]{2,1,0:T(8,128)(2,1)}) custom-call(bf16[64,64]{1,0:T(8,128)(2,1)} %emb_ref.1, f32[16,64]{1,0:T(8,128)} %crd_ref.3), custom_call_target="tpu_custom_call" | custom-call | tf_op jit(solution)/shard_map/pack/pallas_call | solution.py:172
  2.2 12.0 %all-to-all-start = ((bf16[16,64,128]{2,1,0:T(8,128)(2,1)}), bf16[16,64,128]{2,1,0:T(8,128)(2,1)S(1)}, u32[]{:S(2)}, u32[]{:S(2)}) async-start(bf16[16,64,128]{2,1,0:T(8,128)(2,1)} %get-tuple-element.7), calls=%async_computation | async-start | bytes 524288 | tf_op jit(solution)/shard_map/all_to_all | solution.py:182
  14.1 7.4 %collective-permute-start = (bf16[64,128]{1,0:T(8,128)(2,1)}, bf16[64,128]{1,0:T(8,128)(2,1)S(1)}, u32[]{:S(2)}, u32[]{:S(2)}) collective-permute-start(bf16[64,128]{1,0:T(8,128)(2,1)} %get-tuple-element.6), channel_id=1, source_target_pairs={{0,0},{1,32},{2,64},{3,96},{4,128},{5,160},{6,192},{7,224},{8,256}... | collective-permute-start | bytes 49160 | tf_op jit(solution)/shard_map/ppermute | solution.py:181
  21.5 1.1 %collective-permute-done = bf16[64,128]{1,0:T(8,128)(2,1)S(1)} collective-permute-done((bf16[64,128]{1,0:T(8,128)(2,1)}, bf16[64,128]{1,0:T(8,128)(2,1)S(1)}, u32[]{:S(2)}, u32[]{:S(2)}) %collective-permute-start) | collective-permute-done | bytes 16416 | tf_op jit(solution)/shard_map/ppermute | solution.py:181
  22.6 0.5 all-to-all-done
  23.1 0.7 broadcast_in_dim.4
  23.8 11.1 %all-to-all-start.1 = ((bf16[16,64,128]{2,1,0:T(8,128)(2,1)}), bf16[16,64,128]{2,1,0:T(8,128)(2,1)S(1)}, u32[]{:S(2)}, u32[]{:S(2)}) async-start(bf16[16,64,128]{2,1,0:T(8,128)(2,1)} %broadcast_in_dim.4), calls=%async_computation.1 | async-start | bytes 524288 | tf_op jit(solution)/shard_map/all_to_all | solution.py:186
  34.9 5.3 %collective-permute-start.1 = (bf16[1024,128]{1,0:T(8,128)(2,1)S(1)}, bf16[1024,128]{1,0:T(8,128)(2,1)S(1)}, u32[]{:S(2)}, u32[]{:S(2)}) collective-permute-start(bf16[1024,128]{1,0:T(8,128)(2,1)S(1)} %bitcast.4), channel_id=1, source_target_pairs={{0,2},{2,0},{1,3},{3,1},{4,6},{6,4},{5,7},{7,5},{8,10},{10,8},{9,1... | collective-permute-start | bytes 786440 | tf_op jit(solution)/shard_map/ppermute | solution.py:184
  40.3 1.1 %collective-permute-done.1.oth_ref = bf16[1024,128]{1,0:T(8,128)(2,1)S(1)} collective-permute-done((bf16[1024,128]{1,0:T(8,128)(2,1)S(1)}, bf16[1024,128]{1,0:T(8,128)(2,1)S(1)}, u32[]{:S(2)}, u32[]{:S(2)}) %collective-permute-start.1) | collective-permute-done | bytes 262176 | tf_op jit(solution)/shard_map/ppermute | solution.py:184
  41.4 4.1 %all-to-all-done.1 = bf16[16,64,128]{2,1,0:T(8,128)(2,1)S(1)} async-done(((bf16[16,64,128]{2,1,0:T(8,128)(2,1)}), bf16[16,64,128]{2,1,0:T(8,128)(2,1)S(1)}, u32[]{:S(2)}, u32[]{:S(2)}) %all-to-all-start.1) | async-done | bytes 262176 | tf_op jit(solution)/shard_map/all_to_all | solution.py:186
  45.5 9.2 %pairs.1 = f32[32,1,1280]{2,1,0:T(1,128)S(1)} custom-call(bf16[1024,128]{1,0:T(8,128)(2,1)S(1)} %bitcast.5, bf16[1024,128]{1,0:T(8,128)(2,1)S(1)} %collective-permute-done.1.oth_ref, bf16[1024,128]{1,0:T(8,128)(2,1)S(1)} %bitcast.6, bf16[2048,1024]{1,0:T(8,128)(2,1)} %w_hbm.1), custom_call_target="tpu_custom_call" | custom-call | tf_op jit(solution)/shard_map/pairs/pallas_call | solution.py:190
  54.7 21.5 %all_to_all.20.part_ref = f32[32,1,1280]{2,1,0:T(1,128)S(1)} all-to-all(f32[32,1,1280]{2,1,0:T(1,128)S(1)} %pairs.1), channel_id=1, replica_groups=mesh['row'=16,'z'=8,'core'=2,'depth'=2] {'z','core','depth'}, dimensions={0} | all-to-all | bytes 327680 | tf_op jit(solution)/shard_map/all_to_all | solution.py:213
  76.2 0.0 copy-start
  76.2 0.6 broadcast_in_dim.5
  76.8 3.5 %all-to-all-start.3 = ((f32[16,1,128]{2,1,0:T(1,128)}), f32[16,1,128]{2,1,0:T(1,128)S(1)}, u32[]{:S(2)}, u32[]{:S(2)}) async-start(f32[16,1,128]{2,1,0:T(1,128)} %broadcast_in_dim.5), calls=%async_computation.3 | async-start | bytes 16384 | tf_op jit(solution)/shard_map/all_to_all | solution.py:215
  80.3 0.0 copy-done
  80.3 1.7 %finish.1 = f32[16,64]{1,0:T(8,128)} custom-call(f32[32,1,1280]{2,1,0:T(1,128)} %copy-done, f32[16,64]{1,0:T(8,128)} %crd_ref.3), custom_call_target="tpu_custom_call" | custom-call | flops 100000 | bytes 200000 | tf_op jit(solution)/shard_map/finish/pallas_call | solution.py:216
  82.0 7.1 %all-to-all-done.3 = f32[16,1,128]{2,1,0:T(1,128)S(1)} async-done(((f32[16,1,128]{2,1,0:T(1,128)}), f32[16,1,128]{2,1,0:T(1,128)S(1)}, u32[]{:S(2)}, u32[]{:S(2)}) %all-to-all-start.3) | async-done | bytes 8224 | tf_op jit(solution)/shard_map/all_to_all | solution.py:215
  89.1 0.6 fusion
  (2 shorter events, 0.1 us)
Async XLA Ops:
  2.2 20.9 %all-to-all-start = ((bf16[16,64,128]{2,1,0:T(8,128)(2,1)}), bf16[16,64,128]{2,1,0:T(8,128)(2,1)S(1)}, u32[]{:S(2)}, u32[]{:S(2)}) async-start(bf16[16,64,128]{2,1,0:T(8,128)(2,1)} %get-tuple-element.7), calls=%async_computation | async-start | bytes 524288 | tf_op jit(solution)/shard_map/all_to_all | solution.py:182
  14.1 8.5 %collective-permute-start = (bf16[64,128]{1,0:T(8,128)(2,1)}, bf16[64,128]{1,0:T(8,128)(2,1)S(1)}, u32[]{:S(2)}, u32[]{:S(2)}) collective-permute-start(bf16[64,128]{1,0:T(8,128)(2,1)} %get-tuple-element.6), channel_id=1, source_target_pairs={{0,0},{1,32},{2,64},{3,96},{4,128},{5,160},{6,192},{7,224},{8,256}... | collective-permute-start | bytes 49160 | tf_op jit(solution)/shard_map/ppermute | solution.py:181
  23.8 21.7 %all-to-all-start.1 = ((bf16[16,64,128]{2,1,0:T(8,128)(2,1)}), bf16[16,64,128]{2,1,0:T(8,128)(2,1)S(1)}, u32[]{:S(2)}, u32[]{:S(2)}) async-start(bf16[16,64,128]{2,1,0:T(8,128)(2,1)} %broadcast_in_dim.4), calls=%async_computation.1 | async-start | bytes 524288 | tf_op jit(solution)/shard_map/all_to_all | solution.py:186
  34.9 6.5 %collective-permute-start.1 = (bf16[1024,128]{1,0:T(8,128)(2,1)S(1)}, bf16[1024,128]{1,0:T(8,128)(2,1)S(1)}, u32[]{:S(2)}, u32[]{:S(2)}) collective-permute-start(bf16[1024,128]{1,0:T(8,128)(2,1)S(1)} %bitcast.4), channel_id=1, source_target_pairs={{0,2},{2,0},{1,3},{3,1},{4,6},{6,4},{5,7},{7,5},{8,10},{10,8},{9,1... | collective-permute-start | bytes 786440 | tf_op jit(solution)/shard_map/ppermute | solution.py:184
  76.2 4.2 %copy-start = (f32[32,1,1280]{2,1,0:T(1,128)}, f32[32,1,1280]{2,1,0:T(1,128)S(1)}, u32[]{:S(2)}) copy-start(f32[32,1,1280]{2,1,0:T(1,128)S(1)} %all_to_all.20.part_ref) | copy-start | bytes 491524
  76.8 12.2 %all-to-all-start.3 = ((f32[16,1,128]{2,1,0:T(1,128)}), f32[16,1,128]{2,1,0:T(1,128)S(1)}, u32[]{:S(2)}, u32[]{:S(2)}) async-start(f32[16,1,128]{2,1,0:T(1,128)} %broadcast_in_dim.5), calls=%async_computation.3 | async-start | bytes 16384 | tf_op jit(solution)/shard_map/all_to_all | solution.py:215

commit v6 on v5

--- a/solution.py
+++ b/solution.py
@@ -36,7 +36,7 @@
     return hi, mid, low
 
 
-def pack_kernel(emb_ref, crd_ref, own_ref, out_ref):
+def pack_kernel(emb_ref, crd_ref, own_ref):
     emb = emb_ref[...].astype(F32)
     crd = crd_ref[...]
     points = emb.shape[1]
@@ -49,10 +49,7 @@
     for k, sq in enumerate(squares):
         tail = jnp.where(lane == k, sq, tail)
     rows = jnp.concatenate([emb, hi, low, hi, tail], axis=0)
-    mine = rows.T.astype(BF16)
-    own_ref[...] = mine
-    for k in range(out_ref.shape[0]):
-        out_ref[k] = mine
+    own_ref[...] = rows.T.astype(BF16)
 
 
 def pick_sums():
@@ -103,10 +100,10 @@
                 f2 = jnp.maximum(f_tiles[slot, r : r + 16, cut], TINY)
                 x2 = jnp.maximum(x_tiles[slot, r : r + 16, cut], TINY)
                 w = w_ref[pl.ds(pl.multiple_of(base + r, 16), 16), cut].astype(F32)
-                dissim = f2 * lax.rsqrt(f2)
-                inv = lax.rsqrt(x2)
-                diff = dissim - x2 * inv
-                cmat = w * (dissim * jnp.minimum(inv, 1.0) - 1.0)
+                log_f = jnp.log(f2) * 0.5
+                log_x = jnp.log(x2) * 0.5
+                diff = jnp.exp(log_f) - jnp.exp(log_x)
+                cmat = w * (jnp.exp(log_f - jnp.maximum(log_x, 0.0)) - 1.0)
                 c_scr[r : r + 16, cut] = cmat.astype(BF16)
                 miss = w * (diff * diff)
                 size = w * f2
@@ -154,6 +151,11 @@
     new_ref[...] = crd + (rate * crd - pull) / wsum
 
 
+def stress_kernel(part_ref, out_ref):
+    sums = jnp.sum(part_ref[...], axis=0)
+    out_ref[...] = sums[:, 0:1] / sums[:, 1:2]
+
+
 def column_moves(n_row, n_col, n_depth):
     moves = []
     for row in range(n_row):
@@ -171,18 +173,18 @@
 
     packed = pl.pallas_call(
         pack_kernel,
-        out_shape=(
-            jax.ShapeDtypeStruct((points, LANES), BF16),
-            jax.ShapeDtypeStruct((likes, points, LANES), BF16),
-        ),
+        out_shape=jax.ShapeDtypeStruct((points, LANES), BF16),
         name="pack",
     )(embeddings, coords)
     moves = column_moves(n_row, n_z * n_core, n_depth)
-    moved = lax.ppermute(packed[0], ("row", "z", "core", "depth"), moves)
-    own = lax.all_to_all(packed[1], ("z", "depth"), 0, 0, tiled=True).reshape(rows // n_core, LANES)
+    moved = lax.ppermute(packed, ("row", "z", "core", "depth"), moves)
+    copies = jnp.broadcast_to(packed[None], (likes, points, LANES))
+    copies, moved = lax.optimization_barrier((copies, moved))
+    own = lax.all_to_all(copies, ("z", "depth"), 0, 0, tiled=True)
+    moved = jnp.broadcast_to(moved[None], (n_row, points, LANES))
     moved, own = lax.optimization_barrier((moved, own))
+    own = own.reshape(rows // n_core, LANES)
     oth = lax.ppermute(own, "core", [(0, 1), (1, 0)])
-    moved = jnp.broadcast_to(moved[None], (n_row, points, LANES))
     t_cols = lax.all_to_all(moved, "row", 0, 0, tiled=True).reshape(cols, LANES)
 
     vmem = pl.BlockSpec(memory_space=pltpu.VMEM)
@@ -219,8 +221,12 @@
         cost_estimate=pl.CostEstimate(flops=100000, bytes_accessed=200000, transcendentals=0),
         name="finish",
     )(parts, coords)
-    totals = jnp.sum(shares, axis=(0, 1))
-    return (new_coords, totals[0] / totals[1])
+    stress = pl.pallas_call(
+        stress_kernel,
+        out_shape=jax.ShapeDtypeStruct((1, 1), F32),
+        name="stress",
+    )(shares)
+    return (new_coords, stress[0, 0])
 
 
 def solution(mesh):

time: 92.9 us -> 101 us (1.087)
  blocking collectives: 21.5 us -> 42.1 us
  starting transfers between devices: 39.3 us -> 26.5 us
  Pallas kernels: 12.4 us -> 15.7 us
  between operations: 3.07 us -> 0.69 us
  waiting for transfers between devices: 13.8 us -> 12.6 us
    all_to_all x0 -> x1, blocking collectives: none -> 24 us  [shards(): own = lax.all_to_all(copies, ('z', 'depth'), 0, 0, tiled=True)]
    all_to_all x1 -> x0, starting transfers between devices: 12 us -> none  [shards(): lax.all_to_all(packed[1], ('z', 'depth'), 0, 0, tiled=True)]
    all_to_all x1, starting transfers between devices: 11.1 us -> 7.54 us  [shards(): t_cols = lax.all_to_all(moved, 'row', 0, 0, tiled=True).reshape(cols, LANES)]
    all_to_all x1, blocking collectives: 21.5 us -> 18 us  [shards(): parts = lax.all_to_all(parts, ('z', 'core', 'depth'), 0, 0, tiled=True)]
    pallas_call x1, Pallas kernels: 9.16 us -> 11.3 us  [shards(): pl.pallas_call(pairs_kernel, in_specs=[vmem, vmem, vmem, pl.BlockSpec(mem...]
    ppermute x1, starting transfers between devices: 7.39 us -> 8.83 us  [shards(): moved = lax.ppermute(packed, ('row', 'z', 'core', 'depth'), moves)]
    ppermute x1, starting transfers between devices: 5.34 us -> 6.67 us  [shards(): oth = lax.ppermute(own, 'core', [(0, 1), (1, 0)])]
    pallas_call x1 -> x2, Pallas kernels: 1.53 us -> 2.7 us  [the longest x1 1.4 us: shards(): pl.pallas_call(pack_kernel, out_shape=jax.ShapeDtypeStruct((points, LANES...]
  transfers between devices with their start and end apart: 5 -> 4, of which waited for: 5 -> 4; matrix products, arithmetic and copies ran while one was open for 0% -> 0% of each run, Pallas kernels for 2% -> 2%
where the time goes in v6:
time: 101 us; the launch traced here: 100 us
  blocking collectives  42.1 us (42%)
  starting transfers between devices  26.5 us (26%)
  Pallas kernels  15.7 us (16%)
  waiting for transfers between devices  12.6 us (12%)
  local copies, waits for them, and re-layouts  2.72 us (3%)
    all_to_all x1, blocking collectives, shards(): own = lax.all_to_all(copies, ('z', 'depth'), 0, 0, tiled=True)  24 us
    all_to_all x1, blocking collectives, shards(): parts = lax.all_to_all(parts, ('z', 'core', 'depth'), 0, 0, tiled=True)  18 us
    pallas_call x1, Pallas kernels, shards(): pl.pallas_call(pairs_kernel, in_specs=[vmem, vmem, vmem, pl.BlockSpec(mem...  11.3 us
    ppermute x1, starting transfers between devices, shards(): moved = lax.ppermute(packed, ('row', 'z', 'core', 'depth'), moves)  8.83 us
    all_to_all x1, starting transfers between devices, shards(): t_cols = lax.all_to_all(moved, 'row', 0, 0, tiled=True).reshape(cols, LANES)  7.54 us
    all_to_all x1, waiting for transfers between devices, shards(): lax.all_to_all(jnp.broadcast_to(shares, (n_row, 1, 128)), 'row', 0, 0, ti...  7.06 us
    ppermute x1, starting transfers between devices, shards(): oth = lax.ppermute(own, 'core', [(0, 1), (1, 0)])  6.67 us
    all_to_all x1, starting transfers between devices, shards(): lax.all_to_all(jnp.broadcast_to(shares, (n_row, 1, 128)), 'row', 0, 0, ti...  3.48 us
  transfers between devices with their start and end apart: 4, of which 4 were waited for; matrix products, arithmetic and copies ran while one was open for 0% of the time, Pallas kernels for 2%

profile of v6, /device:TPU:1, one launch (start us, length us, event | category | flops | bytes accessed | tf_op | source)
XLA Modules:
  0.0 100.4 jit_solution(13297347320574507621)
XLA Ops:
  0.6 1.4 %pack.1 = bf16[64,128]{1,0:T(8,128)(2,1)} custom-call(bf16[64,64]{1,0:T(8,128)(2,1)} %emb_ref.1, f32[16,64]{1,0:T(8,128)} %crd_ref.3), custom_call_target="tpu_custom_call" | custom-call | tf_op jit(solution)/shard_map/pack/pallas_call | solution.py:174
  2.0 8.8 %collective-permute-start = (bf16[64,128]{1,0:T(8,128)(2,1)}, bf16[64,128]{1,0:T(8,128)(2,1)S(1)}, u32[]{:S(2)}, u32[]{:S(2)}) collective-permute-start(bf16[64,128]{1,0:T(8,128)(2,1)} %pack.1), channel_id=1, source_target_pairs={{0,0},{1,32},{2,64},{3,96},{4,128},{5,160},{6,192},{7,224},{8,256}... | collective-permute-start | bytes 49160 | tf_op jit(solution)/shard_map/ppermute | solution.py:180
  10.9 1.1 %collective-permute-done = bf16[64,128]{1,0:T(8,128)(2,1)S(1)} collective-permute-done((bf16[64,128]{1,0:T(8,128)(2,1)}, bf16[64,128]{1,0:T(8,128)(2,1)S(1)}, u32[]{:S(2)}, u32[]{:S(2)}) %collective-permute-start) | collective-permute-done | bytes 16416 | tf_op jit(solution)/shard_map/ppermute | solution.py:180
  11.9 0.8 broadcast_in_dim.6
  12.7 24.0 %all_to_all.20 = bf16[16,64,128]{2,1,0:T(8,128)(2,1)S(1)} all-to-all(bf16[16,64,128]{2,1,0:T(8,128)(2,1)S(1)} %broadcast_in_dim.6), channel_id=1, replica_groups=mesh['row'=16,'z'=8,'core'=2,'depth'=2] {'z','depth'}, dimensions={0} | all-to-all | bytes 524288 | tf_op jit(solution)/shard_map/all_to_all | solution.py:183
  36.7 0.7 broadcast_in_dim.7
  37.5 7.5 %all-to-all-start.1 = ((bf16[16,64,128]{2,1,0:T(8,128)(2,1)}), bf16[16,64,128]{2,1,0:T(8,128)(2,1)S(1)}, u32[]{:S(2)}, u32[]{:S(2)}) async-start(bf16[16,64,128]{2,1,0:T(8,128)(2,1)} %broadcast_in_dim.7), calls=%async_computation.1 | async-start | bytes 524288 | tf_op jit(solution)/shard_map/all_to_all | solution.py:188
  45.0 6.7 %collective-permute-start.1 = (bf16[1024,128]{1,0:T(8,128)(2,1)S(1)}, bf16[1024,128]{1,0:T(8,128)(2,1)S(1)}, u32[]{:S(2)}, u32[]{:S(2)}) collective-permute-start(bf16[1024,128]{1,0:T(8,128)(2,1)S(1)} %bitcast.3), channel_id=1, source_target_pairs={{0,2},{2,0},{1,3},{3,1},{4,6},{6,4},{5,7},{7,5},{8,10},{10,8},{9,1... | collective-permute-start | bytes 786440 | tf_op jit(solution)/shard_map/ppermute | solution.py:187
  51.7 1.1 %collective-permute-done.1.oth_ref = bf16[1024,128]{1,0:T(8,128)(2,1)S(1)} collective-permute-done((bf16[1024,128]{1,0:T(8,128)(2,1)S(1)}, bf16[1024,128]{1,0:T(8,128)(2,1)S(1)}, u32[]{:S(2)}, u32[]{:S(2)}) %collective-permute-start.1) | collective-permute-done | bytes 262176 | tf_op jit(solution)/shard_map/ppermute | solution.py:187
  52.8 3.4 %all-to-all-done.1 = bf16[16,64,128]{2,1,0:T(8,128)(2,1)S(1)} async-done(((bf16[16,64,128]{2,1,0:T(8,128)(2,1)}), bf16[16,64,128]{2,1,0:T(8,128)(2,1)S(1)}, u32[]{:S(2)}, u32[]{:S(2)}) %all-to-all-start.1) | async-done | bytes 262176 | tf_op jit(solution)/shard_map/all_to_all | solution.py:188
  56.2 11.3 %pairs.1 = f32[32,1,1280]{2,1,0:T(1,128)S(1)} custom-call(bf16[1024,128]{1,0:T(8,128)(2,1)S(1)} %bitcast.4, bf16[1024,128]{1,0:T(8,128)(2,1)S(1)} %collective-permute-done.1.oth_ref, bf16[1024,128]{1,0:T(8,128)(2,1)S(1)} %bitcast.5, bf16[2048,1024]{1,0:T(8,128)(2,1)} %w_hbm.1), custom_call_target="tpu_custom_call" | custom-call | tf_op jit(solution)/shard_map/pairs/pallas_call | solution.py:192
  67.6 18.0 %all_to_all.21.part_ref = f32[32,1,1280]{2,1,0:T(1,128)S(1)} all-to-all(f32[32,1,1280]{2,1,0:T(1,128)S(1)} %pairs.1), channel_id=1, replica_groups=mesh['row'=16,'z'=8,'core'=2,'depth'=2] {'z','core','depth'}, dimensions={0} | all-to-all | bytes 327680 | tf_op jit(solution)/shard_map/all_to_all | solution.py:215
  85.6 0.0 copy-start
  85.7 0.6 broadcast_in_dim.8
  86.3 3.5 %all-to-all-start.3 = ((f32[16,1,128]{2,1,0:T(1,128)}), f32[16,1,128]{2,1,0:T(1,128)S(1)}, u32[]{:S(2)}, u32[]{:S(2)}) async-start(f32[16,1,128]{2,1,0:T(1,128)} %broadcast_in_dim.8), calls=%async_computation.3 | async-start | bytes 16384 | tf_op jit(solution)/shard_map/all_to_all | solution.py:217
  89.8 0.0 copy-done
  89.8 1.7 %finish.1 = f32[16,64]{1,0:T(8,128)} custom-call(f32[32,1,1280]{2,1,0:T(1,128)} %copy-done, f32[16,64]{1,0:T(8,128)} %crd_ref.3), custom_call_target="tpu_custom_call" | custom-call | flops 100000 | bytes 200000 | tf_op jit(solution)/shard_map/finish/pallas_call | solution.py:218
  91.5 7.1 %all-to-all-done.3.part_ref = f32[16,1,128]{2,1,0:T(1,128)S(1)} async-done(((f32[16,1,128]{2,1,0:T(1,128)}), f32[16,1,128]{2,1,0:T(1,128)S(1)}, u32[]{:S(2)}, u32[]{:S(2)}) %all-to-all-start.3) | async-done | bytes 8224 | tf_op jit(solution)/shard_map/all_to_all | solution.py:217
  98.5 0.0 copy-start.1
  98.5 0.6 copy-done.1
  99.1 1.3 %stress.1 = f32[1,1]{1,0:T(1,128)} custom-call(f32[16,1,128]{2,1,0:T(1,128)} %copy-done.1), custom_call_target="tpu_custom_call" | custom-call | tf_op jit(solution)/shard_map/stress/pallas_call | solution.py:224
  (1 shorter events, 0.0 us)
Async XLA Ops:
  2.0 9.9 %collective-permute-start = (bf16[64,128]{1,0:T(8,128)(2,1)}, bf16[64,128]{1,0:T(8,128)(2,1)S(1)}, u32[]{:S(2)}, u32[]{:S(2)}) collective-permute-start(bf16[64,128]{1,0:T(8,128)(2,1)} %pack.1), channel_id=1, source_target_pairs={{0,0},{1,32},{2,64},{3,96},{4,128},{5,160},{6,192},{7,224},{8,256}... | collective-permute-start | bytes 49160 | tf_op jit(solution)/shard_map/ppermute | solution.py:180
  37.5 18.8 %all-to-all-start.1 = ((bf16[16,64,128]{2,1,0:T(8,128)(2,1)}), bf16[16,64,128]{2,1,0:T(8,128)(2,1)S(1)}, u32[]{:S(2)}, u32[]{:S(2)}) async-start(bf16[16,64,128]{2,1,0:T(8,128)(2,1)} %broadcast_in_dim.7), calls=%async_computation.1 | async-start | bytes 524288 | tf_op jit(solution)/shard_map/all_to_all | solution.py:188
  45.0 7.8 %collective-permute-start.1 = (bf16[1024,128]{1,0:T(8,128)(2,1)S(1)}, bf16[1024,128]{1,0:T(8,128)(2,1)S(1)}, u32[]{:S(2)}, u32[]{:S(2)}) collective-permute-start(bf16[1024,128]{1,0:T(8,128)(2,1)S(1)} %bitcast.3), channel_id=1, source_target_pairs={{0,2},{2,0},{1,3},{3,1},{4,6},{6,4},{5,7},{7,5},{8,10},{10,8},{9,1... | collective-permute-start | bytes 786440 | tf_op jit(solution)/shard_map/ppermute | solution.py:187
  85.6 4.2 %copy-start = (f32[32,1,1280]{2,1,0:T(1,128)}, f32[32,1,1280]{2,1,0:T(1,128)S(1)}, u32[]{:S(2)}) copy-start(f32[32,1,1280]{2,1,0:T(1,128)S(1)} %all_to_all.21.part_ref) | copy-start | bytes 491524
  86.3 12.2 %all-to-all-start.3 = ((f32[16,1,128]{2,1,0:T(1,128)}), f32[16,1,128]{2,1,0:T(1,128)S(1)}, u32[]{:S(2)}, u32[]{:S(2)}) async-start(f32[16,1,128]{2,1,0:T(1,128)} %broadcast_in_dim.8), calls=%async_computation.3 | async-start | bytes 16384 | tf_op jit(solution)/shard_map/all_to_all | solution.py:217
  98.5 0.6 copy-start.1

commit v7 on v5

--- a/solution.py
+++ b/solution.py
@@ -55,13 +55,6 @@
         out_ref[k] = mine
 
 
-def pick_sums():
-    a = lax.broadcasted_iota(jnp.int32, (48, LANES), 0)
-    b = lax.broadcasted_iota(jnp.int32, (48, LANES), 1)
-    keep = ((a < 32) & (b == a + XH)) | ((a >= 32) & (b == ONE))
-    return jnp.where(keep, 1.0, 0.0).astype(BF16)
-
-
 def pairs_kernel(own_ref, oth_ref, col_ref, w_hbm, out_ref, w_ref, f_scr, x_scr, flat_scr, c_scr, f_tiles, x_tiles, sems):
     total_rows, total = w_ref.shape
     tm = c_scr.shape[0]
@@ -77,47 +70,54 @@
         fetch(i).start()
     all_cols = col_ref[...]
     last = (((1,), (1,)), ((), ()))
-    f_scr[...] = lax.dot_general(bilinear_form(0), all_cols, last, preferred_element_type=F32).astype(BF16)
+    form_f = bilinear_form(0)
+    f_scr[...] = lax.dot_general(form_f, all_cols, last, preferred_element_type=F32).astype(BF16)
     x_scr[...] = lax.dot_general(bilinear_form(1), all_cols, last, preferred_element_type=F32).astype(BF16)
-    flat_scr[...] = lax.dot_general(pick_sums(), all_cols, last, preferred_element_type=F32).astype(BF16)
-
-    def squares(i, slot):
+    a = lax.broadcasted_iota(jnp.int32, (LANES, LANES), 0)
+    b = lax.broadcasted_iota(jnp.int32, (LANES, LANES), 1)
+    same = jnp.where(a == b, 1.0, 0.0).astype(BF16)
+    flat_scr[...] = lax.dot_general(same, all_cols, last, preferred_element_type=F32).astype(BF16)
+
+    def row_block(i):
         pieces = []
         for k in range(tm // 256):
             cut = pl.ds(pl.multiple_of(i * (tm // 2) + k * 128, 128), 128)
             own, oth = own_ref[cut, :], oth_ref[cut, :]
             pieces += [jnp.where(first, own, oth), jnp.where(first, oth, own)]
-        rows = jnp.concatenate(pieces, axis=0)
+        return jnp.concatenate(pieces, axis=0)
+
+    def squares(rows, slot):
         f_tiles[slot] = jnp.dot(rows, f_scr[...], preferred_element_type=F32)
         x_tiles[slot] = jnp.dot(rows, x_scr[...], preferred_element_type=F32)
 
     def block(i, slot, mis, scl):
         fetch(i).wait()
-        squares(jnp.minimum(i + 1, steps - 1), 1 - slot)
+        squares(row_block(jnp.minimum(i + 1, steps - 1)), 1 - slot)
+        bent = lax.dot_general(form_f, row_block(i), last, preferred_element_type=F32)
         base = i * tm
         acc = jnp.zeros((48, tm), F32)
-        wacc = jnp.zeros((16, tm), F32)
+        wacc = jnp.zeros((LANES, tm), F32)
         for start in range(0, total, tn):
             cut = slice(start, start + tn)
             for r in range(0, tm, 16):
                 f2 = jnp.maximum(f_tiles[slot, r : r + 16, cut], TINY)
                 x2 = jnp.maximum(x_tiles[slot, r : r + 16, cut], TINY)
-                w = w_ref[pl.ds(pl.multiple_of(base + r, 16), 16), cut].astype(F32)
+                wb = w_ref[pl.ds(pl.multiple_of(base + r, 16), 16), cut]
                 dissim = f2 * lax.rsqrt(f2)
                 inv = lax.rsqrt(x2)
                 diff = dissim - x2 * inv
-                cmat = w * (dissim * jnp.minimum(inv, 1.0) - 1.0)
-                c_scr[r : r + 16, cut] = cmat.astype(BF16)
-                miss = w * (diff * diff)
-                size = w * f2
+                c_scr[r : r + 16, cut] = wb * (dissim * jnp.minimum(inv, 1.0)).astype(BF16)
+                miss = wb.astype(F32) * (diff * diff)
                 mis += miss[0:8] + miss[8:16]
-                scl += size[0:8] + size[8:16]
             wb = w_ref[pl.ds(pl.multiple_of(base, tm), tm), cut]
-            acc += lax.dot_general(flat_scr[:, cut], c_scr[:, cut], last, preferred_element_type=F32)
-            wacc += lax.dot_general(flat_scr[32:, cut], wb, last, preferred_element_type=F32)
-        pull = acc[0:16] + acc[16:32]
-        rate = acc[32:33]
-        wsum = wacc[0:1]
+            picked = jnp.concatenate([flat_scr[XH : XH + 32, cut], flat_scr[QF:, cut]], axis=0)
+            acc += lax.dot_general(picked, c_scr[:, cut], last, preferred_element_type=F32)
+            wacc += lax.dot_general(flat_scr[:, cut], wb, last, preferred_element_type=F32)
+        scl += jnp.sum((bent * wacc).reshape(LANES // 8, 8, tm), axis=0)
+        less = acc[0:32] - wacc[XH : XH + 32]
+        pull = less[0:16] + less[16:32]
+        wsum = wacc[ONE : ONE + 1]
+        rate = acc[32 + ONE - QF : 33 + ONE - QF] - wsum
         for k in range(tm // 64):
             cut = slice(64 * k, 64 * k + 64)
             to = i * (tm // 64) + k
@@ -131,9 +131,10 @@
         carry = block(2 * k, 0, *carry)
         return block(2 * k + 1, 1, *carry)
 
-    squares(0, 0)
-    zero = jnp.zeros((8, tn), F32)
-    mis, scl = lax.fori_loop(0, steps // 2, two, (zero, zero))
+    squares(row_block(0), 0)
+    mis, scl = lax.fori_loop(
+        0, steps // 2, two, (jnp.zeros((8, tn), F32), jnp.zeros((8, tm), F32))
+    )
     if steps % 2:
         mis, scl = block(steps - 1, 0, mis, scl)
     mis = jnp.sum(jnp.sum(mis, axis=0, keepdims=True), axis=1, keepdims=True)
@@ -152,6 +153,11 @@
     wsum = lines[8][:, 64:128]
     crd = crd_ref[...]
     new_ref[...] = crd + (rate * crd - pull) / wsum
+
+
+def stress_kernel(part_ref, out_ref):
+    sums = jnp.sum(part_ref[...], axis=0)
+    out_ref[...] = sums[:, 0:1] / sums[:, 1:2]
 
 
 def column_moves(n_row, n_col, n_depth):
@@ -180,9 +186,9 @@
     moves = column_moves(n_row, n_z * n_core, n_depth)
     moved = lax.ppermute(packed[0], ("row", "z", "core", "depth"), moves)
     own = lax.all_to_all(packed[1], ("z", "depth"), 0, 0, tiled=True).reshape(rows // n_core, LANES)
+    moved = jnp.broadcast_to(moved[None], (n_row, points, LANES))
     moved, own = lax.optimization_barrier((moved, own))
     oth = lax.ppermute(own, "core", [(0, 1), (1, 0)])
-    moved = jnp.broadcast_to(moved[None], (n_row, points, LANES))
     t_cols = lax.all_to_all(moved, "row", 0, 0, tiled=True).reshape(cols, LANES)
 
     vmem = pl.BlockSpec(memory_space=pltpu.VMEM)
@@ -201,7 +207,7 @@
             pltpu.VMEM((rows, cols), BF16),
             pltpu.VMEM((LANES, cols), BF16),
             pltpu.VMEM((LANES, cols), BF16),
-            pltpu.VMEM((48, cols), BF16),
+            pltpu.VMEM((LANES, cols), BF16),
             pltpu.VMEM((tm, cols), BF16),
             pltpu.VMEM((2, tm, cols), F32),
             pltpu.VMEM((2, tm, cols), F32),
@@ -219,8 +225,12 @@
         cost_estimate=pl.CostEstimate(flops=100000, bytes_accessed=200000, transcendentals=0),
         name="finish",
     )(parts, coords)
-    totals = jnp.sum(shares, axis=(0, 1))
-    return (new_coords, totals[0] / totals[1])
+    stress = pl.pallas_call(
+        stress_kernel,
+        out_shape=jax.ShapeDtypeStruct((1, 1), F32),
+        name="stress",
+    )(shares)
+    return (new_coords, stress[0, 0])
 
 
 def solution(mesh):

time: 92.9 us -> 91.9 us (0.989)
  between operations: 3.07 us -> 0.69 us
  Pallas kernels: 12.4 us -> 13.7 us
    pallas_call x0 -> x1, Pallas kernels: none -> 1.3 us  [shards(): pl.pallas_call(stress_kernel, out_shape=jax.ShapeDtypeStruct((1, 1), F32)...]
where the time goes in v7:
time: 91.9 us; the launch traced here: 90.9 us
  starting transfers between devices  39.3 us (43%)
  blocking collectives  21.5 us (23%)
  waiting for transfers between devices  13.8 us (15%)
  Pallas kernels  13.7 us (15%)
  local copies, waits for them, and re-layouts  1.94 us (2%)
    all_to_all x1, blocking collectives, shards(): parts = lax.all_to_all(parts, ('z', 'core', 'depth'), 0, 0, tiled=True)  21.5 us
    all_to_all x1, starting transfers between devices, shards(): lax.all_to_all(packed[1], ('z', 'depth'), 0, 0, tiled=True)  12 us
    all_to_all x1, starting transfers between devices, shards(): t_cols = lax.all_to_all(moved, 'row', 0, 0, tiled=True).reshape(cols, LANES)  11.1 us
    pallas_call x1, Pallas kernels, shards(): pl.pallas_call(pairs_kernel, in_specs=[vmem, vmem, vmem, pl.BlockSpec(mem...  9.15 us
    ppermute x1, starting transfers between devices, shards(): moved = lax.ppermute(packed[0], ('row', 'z', 'core', 'depth'), moves)  7.39 us
    all_to_all x1, waiting for transfers between devices, shards(): lax.all_to_all(jnp.broadcast_to(shares, (n_row, 1, 128)), 'row', 0, 0, ti...  7.06 us
    ppermute x1, starting transfers between devices, shards(): oth = lax.ppermute(own, 'core', [(0, 1), (1, 0)])  5.34 us
    all_to_all x1, waiting for transfers between devices, shards(): t_cols = lax.all_to_all(moved, 'row', 0, 0, tiled=True).reshape(cols, LANES)  4.11 us
  transfers between devices with their start and end apart: 5, of which 5 were waited for; matrix products, arithmetic and copies ran while one was open for 0% of the time, Pallas kernels for 2%

profile of v7, /device:TPU:1, one launch (start us, length us, event | category | flops | bytes accessed | tf_op | source)
XLA Modules:
  0.0 90.9 jit_solution(17246176491708195618)
XLA Ops:
  0.6 1.5 %pack.1 = (bf16[64,128]{1,0:T(8,128)(2,1)}, bf16[16,64,128]{2,1,0:T(8,128)(2,1)}) custom-call(bf16[64,64]{1,0:T(8,128)(2,1)} %emb_ref.1, f32[16,64]{1,0:T(8,128)} %crd_ref.3), custom_call_target="tpu_custom_call" | custom-call | tf_op jit(solution)/shard_map/pack/pallas_call | solution.py:178
  2.1 12.0 %all-to-all-start = ((bf16[16,64,128]{2,1,0:T(8,128)(2,1)}), bf16[16,64,128]{2,1,0:T(8,128)(2,1)S(1)}, u32[]{:S(2)}, u32[]{:S(2)}) async-start(bf16[16,64,128]{2,1,0:T(8,128)(2,1)} %get-tuple-element.7), calls=%async_computation | async-start | bytes 524288 | tf_op jit(solution)/shard_map/all_to_all | solution.py:188
  14.1 7.4 %collective-permute-start = (bf16[64,128]{1,0:T(8,128)(2,1)}, bf16[64,128]{1,0:T(8,128)(2,1)S(1)}, u32[]{:S(2)}, u32[]{:S(2)}) collective-permute-start(bf16[64,128]{1,0:T(8,128)(2,1)} %get-tuple-element.6), channel_id=1, source_target_pairs={{0,0},{1,32},{2,64},{3,96},{4,128},{5,160},{6,192},{7,224},{8,256}... | collective-permute-start | bytes 49160 | tf_op jit(solution)/shard_map/ppermute | solution.py:187
  21.5 1.1 %collective-permute-done = bf16[64,128]{1,0:T(8,128)(2,1)S(1)} collective-permute-done((bf16[64,128]{1,0:T(8,128)(2,1)}, bf16[64,128]{1,0:T(8,128)(2,1)S(1)}, u32[]{:S(2)}, u32[]{:S(2)}) %collective-permute-start) | collective-permute-done | bytes 16416 | tf_op jit(solution)/shard_map/ppermute | solution.py:187
  22.6 0.5 all-to-all-done
  23.1 0.7 broadcast_in_dim.4
  23.8 11.1 %all-to-all-start.1 = ((bf16[16,64,128]{2,1,0:T(8,128)(2,1)}), bf16[16,64,128]{2,1,0:T(8,128)(2,1)S(1)}, u32[]{:S(2)}, u32[]{:S(2)}) async-start(bf16[16,64,128]{2,1,0:T(8,128)(2,1)} %broadcast_in_dim.4), calls=%async_computation.1 | async-start | bytes 524288 | tf_op jit(solution)/shard_map/all_to_all | solution.py:192
  34.9 5.3 %collective-permute-start.1 = (bf16[1024,128]{1,0:T(8,128)(2,1)S(1)}, bf16[1024,128]{1,0:T(8,128)(2,1)S(1)}, u32[]{:S(2)}, u32[]{:S(2)}) collective-permute-start(bf16[1024,128]{1,0:T(8,128)(2,1)S(1)} %bitcast.3), channel_id=1, source_target_pairs={{0,2},{2,0},{1,3},{3,1},{4,6},{6,4},{5,7},{7,5},{8,10},{10,8},{9,1... | collective-permute-start | bytes 786440 | tf_op jit(solution)/shard_map/ppermute | solution.py:191
  40.3 1.1 %collective-permute-done.1.oth_ref = bf16[1024,128]{1,0:T(8,128)(2,1)S(1)} collective-permute-done((bf16[1024,128]{1,0:T(8,128)(2,1)S(1)}, bf16[1024,128]{1,0:T(8,128)(2,1)S(1)}, u32[]{:S(2)}, u32[]{:S(2)}) %collective-permute-start.1) | collective-permute-done | bytes 262176 | tf_op jit(solution)/shard_map/ppermute | solution.py:191
  41.4 4.1 %all-to-all-done.1 = bf16[16,64,128]{2,1,0:T(8,128)(2,1)S(1)} async-done(((bf16[16,64,128]{2,1,0:T(8,128)(2,1)}), bf16[16,64,128]{2,1,0:T(8,128)(2,1)S(1)}, u32[]{:S(2)}, u32[]{:S(2)}) %all-to-all-start.1) | async-done | bytes 262176 | tf_op jit(solution)/shard_map/all_to_all | solution.py:192
  45.5 9.1 %pairs.1 = f32[32,1,1280]{2,1,0:T(1,128)S(1)} custom-call(bf16[1024,128]{1,0:T(8,128)(2,1)S(1)} %bitcast.4, bf16[1024,128]{1,0:T(8,128)(2,1)S(1)} %collective-permute-done.1.oth_ref, bf16[1024,128]{1,0:T(8,128)(2,1)S(1)} %bitcast.5, bf16[2048,1024]{1,0:T(8,128)(2,1)} %w_hbm.1), custom_call_target="tpu_custom_call" | custom-call | tf_op jit(solution)/shard_map/pairs/pallas_call | solution.py:196
  54.7 21.5 %all_to_all.20.part_ref = f32[32,1,1280]{2,1,0:T(1,128)S(1)} all-to-all(f32[32,1,1280]{2,1,0:T(1,128)S(1)} %pairs.1), channel_id=1, replica_groups=mesh['row'=16,'z'=8,'core'=2,'depth'=2] {'z','core','depth'}, dimensions={0} | all-to-all | bytes 327680 | tf_op jit(solution)/shard_map/all_to_all | solution.py:219
  76.1 0.0 copy-start
  76.2 0.6 broadcast_in_dim.5
  76.8 3.5 %all-to-all-start.3 = ((f32[16,1,128]{2,1,0:T(1,128)}), f32[16,1,128]{2,1,0:T(1,128)S(1)}, u32[]{:S(2)}, u32[]{:S(2)}) async-start(f32[16,1,128]{2,1,0:T(1,128)} %broadcast_in_dim.5), calls=%async_computation.3 | async-start | bytes 16384 | tf_op jit(solution)/shard_map/all_to_all | solution.py:221
  80.3 0.0 copy-done
  80.3 1.7 %finish.1 = f32[16,64]{1,0:T(8,128)} custom-call(f32[32,1,1280]{2,1,0:T(1,128)} %copy-done, f32[16,64]{1,0:T(8,128)} %crd_ref.3), custom_call_target="tpu_custom_call" | custom-call | flops 100000 | bytes 200000 | tf_op jit(solution)/shard_map/finish/pallas_call | solution.py:222
  82.0 7.1 %all-to-all-done.3.part_ref = f32[16,1,128]{2,1,0:T(1,128)S(1)} async-done(((f32[16,1,128]{2,1,0:T(1,128)}), f32[16,1,128]{2,1,0:T(1,128)S(1)}, u32[]{:S(2)}, u32[]{:S(2)}) %all-to-all-start.3) | async-done | bytes 8224 | tf_op jit(solution)/shard_map/all_to_all | solution.py:221
  89.1 0.0 copy-start.1
  89.1 0.6 copy-done.1
  89.6 1.3 %stress.1 = f32[1,1]{1,0:T(1,128)} custom-call(f32[16,1,128]{2,1,0:T(1,128)} %copy-done.1), custom_call_target="tpu_custom_call" | custom-call | tf_op jit(solution)/shard_map/stress/pallas_call | solution.py:228
  (1 shorter events, 0.0 us)
Async XLA Ops:
  2.1 20.9 %all-to-all-start = ((bf16[16,64,128]{2,1,0:T(8,128)(2,1)}), bf16[16,64,128]{2,1,0:T(8,128)(2,1)S(1)}, u32[]{:S(2)}, u32[]{:S(2)}) async-start(bf16[16,64,128]{2,1,0:T(8,128)(2,1)} %get-tuple-element.7), calls=%async_computation | async-start | bytes 524288 | tf_op jit(solution)/shard_map/all_to_all | solution.py:188
  14.1 8.5 %collective-permute-start = (bf16[64,128]{1,0:T(8,128)(2,1)}, bf16[64,128]{1,0:T(8,128)(2,1)S(1)}, u32[]{:S(2)}, u32[]{:S(2)}) collective-permute-start(bf16[64,128]{1,0:T(8,128)(2,1)} %get-tuple-element.6), channel_id=1, source_target_pairs={{0,0},{1,32},{2,64},{3,96},{4,128},{5,160},{6,192},{7,224},{8,256}... | collective-permute-start | bytes 49160 | tf_op jit(solution)/shard_map/ppermute | solution.py:187
  23.8 21.7 %all-to-all-start.1 = ((bf16[16,64,128]{2,1,0:T(8,128)(2,1)}), bf16[16,64,128]{2,1,0:T(8,128)(2,1)S(1)}, u32[]{:S(2)}, u32[]{:S(2)}) async-start(bf16[16,64,128]{2,1,0:T(8,128)(2,1)} %broadcast_in_dim.4), calls=%async_computation.1 | async-start | bytes 524288 | tf_op jit(solution)/shard_map/all_to_all | solution.py:192
  34.9 6.5 %collective-permute-start.1 = (bf16[1024,128]{1,0:T(8,128)(2,1)S(1)}, bf16[1024,128]{1,0:T(8,128)(2,1)S(1)}, u32[]{:S(2)}, u32[]{:S(2)}) collective-permute-start(bf16[1024,128]{1,0:T(8,128)(2,1)S(1)} %bitcast.3), channel_id=1, source_target_pairs={{0,2},{2,0},{1,3},{3,1},{4,6},{6,4},{5,7},{7,5},{8,10},{10,8},{9,1... | collective-permute-start | bytes 786440 | tf_op jit(solution)/shard_map/ppermute | solution.py:191
  76.1 4.1 %copy-start = (f32[32,1,1280]{2,1,0:T(1,128)}, f32[32,1,1280]{2,1,0:T(1,128)S(1)}, u32[]{:S(2)}) copy-start(f32[32,1,1280]{2,1,0:T(1,128)S(1)} %all_to_all.20.part_ref) | copy-start | bytes 491524
  76.8 12.3 %all-to-all-start.3 = ((f32[16,1,128]{2,1,0:T(1,128)}), f32[16,1,128]{2,1,0:T(1,128)S(1)}, u32[]{:S(2)}, u32[]{:S(2)}) async-start(f32[16,1,128]{2,1,0:T(1,128)} %broadcast_in_dim.5), calls=%async_computation.3 | async-start | bytes 16384 | tf_op jit(solution)/shard_map/all_to_all | solution.py:221
  89.1 0.6 copy-start.1

commit v8 on v7

--- a/solution.py
+++ b/solution.py
@@ -90,25 +90,26 @@
         f_tiles[slot] = jnp.dot(rows, f_scr[...], preferred_element_type=F32)
         x_tiles[slot] = jnp.dot(rows, x_scr[...], preferred_element_type=F32)
 
-    def block(i, slot, mis, scl):
+    def block(i, slot, mis, scl, more=True):
         fetch(i).wait()
-        squares(row_block(jnp.minimum(i + 1, steps - 1)), 1 - slot)
+        if more:
+            squares(row_block(i + 1), 1 - slot)
         bent = lax.dot_general(form_f, row_block(i), last, preferred_element_type=F32)
         base = i * tm
         acc = jnp.zeros((48, tm), F32)
         wacc = jnp.zeros((LANES, tm), F32)
         for start in range(0, total, tn):
             cut = slice(start, start + tn)
-            for r in range(0, tm, 16):
-                f2 = jnp.maximum(f_tiles[slot, r : r + 16, cut], TINY)
-                x2 = jnp.maximum(x_tiles[slot, r : r + 16, cut], TINY)
-                wb = w_ref[pl.ds(pl.multiple_of(base + r, 16), 16), cut]
+            for r in range(0, tm, 32):
+                f2 = jnp.maximum(f_tiles[slot, r : r + 32, cut], TINY)
+                x2 = jnp.maximum(x_tiles[slot, r : r + 32, cut], TINY)
+                w = w_ref[pl.ds(pl.multiple_of(base + r, 32), 32), cut].astype(F32)
                 dissim = f2 * lax.rsqrt(f2)
                 inv = lax.rsqrt(x2)
                 diff = dissim - x2 * inv
-                c_scr[r : r + 16, cut] = wb * (dissim * jnp.minimum(inv, 1.0)).astype(BF16)
-                miss = wb.astype(F32) * (diff * diff)
-                mis += miss[0:8] + miss[8:16]
+                c_scr[r : r + 32, cut] = (w * (dissim * jnp.minimum(inv, 1.0))).astype(BF16)
+                miss = w * (diff * diff)
+                mis += (miss[0:8] + miss[8:16]) + (miss[16:24] + miss[24:32])
             wb = w_ref[pl.ds(pl.multiple_of(base, tm), tm), cut]
             picked = jnp.concatenate([flat_scr[XH : XH + 32, cut], flat_scr[QF:, cut]], axis=0)
             acc += lax.dot_general(picked, c_scr[:, cut], last, preferred_element_type=F32)
@@ -132,11 +133,11 @@
         return block(2 * k + 1, 1, *carry)
 
     squares(row_block(0), 0)
-    mis, scl = lax.fori_loop(
-        0, steps // 2, two, (jnp.zeros((8, tn), F32), jnp.zeros((8, tm), F32))
-    )
-    if steps % 2:
-        mis, scl = block(steps - 1, 0, mis, scl)
+    pairs = (steps - 1) // 2
+    sums = lax.fori_loop(0, pairs, two, (jnp.zeros((8, tn), F32), jnp.zeros((8, tm), F32)))
+    for i in range(2 * pairs, steps):
+        sums = block(i, i % 2, *sums, more=i + 1 < steps)
+    mis, scl = sums
     mis = jnp.sum(jnp.sum(mis, axis=0, keepdims=True), axis=1, keepdims=True)
     scl = jnp.sum(jnp.sum(scl, axis=0, keepdims=True), axis=1, keepdims=True)
     at = lax.broadcasted_iota(jnp.int32, (1, 128), 1)

time: 91.9 us -> 91.4 us (level)
  no operation moved by 1% of the time
where the time goes in v8:
time: 91.4 us; the launch traced here: 90.5 us
  starting transfers between devices  39.3 us (43%)
  blocking collectives  21.5 us (24%)
  waiting for transfers between devices  13.8 us (15%)
  Pallas kernels  13.2 us (14%)
  local copies, waits for them, and re-layouts  1.94 us (2%)
    all_to_all x1, blocking collectives, shards(): parts = lax.all_to_all(parts, ('z', 'core', 'depth'), 0, 0, tiled=True)  21.5 us
    all_to_all x1, starting transfers between devices, shards(): lax.all_to_all(packed[1], ('z', 'depth'), 0, 0, tiled=True)  12 us
    all_to_all x1, starting transfers between devices, shards(): t_cols = lax.all_to_all(moved, 'row', 0, 0, tiled=True).reshape(cols, LANES)  11.1 us
    pallas_call x1, Pallas kernels, shards(): pl.pallas_call(pairs_kernel, in_specs=[vmem, vmem, vmem, pl.BlockSpec(mem...  8.69 us
    ppermute x1, starting transfers between devices, shards(): moved = lax.ppermute(packed[0], ('row', 'z', 'core', 'depth'), moves)  7.39 us
    all_to_all x1, waiting for transfers between devices, shards(): lax.all_to_all(jnp.broadcast_to(shares, (n_row, 1, 128)), 'row', 0, 0, ti...  7.06 us
    ppermute x1, starting transfers between devices, shards(): oth = lax.ppermute(own, 'core', [(0, 1), (1, 0)])  5.34 us
    all_to_all x1, waiting for transfers between devices, shards(): t_cols = lax.all_to_all(moved, 'row', 0, 0, tiled=True).reshape(cols, LANES)  4.11 us
  transfers between devices with their start and end apart: 5, of which 5 were waited for; matrix products, arithmetic and copies ran while one was open for 0% of the time, Pallas kernels for 2%

profile of v8, /device:TPU:1, one launch (start us, length us, event | category | flops | bytes accessed | tf_op | source)
XLA Modules:
  0.0 90.5 jit_solution(17135371656738290690)
XLA Ops:
  0.6 1.5 %pack.1 = (bf16[64,128]{1,0:T(8,128)(2,1)}, bf16[16,64,128]{2,1,0:T(8,128)(2,1)}) custom-call(bf16[64,64]{1,0:T(8,128)(2,1)} %emb_ref.1, f32[16,64]{1,0:T(8,128)} %crd_ref.3), custom_call_target="tpu_custom_call" | custom-call | tf_op jit(solution)/shard_map/pack/pallas_call | solution.py:179
  2.1 12.0 %all-to-all-start = ((bf16[16,64,128]{2,1,0:T(8,128)(2,1)}), bf16[16,64,128]{2,1,0:T(8,128)(2,1)S(1)}, u32[]{:S(2)}, u32[]{:S(2)}) async-start(bf16[16,64,128]{2,1,0:T(8,128)(2,1)} %get-tuple-element.7), calls=%async_computation | async-start | bytes 524288 | tf_op jit(solution)/shard_map/all_to_all | solution.py:189
  14.1 7.4 %collective-permute-start = (bf16[64,128]{1,0:T(8,128)(2,1)}, bf16[64,128]{1,0:T(8,128)(2,1)S(1)}, u32[]{:S(2)}, u32[]{:S(2)}) collective-permute-start(bf16[64,128]{1,0:T(8,128)(2,1)} %get-tuple-element.6), channel_id=1, source_target_pairs={{0,0},{1,32},{2,64},{3,96},{4,128},{5,160},{6,192},{7,224},{8,256}... | collective-permute-start | bytes 49160 | tf_op jit(solution)/shard_map/ppermute | solution.py:188
  21.5 1.1 %collective-permute-done = bf16[64,128]{1,0:T(8,128)(2,1)S(1)} collective-permute-done((bf16[64,128]{1,0:T(8,128)(2,1)}, bf16[64,128]{1,0:T(8,128)(2,1)S(1)}, u32[]{:S(2)}, u32[]{:S(2)}) %collective-permute-start) | collective-permute-done | bytes 16416 | tf_op jit(solution)/shard_map/ppermute | solution.py:188
  22.6 0.5 all-to-all-done
  23.1 0.7 broadcast_in_dim.4
  23.8 11.1 %all-to-all-start.1 = ((bf16[16,64,128]{2,1,0:T(8,128)(2,1)}), bf16[16,64,128]{2,1,0:T(8,128)(2,1)S(1)}, u32[]{:S(2)}, u32[]{:S(2)}) async-start(bf16[16,64,128]{2,1,0:T(8,128)(2,1)} %broadcast_in_dim.4), calls=%async_computation.1 | async-start | bytes 524288 | tf_op jit(solution)/shard_map/all_to_all | solution.py:193
  34.9 5.3 %collective-permute-start.1 = (bf16[1024,128]{1,0:T(8,128)(2,1)S(1)}, bf16[1024,128]{1,0:T(8,128)(2,1)S(1)}, u32[]{:S(2)}, u32[]{:S(2)}) collective-permute-start(bf16[1024,128]{1,0:T(8,128)(2,1)S(1)} %bitcast.3), channel_id=1, source_target_pairs={{0,2},{2,0},{1,3},{3,1},{4,6},{6,4},{5,7},{7,5},{8,10},{10,8},{9,1... | collective-permute-start | bytes 786440 | tf_op jit(solution)/shard_map/ppermute | solution.py:192
  40.3 1.1 %collective-permute-done.1.oth_ref = bf16[1024,128]{1,0:T(8,128)(2,1)S(1)} collective-permute-done((bf16[1024,128]{1,0:T(8,128)(2,1)S(1)}, bf16[1024,128]{1,0:T(8,128)(2,1)S(1)}, u32[]{:S(2)}, u32[]{:S(2)}) %collective-permute-start.1) | collective-permute-done | bytes 262176 | tf_op jit(solution)/shard_map/ppermute | solution.py:192
  41.4 4.1 %all-to-all-done.1 = bf16[16,64,128]{2,1,0:T(8,128)(2,1)S(1)} async-done(((bf16[16,64,128]{2,1,0:T(8,128)(2,1)}), bf16[16,64,128]{2,1,0:T(8,128)(2,1)S(1)}, u32[]{:S(2)}, u32[]{:S(2)}) %all-to-all-start.1) | async-done | bytes 262176 | tf_op jit(solution)/shard_map/all_to_all | solution.py:193
  45.5 8.7 %pairs.1 = f32[32,1,1280]{2,1,0:T(1,128)S(1)} custom-call(bf16[1024,128]{1,0:T(8,128)(2,1)S(1)} %bitcast.4, bf16[1024,128]{1,0:T(8,128)(2,1)S(1)} %collective-permute-done.1.oth_ref, bf16[1024,128]{1,0:T(8,128)(2,1)S(1)} %bitcast.5, bf16[2048,1024]{1,0:T(8,128)(2,1)} %w_hbm.1), custom_call_target="tpu_custom_call" | custom-call | tf_op jit(solution)/shard_map/pairs/pallas_call | solution.py:197
  54.2 21.5 %all_to_all.20.part_ref = f32[32,1,1280]{2,1,0:T(1,128)S(1)} all-to-all(f32[32,1,1280]{2,1,0:T(1,128)S(1)} %pairs.1), channel_id=1, replica_groups=mesh['row'=16,'z'=8,'core'=2,'depth'=2] {'z','core','depth'}, dimensions={0} | all-to-all | bytes 327680 | tf_op jit(solution)/shard_map/all_to_all | solution.py:220
  75.7 0.0 copy-start
  75.7 0.6 broadcast_in_dim.5
  76.3 3.5 %all-to-all-start.3 = ((f32[16,1,128]{2,1,0:T(1,128)}), f32[16,1,128]{2,1,0:T(1,128)S(1)}, u32[]{:S(2)}, u32[]{:S(2)}) async-start(f32[16,1,128]{2,1,0:T(1,128)} %broadcast_in_dim.5), calls=%async_computation.3 | async-start | bytes 16384 | tf_op jit(solution)/shard_map/all_to_all | solution.py:222
  79.8 0.0 copy-done
  79.8 1.7 %finish.1 = f32[16,64]{1,0:T(8,128)} custom-call(f32[32,1,1280]{2,1,0:T(1,128)} %copy-done, f32[16,64]{1,0:T(8,128)} %crd_ref.3), custom_call_target="tpu_custom_call" | custom-call | flops 100000 | bytes 200000 | tf_op jit(solution)/shard_map/finish/pallas_call | solution.py:223
  81.5 7.1 %all-to-all-done.3.part_ref = f32[16,1,128]{2,1,0:T(1,128)S(1)} async-done(((f32[16,1,128]{2,1,0:T(1,128)}), f32[16,1,128]{2,1,0:T(1,128)S(1)}, u32[]{:S(2)}, u32[]{:S(2)}) %all-to-all-start.3) | async-done | bytes 8224 | tf_op jit(solution)/shard_map/all_to_all | solution.py:222
  88.6 0.0 copy-start.1
  88.6 0.6 copy-done.1
  89.2 1.3 %stress.1 = f32[1,1]{1,0:T(1,128)} custom-call(f32[16,1,128]{2,1,0:T(1,128)} %copy-done.1), custom_call_target="tpu_custom_call" | custom-call | tf_op jit(solution)/shard_map/stress/pallas_call | solution.py:229
  (1 shorter events, 0.0 us)
Async XLA Ops:
  2.1 20.9 %all-to-all-start = ((bf16[16,64,128]{2,1,0:T(8,128)(2,1)}), bf16[16,64,128]{2,1,0:T(8,128)(2,1)S(1)}, u32[]{:S(2)}, u32[]{:S(2)}) async-start(bf16[16,64,128]{2,1,0:T(8,128)(2,1)} %get-tuple-element.7), calls=%async_computation | async-start | bytes 524288 | tf_op jit(solution)/shard_map/all_to_all | solution.py:189
  14.1 8.5 %collective-permute-start = (bf16[64,128]{1,0:T(8,128)(2,1)}, bf16[64,128]{1,0:T(8,128)(2,1)S(1)}, u32[]{:S(2)}, u32[]{:S(2)}) collective-permute-start(bf16[64,128]{1,0:T(8,128)(2,1)} %get-tuple-element.6), channel_id=1, source_target_pairs={{0,0},{1,32},{2,64},{3,96},{4,128},{5,160},{6,192},{7,224},{8,256}... | collective-permute-start | bytes 49160 | tf_op jit(solution)/shard_map/ppermute | solution.py:188
  23.8 21.7 %all-to-all-start.1 = ((bf16[16,64,128]{2,1,0:T(8,128)(2,1)}), bf16[16,64,128]{2,1,0:T(8,128)(2,1)S(1)}, u32[]{:S(2)}, u32[]{:S(2)}) async-start(bf16[16,64,128]{2,1,0:T(8,128)(2,1)} %broadcast_in_dim.4), calls=%async_computation.1 | async-start | bytes 524288 | tf_op jit(solution)/shard_map/all_to_all | solution.py:193
  34.9 6.5 %collective-permute-start.1 = (bf16[1024,128]{1,0:T(8,128)(2,1)S(1)}, bf16[1024,128]{1,0:T(8,128)(2,1)S(1)}, u32[]{:S(2)}, u32[]{:S(2)}) collective-permute-start(bf16[1024,128]{1,0:T(8,128)(2,1)S(1)} %bitcast.3), channel_id=1, source_target_pairs={{0,2},{2,0},{1,3},{3,1},{4,6},{6,4},{5,7},{7,5},{8,10},{10,8},{9,1... | collective-permute-start | bytes 786440 | tf_op jit(solution)/shard_map/ppermute | solution.py:192
  75.7 4.1 %copy-start = (f32[32,1,1280]{2,1,0:T(1,128)}, f32[32,1,1280]{2,1,0:T(1,128)S(1)}, u32[]{:S(2)}) copy-start(f32[32,1,1280]{2,1,0:T(1,128)S(1)} %all_to_all.20.part_ref) | copy-start | bytes 491524
  76.3 12.3 %all-to-all-start.3 = ((f32[16,1,128]{2,1,0:T(1,128)}), f32[16,1,128]{2,1,0:T(1,128)S(1)}, u32[]{:S(2)}, u32[]{:S(2)}) async-start(f32[16,1,128]{2,1,0:T(1,128)} %broadcast_in_dim.5), calls=%async_computation.3 | async-start | bytes 16384 | tf_op jit(solution)/shard_map/all_to_all | solution.py:222
  88.6 0.6 copy-start.1

commit v9 on v8

--- a/solution.py
+++ b/solution.py
@@ -55,9 +55,15 @@
         out_ref[k] = mine
 
 
+def spread_kernel(own_ref, out_ref):
+    own = own_ref[...]
+    for k in range(out_ref.shape[0]):
+        out_ref[k] = own
+
+
 def pairs_kernel(own_ref, oth_ref, col_ref, w_hbm, out_ref, w_ref, f_scr, x_scr, flat_scr, c_scr, f_tiles, x_tiles, sems):
     total_rows, total = w_ref.shape
-    tm = c_scr.shape[0]
+    tm = c_scr.shape[1]
     tn = min(256, total)
     steps = total_rows // tm
     first = lax.axis_index("core") == 0
@@ -90,14 +96,8 @@
         f_tiles[slot] = jnp.dot(rows, f_scr[...], preferred_element_type=F32)
         x_tiles[slot] = jnp.dot(rows, x_scr[...], preferred_element_type=F32)
 
-    def block(i, slot, mis, scl, more=True):
-        fetch(i).wait()
-        if more:
-            squares(row_block(i + 1), 1 - slot)
-        bent = lax.dot_general(form_f, row_block(i), last, preferred_element_type=F32)
+    def chain(i, slot, mis):
         base = i * tm
-        acc = jnp.zeros((48, tm), F32)
-        wacc = jnp.zeros((LANES, tm), F32)
         for start in range(0, total, tn):
             cut = slice(start, start + tn)
             for r in range(0, tm, 32):
@@ -107,13 +107,18 @@
                 dissim = f2 * lax.rsqrt(f2)
                 inv = lax.rsqrt(x2)
                 diff = dissim - x2 * inv
-                c_scr[r : r + 32, cut] = (w * (dissim * jnp.minimum(inv, 1.0))).astype(BF16)
+                c_scr[slot, r : r + 32, cut] = (w * (dissim * jnp.minimum(inv, 1.0))).astype(BF16)
                 miss = w * (diff * diff)
                 mis += (miss[0:8] + miss[8:16]) + (miss[16:24] + miss[24:32])
-            wb = w_ref[pl.ds(pl.multiple_of(base, tm), tm), cut]
-            picked = jnp.concatenate([flat_scr[XH : XH + 32, cut], flat_scr[QF:, cut]], axis=0)
-            acc += lax.dot_general(picked, c_scr[:, cut], last, preferred_element_type=F32)
-            wacc += lax.dot_general(flat_scr[:, cut], wb, last, preferred_element_type=F32)
+        return mis
+
+    def sums_of(i, slot, scl):
+        rows = row_block(i)
+        bent = lax.dot_general(form_f, rows, last, preferred_element_type=F32)
+        picked = jnp.concatenate([flat_scr[XH : XH + 32, :], flat_scr[QF:, :]], axis=0)
+        acc = lax.dot_general(picked, c_scr[slot], last, preferred_element_type=F32)
+        wb = w_ref[pl.ds(pl.multiple_of(i * tm, tm), tm), :]
+        wacc = lax.dot_general(flat_scr[...], wb, last, preferred_element_type=F32)
         scl += jnp.sum((bent * wacc).reshape(LANES // 8, 8, tm), axis=0)
         less = acc[0:32] - wacc[XH : XH + 32]
         pull = less[0:16] + less[16:32]
@@ -126,18 +131,29 @@
                 line = jnp.concatenate([pull[j : j + 1, cut], pull[j + 8 : j + 9, cut]], axis=1)
                 out_ref[to, :, 128 * j : 128 * j + 128] = line
             out_ref[to, :, 1024:1152] = jnp.concatenate([rate[:, cut], wsum[:, cut]], axis=1)
-        return mis, scl
+        return scl
+
+    def stage(i, slot, mis, scl, ahead=True, behind=True):
+        fetch(i).wait()
+        if ahead:
+            squares(row_block(i + 1), 1 - slot)
+        if behind:
+            scl = sums_of(i - 1, 1 - slot, scl)
+        return chain(i, slot, mis), scl
 
     def two(k, carry):
-        carry = block(2 * k, 0, *carry)
-        return block(2 * k + 1, 1, *carry)
+        carry = stage(2 * k + 1, 1, *carry)
+        return stage(2 * k + 2, 0, *carry)
 
     squares(row_block(0), 0)
-    pairs = (steps - 1) // 2
-    sums = lax.fori_loop(0, pairs, two, (jnp.zeros((8, tn), F32), jnp.zeros((8, tm), F32)))
-    for i in range(2 * pairs, steps):
-        sums = block(i, i % 2, *sums, more=i + 1 < steps)
-    mis, scl = sums
+    carry = (jnp.zeros((8, tn), F32), jnp.zeros((8, tm), F32))
+    carry = stage(0, 0, *carry, ahead=steps > 1, behind=False)
+    loops = max(0, (steps - 2) // 2)
+    carry = lax.fori_loop(0, loops, two, carry)
+    for i in range(2 * loops + 1, steps):
+        carry = stage(i, i % 2, *carry, ahead=i + 1 < steps)
+    mis, scl = carry
+    scl = sums_of(steps - 1, (steps - 1) % 2, scl)
     mis = jnp.sum(jnp.sum(mis, axis=0, keepdims=True), axis=1, keepdims=True)
     scl = jnp.sum(jnp.sum(scl, axis=0, keepdims=True), axis=1, keepdims=True)
     at = lax.broadcasted_iota(jnp.int32, (1, 128), 1)
@@ -187,7 +203,12 @@
     moves = column_moves(n_row, n_z * n_core, n_depth)
     moved = lax.ppermute(packed[0], ("row", "z", "core", "depth"), moves)
     own = lax.all_to_all(packed[1], ("z", "depth"), 0, 0, tiled=True).reshape(rows // n_core, LANES)
-    moved = jnp.broadcast_to(moved[None], (n_row, points, LANES))
+    moved = pl.pallas_call(
+        spread_kernel,
+        out_shape=jax.ShapeDtypeStruct((n_row, points, LANES), BF16),
+        cost_estimate=pl.CostEstimate(flops=10**10, bytes_accessed=10**8, transcendentals=0),
+        name="spread",
+    )(moved)
     moved, own = lax.optimization_barrier((moved, own))
     oth = lax.ppermute(own, "core", [(0, 1), (1, 0)])
     t_cols = lax.all_to_all(moved, "row", 0, 0, tiled=True).reshape(cols, LANES)
@@ -209,7 +230,7 @@
             pltpu.VMEM((LANES, cols), BF16),
             pltpu.VMEM((LANES, cols), BF16),
             pltpu.VMEM((LANES, cols), BF16),
-            pltpu.VMEM((tm, cols), BF16),
+            pltpu.VMEM((2, tm, cols), BF16),
             pltpu.VMEM((2, tm, cols), F32),
             pltpu.VMEM((2, tm, cols), F32),
             pltpu.SemaphoreType.DMA((rows // tm,)),

time: 91.4 us -> 93.1 us (1.019)
  waiting for transfers between devices: 13.8 us -> 25 us
  starting transfers between devices: 39.3 us -> 32.5 us
  blocking collectives: 21.5 us -> 15.5 us
  Pallas kernels: 13.2 us -> 16.6 us
    all_to_all x1, waiting for transfers between devices: 0.47 us -> 9.61 us  [shards(): lax.all_to_all(packed[1], ('z', 'depth'), 0, 0, tiled=True)]
    all_to_all x1, blocking collectives: 21.5 us -> 15.5 us  [shards(): parts = lax.all_to_all(parts, ('z', 'core', 'depth'), 0, 0, tiled=True)]
    all_to_all x1, starting transfers between devices: 12 us -> 6.57 us  [shards(): lax.all_to_all(packed[1], ('z', 'depth'), 0, 0, tiled=True)]
    all_to_all x1, waiting for transfers between devices: 4.11 us -> 7.15 us  [shards(): t_cols = lax.all_to_all(moved, 'row', 0, 0, tiled=True).reshape(cols, LANES)]
    all_to_all x1, starting transfers between devices: 11.1 us -> 9.17 us  [shards(): t_cols = lax.all_to_all(moved, 'row', 0, 0, tiled=True).reshape(cols, LANES)]
    pallas_call x1, Pallas kernels: 8.69 us -> 10.6 us  [shards(): pl.pallas_call(pairs_kernel, in_specs=[vmem, vmem, vmem, pl.BlockSpec(mem...]
    pallas_call x0 -> x1, Pallas kernels: none -> 1.47 us  [shards(): pl.pallas_call(spread_kernel, out_shape=jax.ShapeDtypeStruct((n_row, poin...]
    ppermute x1, starting transfers between devices: 7.39 us -> 8.83 us  [shards(): moved = lax.ppermute(packed[0], ('row', 'z', 'core', 'depth'), moves)]
  transfers between devices with their start and end apart: 5 -> 5, of which waited for: 5 -> 4; matrix products, arithmetic and copies ran while one was open for 0% -> 0% of each run, Pallas kernels for 2% -> 3%
where the time goes in v9:
time: 93.1 us; the launch traced here: 92.1 us
  starting transfers between devices  32.5 us (35%)
  waiting for transfers between devices  25 us (27%)
  Pallas kernels  16.6 us (18%)
  blocking collectives  15.5 us (17%)
  local copies, waits for them, and re-layouts  1.79 us (2%)
    all_to_all x1, blocking collectives, shards(): parts = lax.all_to_all(parts, ('z', 'core', 'depth'), 0, 0, tiled=True)  15.5 us
    pallas_call x1, Pallas kernels, shards(): pl.pallas_call(pairs_kernel, in_specs=[vmem, vmem, vmem, pl.BlockSpec(mem...  10.6 us
    all_to_all x1, waiting for transfers between devices, shards(): lax.all_to_all(packed[1], ('z', 'depth'), 0, 0, tiled=True)  9.61 us
    all_to_all x1, starting transfers between devices, shards(): t_cols = lax.all_to_all(moved, 'row', 0, 0, tiled=True).reshape(cols, LANES)  9.17 us
    ppermute x1, starting transfers between devices, shards(): moved = lax.ppermute(packed[0], ('row', 'z', 'core', 'depth'), moves)  8.83 us
    all_to_all x1, waiting for transfers between devices, shards(): t_cols = lax.all_to_all(moved, 'row', 0, 0, tiled=True).reshape(cols, LANES)  7.15 us
    all_to_all x1, waiting for transfers between devices, shards(): lax.all_to_all(jnp.broadcast_to(shares, (n_row, 1, 128)), 'row', 0, 0, ti...  7.06 us
    all_to_all x1, starting transfers between devices, shards(): lax.all_to_all(packed[1], ('z', 'depth'), 0, 0, tiled=True)  6.57 us
  transfers between devices with their start and end apart: 5, of which 4 were waited for; matrix products, arithmetic and copies ran while one was open for 0% of the time, Pallas kernels for 3%

profile of v9, /device:TPU:1, one launch (start us, length us, event | category | flops | bytes accessed | tf_op | source)
XLA Modules:
  0.0 92.1 jit_solution(15385761082274590710)
XLA Ops:
  0.6 1.5 %pack.1 = (bf16[64,128]{1,0:T(8,128)(2,1)}, bf16[16,64,128]{2,1,0:T(8,128)(2,1)}) custom-call(bf16[64,64]{1,0:T(8,128)(2,1)} %emb_ref.1, f32[16,64]{1,0:T(8,128)} %crd_ref.3), custom_call_target="tpu_custom_call" | custom-call | tf_op jit(solution)/shard_map/pack/pallas_call | solution.py:195
  2.2 8.8 %collective-permute-start = (bf16[64,128]{1,0:T(8,128)(2,1)}, bf16[64,128]{1,0:T(8,128)(2,1)S(1)}, u32[]{:S(2)}, u32[]{:S(2)}) collective-permute-start(bf16[64,128]{1,0:T(8,128)(2,1)} %get-tuple-element.6), channel_id=1, source_target_pairs={{0,0},{1,32},{2,64},{3,96},{4,128},{5,160},{6,192},{7,224},{8,256}... | collective-permute-start | bytes 49160 | tf_op jit(solution)/shard_map/ppermute | solution.py:204
  11.0 6.6 %all-to-all-start = ((bf16[16,64,128]{2,1,0:T(8,128)(2,1)}), bf16[16,64,128]{2,1,0:T(8,128)(2,1)S(1)}, u32[]{:S(2)}, u32[]{:S(2)}) async-start(bf16[16,64,128]{2,1,0:T(8,128)(2,1)} %get-tuple-element.7), calls=%async_computation | async-start | bytes 524288 | tf_op jit(solution)/shard_map/all_to_all | solution.py:205
  17.6 0.0 collective-permute-done.own_ref
  17.6 0.0 copy-start.2
  17.6 0.6 copy-done.2
  18.2 1.5 %spread.1 = bf16[16,64,128]{2,1,0:T(8,128)(2,1)} custom-call(bf16[64,128]{1,0:T(8,128)(2,1)} %copy-done.2), custom_call_target="tpu_custom_call" | custom-call | flops 10000000000 | bytes 100000000 | tf_op jit(solution)/shard_map/spread/pallas_call | solution.py:206
  19.7 9.6 %all-to-all-done = bf16[16,64,128]{2,1,0:T(8,128)(2,1)S(1)} async-done(((bf16[16,64,128]{2,1,0:T(8,128)(2,1)}), bf16[16,64,128]{2,1,0:T(8,128)(2,1)S(1)}, u32[]{:S(2)}, u32[]{:S(2)}) %all-to-all-start) | async-done | bytes 262176 | tf_op jit(solution)/shard_map/all_to_all | solution.py:205
  29.3 9.2 %all-to-all-start.1 = ((bf16[16,64,128]{2,1,0:T(8,128)(2,1)}), bf16[16,64,128]{2,1,0:T(8,128)(2,1)S(1)}, u32[]{:S(2)}, u32[]{:S(2)}) async-start(bf16[16,64,128]{2,1,0:T(8,128)(2,1)} %spread.1), calls=%async_computation.1 | async-start | bytes 524288 | tf_op jit(solution)/shard_map/all_to_all | solution.py:214
  38.4 4.4 %collective-permute-start.1 = (bf16[1024,128]{1,0:T(8,128)(2,1)S(1)}, bf16[1024,128]{1,0:T(8,128)(2,1)S(1)}, u32[]{:S(2)}, u32[]{:S(2)}) collective-permute-start(bf16[1024,128]{1,0:T(8,128)(2,1)S(1)} %bitcast.3), channel_id=1, source_target_pairs={{0,2},{2,0},{1,3},{3,1},{4,6},{6,4},{5,7},{7,5},{8,10},{10,8},{9,1... | collective-permute-start | bytes 786440 | tf_op jit(solution)/shard_map/ppermute | solution.py:213
  42.9 1.1 %collective-permute-done.1.oth_ref = bf16[1024,128]{1,0:T(8,128)(2,1)S(1)} collective-permute-done((bf16[1024,128]{1,0:T(8,128)(2,1)S(1)}, bf16[1024,128]{1,0:T(8,128)(2,1)S(1)}, u32[]{:S(2)}, u32[]{:S(2)}) %collective-permute-start.1) | collective-permute-done | bytes 262176 | tf_op jit(solution)/shard_map/ppermute | solution.py:213
  44.0 7.1 %all-to-all-done.1 = bf16[16,64,128]{2,1,0:T(8,128)(2,1)S(1)} async-done(((bf16[16,64,128]{2,1,0:T(8,128)(2,1)}), bf16[16,64,128]{2,1,0:T(8,128)(2,1)S(1)}, u32[]{:S(2)}, u32[]{:S(2)}) %all-to-all-start.1) | async-done | bytes 262176 | tf_op jit(solution)/shard_map/all_to_all | solution.py:214
  51.2 10.6 %pairs.1 = f32[32,1,1280]{2,1,0:T(1,128)S(1)} custom-call(bf16[1024,128]{1,0:T(8,128)(2,1)S(1)} %bitcast.4, bf16[1024,128]{1,0:T(8,128)(2,1)S(1)} %collective-permute-done.1.oth_ref, bf16[1024,128]{1,0:T(8,128)(2,1)S(1)} %bitcast.5, bf16[2048,1024]{1,0:T(8,128)(2,1)} %w_hbm.1), custom_call_target="tpu_custom_call" | custom-call | tf_op jit(solution)/shard_map/pairs/pallas_call | solution.py:218
  61.7 15.5 %all_to_all.20.part_ref = f32[32,1,1280]{2,1,0:T(1,128)S(1)} all-to-all(f32[32,1,1280]{2,1,0:T(1,128)S(1)} %pairs.1), channel_id=1, replica_groups=mesh['row'=16,'z'=8,'core'=2,'depth'=2] {'z','core','depth'}, dimensions={0} | all-to-all | bytes 327680 | tf_op jit(solution)/shard_map/all_to_all | solution.py:241
  77.3 0.0 copy-start
  77.3 0.6 broadcast_in_dim.2
  77.9 3.5 %all-to-all-start.3 = ((f32[16,1,128]{2,1,0:T(1,128)}), f32[16,1,128]{2,1,0:T(1,128)S(1)}, u32[]{:S(2)}, u32[]{:S(2)}) async-start(f32[16,1,128]{2,1,0:T(1,128)} %broadcast_in_dim.2), calls=%async_computation.3 | async-start | bytes 16384 | tf_op jit(solution)/shard_map/all_to_all | solution.py:243
  81.4 0.0 copy-done
  81.4 1.7 %finish.1 = f32[16,64]{1,0:T(8,128)} custom-call(f32[32,1,1280]{2,1,0:T(1,128)} %copy-done, f32[16,64]{1,0:T(8,128)} %crd_ref.3), custom_call_target="tpu_custom_call" | custom-call | flops 100000 | bytes 200000 | tf_op jit(solution)/shard_map/finish/pallas_call | solution.py:244
  83.1 7.1 %all-to-all-done.3.part_ref = f32[16,1,128]{2,1,0:T(1,128)S(1)} async-done(((f32[16,1,128]{2,1,0:T(1,128)}), f32[16,1,128]{2,1,0:T(1,128)S(1)}, u32[]{:S(2)}, u32[]{:S(2)}) %all-to-all-start.3) | async-done | bytes 8224 | tf_op jit(solution)/shard_map/all_to_all | solution.py:243
  90.2 0.0 copy-start.1
  90.2 0.6 copy-done.1
  90.8 1.3 %stress.1 = f32[1,1]{1,0:T(1,128)} custom-call(f32[16,1,128]{2,1,0:T(1,128)} %copy-done.1), custom_call_target="tpu_custom_call" | custom-call | tf_op jit(solution)/shard_map/stress/pallas_call | solution.py:250
  (1 shorter events, 0.0 us)
Async XLA Ops:
  2.2 15.4 %collective-permute-start = (bf16[64,128]{1,0:T(8,128)(2,1)}, bf16[64,128]{1,0:T(8,128)(2,1)S(1)}, u32[]{:S(2)}, u32[]{:S(2)}) collective-permute-start(bf16[64,128]{1,0:T(8,128)(2,1)} %get-tuple-element.6), channel_id=1, source_target_pairs={{0,0},{1,32},{2,64},{3,96},{4,128},{5,160},{6,192},{7,224},{8,256}... | collective-permute-start | bytes 49160 | tf_op jit(solution)/shard_map/ppermute | solution.py:204
  11.0 18.3 %all-to-all-start = ((bf16[16,64,128]{2,1,0:T(8,128)(2,1)}), bf16[16,64,128]{2,1,0:T(8,128)(2,1)S(1)}, u32[]{:S(2)}, u32[]{:S(2)}) async-start(bf16[16,64,128]{2,1,0:T(8,128)(2,1)} %get-tuple-element.7), calls=%async_computation | async-start | bytes 524288 | tf_op jit(solution)/shard_map/all_to_all | solution.py:205
  17.6 0.6 copy-start.2
  29.3 21.9 %all-to-all-start.1 = ((bf16[16,64,128]{2,1,0:T(8,128)(2,1)}), bf16[16,64,128]{2,1,0:T(8,128)(2,1)S(1)}, u32[]{:S(2)}, u32[]{:S(2)}) async-start(bf16[16,64,128]{2,1,0:T(8,128)(2,1)} %spread.1), calls=%async_computation.1 | async-start | bytes 524288 | tf_op jit(solution)/shard_map/all_to_all | solution.py:214
  38.4 5.6 %collective-permute-start.1 = (bf16[1024,128]{1,0:T(8,128)(2,1)S(1)}, bf16[1024,128]{1,0:T(8,128)(2,1)S(1)}, u32[]{:S(2)}, u32[]{:S(2)}) collective-permute-start(bf16[1024,128]{1,0:T(8,128)(2,1)S(1)} %bitcast.3), channel_id=1, source_target_pairs={{0,2},{2,0},{1,3},{3,1},{4,6},{6,4},{5,7},{7,5},{8,10},{10,8},{9,1... | collective-permute-start | bytes 786440 | tf_op jit(solution)/shard_map/ppermute | solution.py:213
  77.3 4.2 %copy-start = (f32[32,1,1280]{2,1,0:T(1,128)}, f32[32,1,1280]{2,1,0:T(1,128)S(1)}, u32[]{:S(2)}) copy-start(f32[32,1,1280]{2,1,0:T(1,128)S(1)} %all_to_all.20.part_ref) | copy-start | bytes 491524
  77.9 12.3 %all-to-all-start.3 = ((f32[16,1,128]{2,1,0:T(1,128)}), f32[16,1,128]{2,1,0:T(1,128)S(1)}, u32[]{:S(2)}, u32[]{:S(2)}) async-start(f32[16,1,128]{2,1,0:T(1,128)} %broadcast_in_dim.2), calls=%async_computation.3 | async-start | bytes 16384 | tf_op jit(solution)/shard_map/all_to_all | solution.py:243
  90.2 0.6 copy-start.1

commit v10 on v8

--- a/solution.py
+++ b/solution.py
@@ -39,23 +39,40 @@
 def pack_kernel(emb_ref, crd_ref, own_ref, out_ref):
     emb = emb_ref[...].astype(F32)
     crd = crd_ref[...]
-    points = emb.shape[1]
     hi = crd.astype(BF16).astype(F32)
-    low = (crd - hi).astype(BF16).astype(F32)
-    squares = split3(jnp.sum(emb * emb, axis=0, keepdims=True))
-    squares += split3(jnp.sum(crd * crd, axis=0, keepdims=True))
-    lane = lax.broadcasted_iota(jnp.int32, (16, points), 0)
-    tail = jnp.where((lane >= ONE - QF) & (lane < ONE - QF + 3), 1.0, 0.0)
-    for k, sq in enumerate(squares):
-        tail = jnp.where(lane == k, sq, tail)
-    rows = jnp.concatenate([emb, hi, low, hi, tail], axis=0)
-    mine = rows.T.astype(BF16)
+    feats = jnp.concatenate([emb, hi, crd - hi], axis=0)
+    half = feats.shape[0] // 2
+    mine = jnp.concatenate([feats[:half], feats[half:]], axis=1).astype(BF16)
     own_ref[...] = mine
     for k in range(out_ref.shape[0]):
         out_ref[k] = mine
 
 
-def pairs_kernel(own_ref, oth_ref, col_ref, w_hbm, out_ref, w_ref, f_scr, x_scr, flat_scr, c_scr, f_tiles, x_tiles, sems):
+def unpack(shards):
+    top, low = [], []
+    for sh in shards:
+        sh = sh.astype(F32)
+        top.append(sh[:, 0:64])
+        low.append(sh[:, 64:128])
+    feats = jnp.concatenate([jnp.concatenate(top, axis=1), jnp.concatenate(low, axis=1)], axis=0)
+    emb, hi, low = feats[0:64], feats[XH : XH + 16], feats[XL : XL + 16]
+    crd = hi + low
+    squares = split3(jnp.sum(emb * emb, axis=0, keepdims=True))
+    squares += split3(jnp.sum(crd * crd, axis=0, keepdims=True))
+    at = lax.broadcasted_iota(jnp.int32, (16, feats.shape[1]), 0)
+    tail = jnp.where((at >= ONE - QF) & (at < ONE - QF + 3), 1.0, 0.0)
+    for k, sq in enumerate(squares):
+        tail = jnp.where(at == k, sq, tail)
+    return jnp.concatenate([feats, hi, tail], axis=0)
+
+
+def spread_kernel(own_ref, out_ref):
+    own = own_ref[...]
+    for k in range(out_ref.shape[0]):
+        out_ref[k] = own
+
+
+def pairs_kernel(own_ref, oth_ref, col_ref, w_hbm, out_ref, w_ref, f_scr, x_scr, flat_scr, rows_scr, c_scr, f_tiles, x_tiles, sems):
     total_rows, total = w_ref.shape
     tm = c_scr.shape[0]
     tn = min(256, total)
@@ -68,33 +85,35 @@
 
     for i in range(steps):
         fetch(i).start()
-    all_cols = col_ref[...]
     last = (((1,), (1,)), ((), ()))
     form_f = bilinear_form(0)
-    f_scr[...] = lax.dot_general(form_f, all_cols, last, preferred_element_type=F32).astype(BF16)
-    x_scr[...] = lax.dot_general(bilinear_form(1), all_cols, last, preferred_element_type=F32).astype(BF16)
-    a = lax.broadcasted_iota(jnp.int32, (LANES, LANES), 0)
-    b = lax.broadcasted_iota(jnp.int32, (LANES, LANES), 1)
-    same = jnp.where(a == b, 1.0, 0.0).astype(BF16)
-    flat_scr[...] = lax.dot_general(same, all_cols, last, preferred_element_type=F32).astype(BF16)
-
-    def row_block(i):
-        pieces = []
+    form_x = bilinear_form(1)
+    for s in range(0, col_ref.shape[0], 4):
+        some = unpack([col_ref[k] for k in range(s, min(s + 4, col_ref.shape[0]))]).astype(BF16)
+        cut = slice(64 * s, 64 * s + some.shape[1])
+        flat_scr[:, cut] = some
+        f_scr[:, cut] = jnp.dot(form_f, some, preferred_element_type=F32).astype(BF16)
+        x_scr[:, cut] = jnp.dot(form_x, some, preferred_element_type=F32).astype(BF16)
+
+    def squares(i, slot):
+        shards = []
         for k in range(tm // 256):
-            cut = pl.ds(pl.multiple_of(i * (tm // 2) + k * 128, 128), 128)
-            own, oth = own_ref[cut, :], oth_ref[cut, :]
-            pieces += [jnp.where(first, own, oth), jnp.where(first, oth, own)]
-        return jnp.concatenate(pieces, axis=0)
-
-    def squares(rows, slot):
+            at = i * (tm // 128) + 2 * k
+            own = [own_ref[at], own_ref[at + 1]]
+            oth = [oth_ref[at], oth_ref[at + 1]]
+            shards += [jnp.where(first, a, b) for a, b in zip(own, oth)]
+            shards += [jnp.where(first, b, a) for a, b in zip(own, oth)]
+        feats = unpack(shards)
+        rows_scr[slot] = feats.astype(BF16)
+        rows = feats.T.astype(BF16)
         f_tiles[slot] = jnp.dot(rows, f_scr[...], preferred_element_type=F32)
         x_tiles[slot] = jnp.dot(rows, x_scr[...], preferred_element_type=F32)
 
     def block(i, slot, mis, scl, more=True):
         fetch(i).wait()
         if more:
-            squares(row_block(i + 1), 1 - slot)
-        bent = lax.dot_general(form_f, row_block(i), last, preferred_element_type=F32)
+            squares(i + 1, 1 - slot)
+        bent = jnp.dot(form_f, rows_scr[slot], preferred_element_type=F32)
         base = i * tm
         acc = jnp.zeros((48, tm), F32)
         wacc = jnp.zeros((LANES, tm), F32)
@@ -132,7 +151,7 @@
         carry = block(2 * k, 0, *carry)
         return block(2 * k + 1, 1, *carry)
 
-    squares(row_block(0), 0)
+    squares(0, 0)
     pairs = (steps - 1) // 2
     sums = lax.fori_loop(0, pairs, two, (jnp.zeros((8, tn), F32), jnp.zeros((8, tm), F32)))
     for i in range(2 * pairs, steps):
@@ -176,21 +195,27 @@
     n_row, n_z, n_core, n_depth = (lax.axis_size(a) for a in ("row", "z", "core", "depth"))
     likes = n_z * n_depth
 
+    shard = (48, 128)
     packed = pl.pallas_call(
         pack_kernel,
         out_shape=(
-            jax.ShapeDtypeStruct((points, LANES), BF16),
-            jax.ShapeDtypeStruct((likes, points, LANES), BF16),
+            jax.ShapeDtypeStruct(shard, BF16),
+            jax.ShapeDtypeStruct((likes,) + shard, BF16),
         ),
         name="pack",
     )(embeddings, coords)
     moves = column_moves(n_row, n_z * n_core, n_depth)
     moved = lax.ppermute(packed[0], ("row", "z", "core", "depth"), moves)
-    own = lax.all_to_all(packed[1], ("z", "depth"), 0, 0, tiled=True).reshape(rows // n_core, LANES)
-    moved = jnp.broadcast_to(moved[None], (n_row, points, LANES))
+    own = lax.all_to_all(packed[1], ("z", "depth"), 0, 0, tiled=True)
+    moved = pl.pallas_call(
+        spread_kernel,
+        out_shape=jax.ShapeDtypeStruct((n_row,) + shard, BF16),
+        cost_estimate=pl.CostEstimate(flops=10**10, bytes_accessed=10**8, transcendentals=0),
+        name="spread",
+    )(moved)
     moved, own = lax.optimization_barrier((moved, own))
     oth = lax.ppermute(own, "core", [(0, 1), (1, 0)])
-    t_cols = lax.all_to_all(moved, "row", 0, 0, tiled=True).reshape(cols, LANES)
+    t_cols = lax.all_to_all(moved, "row", 0, 0, tiled=True)
 
     vmem = pl.BlockSpec(memory_space=pltpu.VMEM)
     tm = 256
@@ -209,6 +234,7 @@
             pltpu.VMEM((LANES, cols), BF16),
             pltpu.VMEM((LANES, cols), BF16),
             pltpu.VMEM((LANES, cols), BF16),
+            pltpu.VMEM((2, LANES, tm), BF16),
             pltpu.VMEM((tm, cols), BF16),
             pltpu.VMEM((2, tm, cols), F32),
             pltpu.VMEM((2, tm, cols), F32),

time: 91.4 us -> 89.3 us (0.977)
  waiting for transfers between devices: 13.8 us -> 21.4 us
  starting transfers between devices: 39.3 us -> 32.2 us
  blocking collectives: 21.5 us -> 16.6 us
  Pallas kernels: 13.2 us -> 15.5 us
    all_to_all x2, waiting for transfers between devices: 4.58 us -> 13.3 us  [the longest x1 8.58 us: shards(): own = lax.all_to_all(packed[1], ('z', 'depth'), 0, 0, tiled=True)]
    all_to_all x2, starting transfers between devices: 23.1 us -> 15.2 us  [the longest x1 8.63 us: shards(): t_cols = lax.all_to_all(moved, 'row', 0, 0, tiled=True)]
    all_to_all x1, blocking collectives: 21.5 us -> 16.6 us  [shards(): parts = lax.all_to_all(parts, ('z', 'core', 'depth'), 0, 0, tiled=True)]
    ppermute x1, starting transfers between devices: 7.39 us -> 8.83 us  [shards(): moved = lax.ppermute(packed[0], ('row', 'z', 'core', 'depth'), moves)]
    pallas_call x1 -> x2, Pallas kernels: 1.52 us -> 2.87 us  [the longest x1 1.48 us: shards(): pl.pallas_call(pack_kernel, out_shape=(jax.ShapeDtypeStruct(shard, BF16),...]
    ppermute x1, waiting for transfers between devices: 1.06 us -> 0.01 us  [shards(): moved = lax.ppermute(packed[0], ('row', 'z', 'core', 'depth'), moves)]
    pallas_call x1, Pallas kernels: 8.69 us -> 9.68 us  [shards(): pl.pallas_call(pairs_kernel, in_specs=[vmem, vmem, vmem, pl.BlockSpec(mem...]
  transfers between devices with their start and end apart: 5 -> 5, of which waited for: 5 -> 4; matrix products, arithmetic and copies ran while one was open for 0% -> 0% of each run, Pallas kernels for 2% -> 3%
where the time goes in v10:
time: 89.3 us; the launch traced here: 88.4 us
  starting transfers between devices  32.2 us (36%)
  waiting for transfers between devices  21.4 us (24%)
  blocking collectives  16.6 us (19%)
  Pallas kernels  15.5 us (17%)
  local copies, waits for them, and re-layouts  1.79 us (2%)
    all_to_all x1, blocking collectives, shards(): parts = lax.all_to_all(parts, ('z', 'core', 'depth'), 0, 0, tiled=True)  16.6 us
    pallas_call x1, Pallas kernels, shards(): pl.pallas_call(pairs_kernel, in_specs=[vmem, vmem, vmem, pl.BlockSpec(mem...  9.68 us
    ppermute x1, starting transfers between devices, shards(): moved = lax.ppermute(packed[0], ('row', 'z', 'core', 'depth'), moves)  8.83 us
    all_to_all x1, starting transfers between devices, shards(): t_cols = lax.all_to_all(moved, 'row', 0, 0, tiled=True)  8.63 us
    all_to_all x1, waiting for transfers between devices, shards(): own = lax.all_to_all(packed[1], ('z', 'depth'), 0, 0, tiled=True)  8.58 us
    all_to_all x1, waiting for transfers between devices, shards(): lax.all_to_all(jnp.broadcast_to(shares, (n_row, 1, 128)), 'row', 0, 0, ti...  7.06 us
    all_to_all x1, starting transfers between devices, shards(): own = lax.all_to_all(packed[1], ('z', 'depth'), 0, 0, tiled=True)  6.57 us
    ppermute x1, starting transfers between devices, shards(): oth = lax.ppermute(own, 'core', [(0, 1), (1, 0)])  4.73 us
  transfers between devices with their start and end apart: 5, of which 4 were waited for; matrix products, arithmetic and copies ran while one was open for 0% of the time, Pallas kernels for 3%

profile of v10, /device:TPU:1, one launch (start us, length us, event | category | flops | bytes accessed | tf_op | source)
XLA Modules:
  0.0 88.4 jit_solution(17718303248499133542)
XLA Ops:
  0.6 1.5 %pack.1 = (bf16[48,128]{1,0:T(8,128)(2,1)}, bf16[16,48,128]{2,1,0:T(8,128)(2,1)}) custom-call(bf16[64,64]{1,0:T(8,128)(2,1)} %emb_ref.1, f32[16,64]{1,0:T(8,128)} %crd_ref.3), custom_call_target="tpu_custom_call" | custom-call | tf_op jit(solution)/shard_map/pack/pallas_call | solution.py:199
  2.1 8.8 %collective-permute-start = (bf16[48,128]{1,0:T(8,128)(2,1)}, bf16[48,128]{1,0:T(8,128)(2,1)S(1)}, u32[]{:S(2)}, u32[]{:S(2)}) collective-permute-start(bf16[48,128]{1,0:T(8,128)(2,1)} %get-tuple-element.6), channel_id=1, source_target_pairs={{0,0},{1,32},{2,64},{3,96},{4,128},{5,160},{6,192},{7,224},{8,256}... | collective-permute-start | bytes 36872 | tf_op jit(solution)/shard_map/ppermute | solution.py:208
  10.9 6.6 %all-to-all-start = ((bf16[16,48,128]{2,1,0:T(8,128)(2,1)}), bf16[16,48,128]{2,1,0:T(8,128)(2,1)S(1)}, u32[]{:S(2)}, u32[]{:S(2)}) async-start(bf16[16,48,128]{2,1,0:T(8,128)(2,1)} %get-tuple-element.7), calls=%async_computation | async-start | bytes 393216 | tf_op jit(solution)/shard_map/all_to_all | solution.py:209
  17.5 0.0 collective-permute-done.own_ref
  17.5 0.0 copy-start.2
  17.5 0.6 copy-done.2
  18.1 1.4 %spread.1 = bf16[16,48,128]{2,1,0:T(8,128)(2,1)} custom-call(bf16[48,128]{1,0:T(8,128)(2,1)} %copy-done.2), custom_call_target="tpu_custom_call" | custom-call | flops 10000000000 | bytes 100000000 | tf_op jit(solution)/shard_map/spread/pallas_call | solution.py:210
  19.5 8.6 %all-to-all-done.own_ref = bf16[16,48,128]{2,1,0:T(8,128)(2,1)S(1)} async-done(((bf16[16,48,128]{2,1,0:T(8,128)(2,1)}), bf16[16,48,128]{2,1,0:T(8,128)(2,1)S(1)}, u32[]{:S(2)}, u32[]{:S(2)}) %all-to-all-start) | async-done | bytes 196640 | tf_op jit(solution)/shard_map/all_to_all | solution.py:209
  28.1 8.6 %all-to-all-start.1 = ((bf16[16,48,128]{2,1,0:T(8,128)(2,1)}), bf16[16,48,128]{2,1,0:T(8,128)(2,1)S(1)}, u32[]{:S(2)}, u32[]{:S(2)}) async-start(bf16[16,48,128]{2,1,0:T(8,128)(2,1)} %spread.1), calls=%async_computation.1 | async-start | bytes 393216 | tf_op jit(solution)/shard_map/all_to_all | solution.py:218
  36.7 4.7 %collective-permute-start.1 = (bf16[16,48,128]{2,1,0:T(8,128)(2,1)S(1)}, bf16[16,48,128]{2,1,0:T(8,128)(2,1)S(1)}, u32[]{:S(2)}, u32[]{:S(2)}) collective-permute-start(bf16[16,48,128]{2,1,0:T(8,128)(2,1)S(1)} %all-to-all-done.own_ref), channel_id=1, source_target_pairs={{0,2},{2,0},{1,3},{3,1},{4,6},{6,4},{5,7},{7,5},{8,10},{10,8},{9,1... | collective-permute-start | bytes 589832 | tf_op jit(solution)/shard_map/ppermute | solution.py:217
  41.5 1.0 %collective-permute-done.1.oth_ref = bf16[16,48,128]{2,1,0:T(8,128)(2,1)S(1)} collective-permute-done((bf16[16,48,128]{2,1,0:T(8,128)(2,1)S(1)}, bf16[16,48,128]{2,1,0:T(8,128)(2,1)S(1)}, u32[]{:S(2)}, u32[]{:S(2)}) %collective-permute-start.1) | collective-permute-done | bytes 196640 | tf_op jit(solution)/shard_map/ppermute | solution.py:217
  42.5 4.7 %all-to-all-done.1.col_ref = bf16[16,48,128]{2,1,0:T(8,128)(2,1)S(1)} async-done(((bf16[16,48,128]{2,1,0:T(8,128)(2,1)}), bf16[16,48,128]{2,1,0:T(8,128)(2,1)S(1)}, u32[]{:S(2)}, u32[]{:S(2)}) %all-to-all-start.1) | async-done | bytes 196640 | tf_op jit(solution)/shard_map/all_to_all | solution.py:218
  47.3 9.7 %pairs.1 = f32[32,1,1280]{2,1,0:T(1,128)S(1)} custom-call(bf16[16,48,128]{2,1,0:T(8,128)(2,1)S(1)} %all-to-all-done.own_ref, bf16[16,48,128]{2,1,0:T(8,128)(2,1)S(1)} %collective-permute-done.1.oth_ref, bf16[16,48,128]{2,1,0:T(8,128)(2,1)S(1)} %all-to-all-done.1.col_ref, bf16[2048,1024]{1,0:T(8,128)(2,1)} %w_hbm.1), custom_call_target="tpu_custom_call" | custom-call | tf_op jit(solution)/shard_map/pairs/pallas_call | solution.py:222
  56.9 16.6 %all_to_all.20.part_ref = f32[32,1,1280]{2,1,0:T(1,128)S(1)} all-to-all(f32[32,1,1280]{2,1,0:T(1,128)S(1)} %pairs.1), channel_id=1, replica_groups=mesh['row'=16,'z'=8,'core'=2,'depth'=2] {'z','core','depth'}, dimensions={0} | all-to-all | bytes 327680 | tf_op jit(solution)/shard_map/all_to_all | solution.py:246
  73.6 0.0 copy-start
  73.6 0.6 broadcast_in_dim.2
  74.2 3.5 %all-to-all-start.3 = ((f32[16,1,128]{2,1,0:T(1,128)}), f32[16,1,128]{2,1,0:T(1,128)S(1)}, u32[]{:S(2)}, u32[]{:S(2)}) async-start(f32[16,1,128]{2,1,0:T(1,128)} %broadcast_in_dim.2), calls=%async_computation.3 | async-start | bytes 16384 | tf_op jit(solution)/shard_map/all_to_all | solution.py:248
  77.7 0.0 copy-done
  77.7 1.7 %finish.1 = f32[16,64]{1,0:T(8,128)} custom-call(f32[32,1,1280]{2,1,0:T(1,128)} %copy-done, f32[16,64]{1,0:T(8,128)} %crd_ref.3), custom_call_target="tpu_custom_call" | custom-call | flops 100000 | bytes 200000 | tf_op jit(solution)/shard_map/finish/pallas_call | solution.py:249
  79.4 7.1 %all-to-all-done.3.part_ref = f32[16,1,128]{2,1,0:T(1,128)S(1)} async-done(((f32[16,1,128]{2,1,0:T(1,128)}), f32[16,1,128]{2,1,0:T(1,128)S(1)}, u32[]{:S(2)}, u32[]{:S(2)}) %all-to-all-start.3) | async-done | bytes 8224 | tf_op jit(solution)/shard_map/all_to_all | solution.py:248
  86.5 0.0 copy-start.1
  86.5 0.6 copy-done.1
  87.1 1.3 %stress.1 = f32[1,1]{1,0:T(1,128)} custom-call(f32[16,1,128]{2,1,0:T(1,128)} %copy-done.1), custom_call_target="tpu_custom_call" | custom-call | tf_op jit(solution)/shard_map/stress/pallas_call | solution.py:255
  (1 shorter events, 0.0 us)
Async XLA Ops:
  2.1 15.4 %collective-permute-start = (bf16[48,128]{1,0:T(8,128)(2,1)}, bf16[48,128]{1,0:T(8,128)(2,1)S(1)}, u32[]{:S(2)}, u32[]{:S(2)}) collective-permute-start(bf16[48,128]{1,0:T(8,128)(2,1)} %get-tuple-element.6), channel_id=1, source_target_pairs={{0,0},{1,32},{2,64},{3,96},{4,128},{5,160},{6,192},{7,224},{8,256}... | collective-permute-start | bytes 36872 | tf_op jit(solution)/shard_map/ppermute | solution.py:208
  10.9 17.2 %all-to-all-start = ((bf16[16,48,128]{2,1,0:T(8,128)(2,1)}), bf16[16,48,128]{2,1,0:T(8,128)(2,1)S(1)}, u32[]{:S(2)}, u32[]{:S(2)}) async-start(bf16[16,48,128]{2,1,0:T(8,128)(2,1)} %get-tuple-element.7), calls=%async_computation | async-start | bytes 393216 | tf_op jit(solution)/shard_map/all_to_all | solution.py:209
  17.5 0.6 copy-start.2
  28.1 19.2 %all-to-all-start.1 = ((bf16[16,48,128]{2,1,0:T(8,128)(2,1)}), bf16[16,48,128]{2,1,0:T(8,128)(2,1)S(1)}, u32[]{:S(2)}, u32[]{:S(2)}) async-start(bf16[16,48,128]{2,1,0:T(8,128)(2,1)} %spread.1), calls=%async_computation.1 | async-start | bytes 393216 | tf_op jit(solution)/shard_map/all_to_all | solution.py:218
  36.7 5.8 %collective-permute-start.1 = (bf16[16,48,128]{2,1,0:T(8,128)(2,1)S(1)}, bf16[16,48,128]{2,1,0:T(8,128)(2,1)S(1)}, u32[]{:S(2)}, u32[]{:S(2)}) collective-permute-start(bf16[16,48,128]{2,1,0:T(8,128)(2,1)S(1)} %all-to-all-done.own_ref), channel_id=1, source_target_pairs={{0,2},{2,0},{1,3},{3,1},{4,6},{6,4},{5,7},{7,5},{8,10},{10,8},{9,1... | collective-permute-start | bytes 589832 | tf_op jit(solution)/shard_map/ppermute | solution.py:217
  73.6 4.2 %copy-start = (f32[32,1,1280]{2,1,0:T(1,128)}, f32[32,1,1280]{2,1,0:T(1,128)S(1)}, u32[]{:S(2)}) copy-start(f32[32,1,1280]{2,1,0:T(1,128)S(1)} %all_to_all.20.part_ref) | copy-start | bytes 491524
  74.2 12.3 %all-to-all-start.3 = ((f32[16,1,128]{2,1,0:T(1,128)}), f32[16,1,128]{2,1,0:T(1,128)S(1)}, u32[]{:S(2)}, u32[]{:S(2)}) async-start(f32[16,1,128]{2,1,0:T(1,128)} %broadcast_in_dim.2), calls=%async_computation.3 | async-start | bytes 16384 | tf_op jit(solution)/shard_map/all_to_all | solution.py:248
  86.5 0.6 copy-start.1

commit v11 on v10

--- a/solution.py
+++ b/solution.py
@@ -95,7 +95,7 @@
         f_scr[:, cut] = jnp.dot(form_f, some, preferred_element_type=F32).astype(BF16)
         x_scr[:, cut] = jnp.dot(form_x, some, preferred_element_type=F32).astype(BF16)
 
-    def squares(i, slot):
+    def row_block(i, slot):
         shards = []
         for k in range(tm // 256):
             at = i * (tm // 128) + 2 * k
@@ -105,34 +105,48 @@
             shards += [jnp.where(first, b, a) for a, b in zip(own, oth)]
         feats = unpack(shards)
         rows_scr[slot] = feats.astype(BF16)
-        rows = feats.T.astype(BF16)
-        f_tiles[slot] = jnp.dot(rows, f_scr[...], preferred_element_type=F32)
-        x_tiles[slot] = jnp.dot(rows, x_scr[...], preferred_element_type=F32)
+        return feats.T.astype(BF16)
+
+    def squares(rows, slot, cut):
+        f_tiles[slot, :, cut] = jnp.dot(rows, f_scr[:, cut], preferred_element_type=F32)
+        x_tiles[slot, :, cut] = jnp.dot(rows, x_scr[:, cut], preferred_element_type=F32)
+
+    def chain(base, slot, cut, mis):
+        for r in range(0, tm, 32):
+            f2 = jnp.maximum(f_tiles[slot, r : r + 32, cut], TINY)
+            x2 = jnp.maximum(x_tiles[slot, r : r + 32, cut], TINY)
+            w = w_ref[pl.ds(pl.multiple_of(base + r, 32), 32), cut].astype(F32)
+            dissim = f2 * lax.rsqrt(f2)
+            inv = lax.rsqrt(x2)
+            diff = dissim - x2 * inv
+            c_scr[r : r + 32, cut] = (w * (dissim * jnp.minimum(inv, 1.0))).astype(BF16)
+            miss = w * (diff * diff)
+            mis += (miss[0:8] + miss[8:16]) + (miss[16:24] + miss[24:32])
+        return mis
+
+    tiles = [slice(start, start + tn) for start in range(0, total, tn)]
 
     def block(i, slot, mis, scl, more=True):
         fetch(i).wait()
         if more:
-            squares(i + 1, 1 - slot)
+            rows = row_block(i + 1, 1 - slot)
         bent = jnp.dot(form_f, rows_scr[slot], preferred_element_type=F32)
         base = i * tm
         acc = jnp.zeros((48, tm), F32)
         wacc = jnp.zeros((LANES, tm), F32)
-        for start in range(0, total, tn):
-            cut = slice(start, start + tn)
-            for r in range(0, tm, 32):
-                f2 = jnp.maximum(f_tiles[slot, r : r + 32, cut], TINY)
-                x2 = jnp.maximum(x_tiles[slot, r : r + 32, cut], TINY)
-                w = w_ref[pl.ds(pl.multiple_of(base + r, 32), 32), cut].astype(F32)
-                dissim = f2 * lax.rsqrt(f2)
-                inv = lax.rsqrt(x2)
-                diff = dissim - x2 * inv
-                c_scr[r : r + 32, cut] = (w * (dissim * jnp.minimum(inv, 1.0))).astype(BF16)
-                miss = w * (diff * diff)
-                mis += (miss[0:8] + miss[8:16]) + (miss[16:24] + miss[24:32])
-            wb = w_ref[pl.ds(pl.multiple_of(base, tm), tm), cut]
-            picked = jnp.concatenate([flat_scr[XH : XH + 32, cut], flat_scr[QF:, cut]], axis=0)
-            acc += lax.dot_general(picked, c_scr[:, cut], last, preferred_element_type=F32)
-            wacc += lax.dot_general(flat_scr[:, cut], wb, last, preferred_element_type=F32)
+        for n in range(len(tiles) + 1):
+            if n < len(tiles):
+                cut = tiles[n]
+                if more:
+                    squares(rows, 1 - slot, cut)
+                wb = w_ref[pl.ds(pl.multiple_of(base, tm), tm), cut]
+                wacc += lax.dot_general(flat_scr[:, cut], wb, last, preferred_element_type=F32)
+            if n > 0:
+                old = tiles[n - 1]
+                picked = jnp.concatenate([flat_scr[XH : XH + 32, old], flat_scr[QF:, old]], axis=0)
+                acc += lax.dot_general(picked, c_scr[:, old], last, preferred_element_type=F32)
+            if n < len(tiles):
+                mis = chain(base, slot, cut, mis)
         scl += jnp.sum((bent * wacc).reshape(LANES // 8, 8, tm), axis=0)
         less = acc[0:32] - wacc[XH : XH + 32]
         pull = less[0:16] + less[16:32]
@@ -151,7 +165,7 @@
         carry = block(2 * k, 0, *carry)
         return block(2 * k + 1, 1, *carry)
 
-    squares(0, 0)
+    squares(row_block(0, 0), 0, slice(0, total))
     pairs = (steps - 1) // 2
     sums = lax.fori_loop(0, pairs, two, (jnp.zeros((8, tn), F32), jnp.zeros((8, tm), F32)))
     for i in range(2 * pairs, steps):

time: 89.3 us -> 89 us (level)
  transfers between devices with their start and end apart: 5 -> 5, of which waited for: 4 -> 4; matrix products, arithmetic and copies ran while one was open for 0% -> 0% of each run, Pallas kernels for 3% -> 4%
where the time goes in v11:
time: 89 us; the launch traced here: 88.1 us
  starting transfers between devices  32.2 us (36%)
  waiting for transfers between devices  21.4 us (24%)
  blocking collectives  16.6 us (19%)
  Pallas kernels  15.2 us (17%)
  local copies, waits for them, and re-layouts  1.79 us (2%)
    all_to_all x1, blocking collectives, shards(): parts = lax.all_to_all(parts, ('z', 'core', 'depth'), 0, 0, tiled=True)  16.6 us
    pallas_call x1, Pallas kernels, shards(): pl.pallas_call(pairs_kernel, in_specs=[vmem, vmem, vmem, pl.BlockSpec(mem...  9.38 us
    ppermute x1, starting transfers between devices, shards(): moved = lax.ppermute(packed[0], ('row', 'z', 'core', 'depth'), moves)  8.83 us
    all_to_all x1, starting transfers between devices, shards(): t_cols = lax.all_to_all(moved, 'row', 0, 0, tiled=True)  8.63 us
    all_to_all x1, waiting for transfers between devices, shards(): own = lax.all_to_all(packed[1], ('z', 'depth'), 0, 0, tiled=True)  8.58 us
    all_to_all x1, waiting for transfers between devices, shards(): lax.all_to_all(jnp.broadcast_to(shares, (n_row, 1, 128)), 'row', 0, 0, ti...  7.06 us
    all_to_all x1, starting transfers between devices, shards(): own = lax.all_to_all(packed[1], ('z', 'depth'), 0, 0, tiled=True)  6.57 us
    ppermute x1, starting transfers between devices, shards(): oth = lax.ppermute(own, 'core', [(0, 1), (1, 0)])  4.73 us
  transfers between devices with their start and end apart: 5, of which 4 were waited for; matrix products, arithmetic and copies ran while one was open for 0% of the time, Pallas kernels for 4%

profile of v11, /device:TPU:1, one launch (start us, length us, event | category | flops | bytes accessed | tf_op | source)
XLA Modules:
  0.0 88.1 jit_solution(5270232640553396643)
XLA Ops:
  0.6 1.5 %pack.1 = (bf16[48,128]{1,0:T(8,128)(2,1)}, bf16[16,48,128]{2,1,0:T(8,128)(2,1)}) custom-call(bf16[64,64]{1,0:T(8,128)(2,1)} %emb_ref.1, f32[16,64]{1,0:T(8,128)} %crd_ref.3), custom_call_target="tpu_custom_call" | custom-call | tf_op jit(solution)/shard_map/pack/pallas_call | solution.py:213
  2.1 8.8 %collective-permute-start = (bf16[48,128]{1,0:T(8,128)(2,1)}, bf16[48,128]{1,0:T(8,128)(2,1)S(1)}, u32[]{:S(2)}, u32[]{:S(2)}) collective-permute-start(bf16[48,128]{1,0:T(8,128)(2,1)} %get-tuple-element.6), channel_id=1, source_target_pairs={{0,0},{1,32},{2,64},{3,96},{4,128},{5,160},{6,192},{7,224},{8,256}... | collective-permute-start | bytes 36872 | tf_op jit(solution)/shard_map/ppermute | solution.py:222
  10.9 6.6 %all-to-all-start = ((bf16[16,48,128]{2,1,0:T(8,128)(2,1)}), bf16[16,48,128]{2,1,0:T(8,128)(2,1)S(1)}, u32[]{:S(2)}, u32[]{:S(2)}) async-start(bf16[16,48,128]{2,1,0:T(8,128)(2,1)} %get-tuple-element.7), calls=%async_computation | async-start | bytes 393216 | tf_op jit(solution)/shard_map/all_to_all | solution.py:223
  17.5 0.0 collective-permute-done.own_ref
  17.5 0.0 copy-start.2
  17.5 0.6 copy-done.2
  18.1 1.4 %spread.1 = bf16[16,48,128]{2,1,0:T(8,128)(2,1)} custom-call(bf16[48,128]{1,0:T(8,128)(2,1)} %copy-done.2), custom_call_target="tpu_custom_call" | custom-call | flops 10000000000 | bytes 100000000 | tf_op jit(solution)/shard_map/spread/pallas_call | solution.py:224
  19.5 8.6 %all-to-all-done.own_ref = bf16[16,48,128]{2,1,0:T(8,128)(2,1)S(1)} async-done(((bf16[16,48,128]{2,1,0:T(8,128)(2,1)}), bf16[16,48,128]{2,1,0:T(8,128)(2,1)S(1)}, u32[]{:S(2)}, u32[]{:S(2)}) %all-to-all-start) | async-done | bytes 196640 | tf_op jit(solution)/shard_map/all_to_all | solution.py:223
  28.1 8.6 %all-to-all-start.1 = ((bf16[16,48,128]{2,1,0:T(8,128)(2,1)}), bf16[16,48,128]{2,1,0:T(8,128)(2,1)S(1)}, u32[]{:S(2)}, u32[]{:S(2)}) async-start(bf16[16,48,128]{2,1,0:T(8,128)(2,1)} %spread.1), calls=%async_computation.1 | async-start | bytes 393216 | tf_op jit(solution)/shard_map/all_to_all | solution.py:232
  36.7 4.7 %collective-permute-start.1 = (bf16[16,48,128]{2,1,0:T(8,128)(2,1)S(1)}, bf16[16,48,128]{2,1,0:T(8,128)(2,1)S(1)}, u32[]{:S(2)}, u32[]{:S(2)}) collective-permute-start(bf16[16,48,128]{2,1,0:T(8,128)(2,1)S(1)} %all-to-all-done.own_ref), channel_id=1, source_target_pairs={{0,2},{2,0},{1,3},{3,1},{4,6},{6,4},{5,7},{7,5},{8,10},{10,8},{9,1... | collective-permute-start | bytes 589832 | tf_op jit(solution)/shard_map/ppermute | solution.py:231
  41.5 1.0 %collective-permute-done.1.oth_ref = bf16[16,48,128]{2,1,0:T(8,128)(2,1)S(1)} collective-permute-done((bf16[16,48,128]{2,1,0:T(8,128)(2,1)S(1)}, bf16[16,48,128]{2,1,0:T(8,128)(2,1)S(1)}, u32[]{:S(2)}, u32[]{:S(2)}) %collective-permute-start.1) | collective-permute-done | bytes 196640 | tf_op jit(solution)/shard_map/ppermute | solution.py:231
  42.5 4.7 %all-to-all-done.1.col_ref = bf16[16,48,128]{2,1,0:T(8,128)(2,1)S(1)} async-done(((bf16[16,48,128]{2,1,0:T(8,128)(2,1)}), bf16[16,48,128]{2,1,0:T(8,128)(2,1)S(1)}, u32[]{:S(2)}, u32[]{:S(2)}) %all-to-all-start.1) | async-done | bytes 196640 | tf_op jit(solution)/shard_map/all_to_all | solution.py:232
  47.3 9.4 %pairs.1 = f32[32,1,1280]{2,1,0:T(1,128)S(1)} custom-call(bf16[16,48,128]{2,1,0:T(8,128)(2,1)S(1)} %all-to-all-done.own_ref, bf16[16,48,128]{2,1,0:T(8,128)(2,1)S(1)} %collective-permute-done.1.oth_ref, bf16[16,48,128]{2,1,0:T(8,128)(2,1)S(1)} %all-to-all-done.1.col_ref, bf16[2048,1024]{1,0:T(8,128)(2,1)} %w_hbm.1), custom_call_target="tpu_custom_call" | custom-call | tf_op jit(solution)/shard_map/pairs/pallas_call | solution.py:236
  56.6 16.6 %all_to_all.20.part_ref = f32[32,1,1280]{2,1,0:T(1,128)S(1)} all-to-all(f32[32,1,1280]{2,1,0:T(1,128)S(1)} %pairs.1), channel_id=1, replica_groups=mesh['row'=16,'z'=8,'core'=2,'depth'=2] {'z','core','depth'}, dimensions={0} | all-to-all | bytes 327680 | tf_op jit(solution)/shard_map/all_to_all | solution.py:260
  73.3 0.0 copy-start
  73.3 0.6 broadcast_in_dim.2
  73.9 3.5 %all-to-all-start.3 = ((f32[16,1,128]{2,1,0:T(1,128)}), f32[16,1,128]{2,1,0:T(1,128)S(1)}, u32[]{:S(2)}, u32[]{:S(2)}) async-start(f32[16,1,128]{2,1,0:T(1,128)} %broadcast_in_dim.2), calls=%async_computation.3 | async-start | bytes 16384 | tf_op jit(solution)/shard_map/all_to_all | solution.py:262
  77.4 0.0 copy-done
  77.4 1.7 %finish.1 = f32[16,64]{1,0:T(8,128)} custom-call(f32[32,1,1280]{2,1,0:T(1,128)} %copy-done, f32[16,64]{1,0:T(8,128)} %crd_ref.3), custom_call_target="tpu_custom_call" | custom-call | flops 100000 | bytes 200000 | tf_op jit(solution)/shard_map/finish/pallas_call | solution.py:263
  79.1 7.1 %all-to-all-done.3.part_ref = f32[16,1,128]{2,1,0:T(1,128)S(1)} async-done(((f32[16,1,128]{2,1,0:T(1,128)}), f32[16,1,128]{2,1,0:T(1,128)S(1)}, u32[]{:S(2)}, u32[]{:S(2)}) %all-to-all-start.3) | async-done | bytes 8224 | tf_op jit(solution)/shard_map/all_to_all | solution.py:262
  86.2 0.0 copy-start.1
  86.2 0.6 copy-done.1
  86.8 1.3 %stress.1 = f32[1,1]{1,0:T(1,128)} custom-call(f32[16,1,128]{2,1,0:T(1,128)} %copy-done.1), custom_call_target="tpu_custom_call" | custom-call | tf_op jit(solution)/shard_map/stress/pallas_call | solution.py:269
  (1 shorter events, 0.0 us)
Async XLA Ops:
  2.1 15.4 %collective-permute-start = (bf16[48,128]{1,0:T(8,128)(2,1)}, bf16[48,128]{1,0:T(8,128)(2,1)S(1)}, u32[]{:S(2)}, u32[]{:S(2)}) collective-permute-start(bf16[48,128]{1,0:T(8,128)(2,1)} %get-tuple-element.6), channel_id=1, source_target_pairs={{0,0},{1,32},{2,64},{3,96},{4,128},{5,160},{6,192},{7,224},{8,256}... | collective-permute-start | bytes 36872 | tf_op jit(solution)/shard_map/ppermute | solution.py:222
  10.9 17.2 %all-to-all-start = ((bf16[16,48,128]{2,1,0:T(8,128)(2,1)}), bf16[16,48,128]{2,1,0:T(8,128)(2,1)S(1)}, u32[]{:S(2)}, u32[]{:S(2)}) async-start(bf16[16,48,128]{2,1,0:T(8,128)(2,1)} %get-tuple-element.7), calls=%async_computation | async-start | bytes 393216 | tf_op jit(solution)/shard_map/all_to_all | solution.py:223
  17.5 0.6 copy-start.2
  28.1 19.2 %all-to-all-start.1 = ((bf16[16,48,128]{2,1,0:T(8,128)(2,1)}), bf16[16,48,128]{2,1,0:T(8,128)(2,1)S(1)}, u32[]{:S(2)}, u32[]{:S(2)}) async-start(bf16[16,48,128]{2,1,0:T(8,128)(2,1)} %spread.1), calls=%async_computation.1 | async-start | bytes 393216 | tf_op jit(solution)/shard_map/all_to_all | solution.py:232
  36.7 5.8 %collective-permute-start.1 = (bf16[16,48,128]{2,1,0:T(8,128)(2,1)S(1)}, bf16[16,48,128]{2,1,0:T(8,128)(2,1)S(1)}, u32[]{:S(2)}, u32[]{:S(2)}) collective-permute-start(bf16[16,48,128]{2,1,0:T(8,128)(2,1)S(1)} %all-to-all-done.own_ref), channel_id=1, source_target_pairs={{0,2},{2,0},{1,3},{3,1},{4,6},{6,4},{5,7},{7,5},{8,10},{10,8},{9,1... | collective-permute-start | bytes 589832 | tf_op jit(solution)/shard_map/ppermute | solution.py:231
  73.3 4.2 %copy-start = (f32[32,1,1280]{2,1,0:T(1,128)}, f32[32,1,1280]{2,1,0:T(1,128)S(1)}, u32[]{:S(2)}) copy-start(f32[32,1,1280]{2,1,0:T(1,128)S(1)} %all_to_all.20.part_ref) | copy-start | bytes 491524
  73.9 12.3 %all-to-all-start.3 = ((f32[16,1,128]{2,1,0:T(1,128)}), f32[16,1,128]{2,1,0:T(1,128)S(1)}, u32[]{:S(2)}, u32[]{:S(2)}) async-start(f32[16,1,128]{2,1,0:T(1,128)} %broadcast_in_dim.2), calls=%async_computation.3 | async-start | bytes 16384 | tf_op jit(solution)/shard_map/all_to_all | solution.py:262
  86.2 0.6 copy-start.1

commit v12 on v11

--- a/solution.py
+++ b/solution.py
@@ -232,7 +232,7 @@
     t_cols = lax.all_to_all(moved, "row", 0, 0, tiled=True)
 
     vmem = pl.BlockSpec(memory_space=pltpu.VMEM)
-    tm = 256
+    tm = min(512, rows)
     parts = pl.pallas_call(
         pairs_kernel,
         in_specs=[

time: 89 us -> 89.1 us (level)
  transfers between devices with their start and end apart: 5 -> 5, of which waited for: 4 -> 4; matrix products, arithmetic and copies ran while one was open for 0% -> 0% of each run, Pallas kernels for 4% -> 3%
where the time goes in v12:
time: 89.1 us; the launch traced here: 88.2 us
  starting transfers between devices  32.2 us (36%)
  waiting for transfers between devices  21.4 us (24%)
  blocking collectives  16.6 us (19%)
  Pallas kernels  15.3 us (17%)
  local copies, waits for them, and re-layouts  1.79 us (2%)
    all_to_all x1, blocking collectives, shards(): parts = lax.all_to_all(parts, ('z', 'core', 'depth'), 0, 0, tiled=True)  16.6 us
    pallas_call x1, Pallas kernels, shards(): pl.pallas_call(pairs_kernel, in_specs=[vmem, vmem, vmem, pl.BlockSpec(mem...  9.47 us
    ppermute x1, starting transfers between devices, shards(): moved = lax.ppermute(packed[0], ('row', 'z', 'core', 'depth'), moves)  8.83 us
    all_to_all x1, starting transfers between devices, shards(): t_cols = lax.all_to_all(moved, 'row', 0, 0, tiled=True)  8.63 us
    all_to_all x1, waiting for transfers between devices, shards(): own = lax.all_to_all(packed[1], ('z', 'depth'), 0, 0, tiled=True)  8.58 us
    all_to_all x1, waiting for transfers between devices, shards(): lax.all_to_all(jnp.broadcast_to(shares, (n_row, 1, 128)), 'row', 0, 0, ti...  7.06 us
    all_to_all x1, starting transfers between devices, shards(): own = lax.all_to_all(packed[1], ('z', 'depth'), 0, 0, tiled=True)  6.57 us
    ppermute x1, starting transfers between devices, shards(): oth = lax.ppermute(own, 'core', [(0, 1), (1, 0)])  4.73 us
  transfers between devices with their start and end apart: 5, of which 4 were waited for; matrix products, arithmetic and copies ran while one was open for 0% of the time, Pallas kernels for 3%

profile of v12, /device:TPU:1, one launch (start us, length us, event | category | flops | bytes accessed | tf_op | source)
XLA Modules:
  0.0 88.2 jit_solution(17099419998434184558)
XLA Ops:
  0.6 1.5 %pack.1 = (bf16[48,128]{1,0:T(8,128)(2,1)}, bf16[16,48,128]{2,1,0:T(8,128)(2,1)}) custom-call(bf16[64,64]{1,0:T(8,128)(2,1)} %emb_ref.1, f32[16,64]{1,0:T(8,128)} %crd_ref.3), custom_call_target="tpu_custom_call" | custom-call | tf_op jit(solution)/shard_map/pack/pallas_call | solution.py:213
  2.1 8.8 %collective-permute-start = (bf16[48,128]{1,0:T(8,128)(2,1)}, bf16[48,128]{1,0:T(8,128)(2,1)S(1)}, u32[]{:S(2)}, u32[]{:S(2)}) collective-permute-start(bf16[48,128]{1,0:T(8,128)(2,1)} %get-tuple-element.6), channel_id=1, source_target_pairs={{0,0},{1,32},{2,64},{3,96},{4,128},{5,160},{6,192},{7,224},{8,256}... | collective-permute-start | bytes 36872 | tf_op jit(solution)/shard_map/ppermute | solution.py:222
  10.9 6.6 %all-to-all-start = ((bf16[16,48,128]{2,1,0:T(8,128)(2,1)}), bf16[16,48,128]{2,1,0:T(8,128)(2,1)S(1)}, u32[]{:S(2)}, u32[]{:S(2)}) async-start(bf16[16,48,128]{2,1,0:T(8,128)(2,1)} %get-tuple-element.7), calls=%async_computation | async-start | bytes 393216 | tf_op jit(solution)/shard_map/all_to_all | solution.py:223
  17.5 0.0 collective-permute-done.own_ref
  17.5 0.0 copy-start.2
  17.5 0.6 copy-done.2
  18.1 1.4 %spread.1 = bf16[16,48,128]{2,1,0:T(8,128)(2,1)} custom-call(bf16[48,128]{1,0:T(8,128)(2,1)} %copy-done.2), custom_call_target="tpu_custom_call" | custom-call | flops 10000000000 | bytes 100000000 | tf_op jit(solution)/shard_map/spread/pallas_call | solution.py:224
  19.5 8.6 %all-to-all-done.own_ref = bf16[16,48,128]{2,1,0:T(8,128)(2,1)S(1)} async-done(((bf16[16,48,128]{2,1,0:T(8,128)(2,1)}), bf16[16,48,128]{2,1,0:T(8,128)(2,1)S(1)}, u32[]{:S(2)}, u32[]{:S(2)}) %all-to-all-start) | async-done | bytes 196640 | tf_op jit(solution)/shard_map/all_to_all | solution.py:223
  28.1 8.6 %all-to-all-start.1 = ((bf16[16,48,128]{2,1,0:T(8,128)(2,1)}), bf16[16,48,128]{2,1,0:T(8,128)(2,1)S(1)}, u32[]{:S(2)}, u32[]{:S(2)}) async-start(bf16[16,48,128]{2,1,0:T(8,128)(2,1)} %spread.1), calls=%async_computation.1 | async-start | bytes 393216 | tf_op jit(solution)/shard_map/all_to_all | solution.py:232
  36.7 4.7 %collective-permute-start.1 = (bf16[16,48,128]{2,1,0:T(8,128)(2,1)S(1)}, bf16[16,48,128]{2,1,0:T(8,128)(2,1)S(1)}, u32[]{:S(2)}, u32[]{:S(2)}) collective-permute-start(bf16[16,48,128]{2,1,0:T(8,128)(2,1)S(1)} %all-to-all-done.own_ref), channel_id=1, source_target_pairs={{0,2},{2,0},{1,3},{3,1},{4,6},{6,4},{5,7},{7,5},{8,10},{10,8},{9,1... | collective-permute-start | bytes 589832 | tf_op jit(solution)/shard_map/ppermute | solution.py:231
  41.5 1.0 %collective-permute-done.1.oth_ref = bf16[16,48,128]{2,1,0:T(8,128)(2,1)S(1)} collective-permute-done((bf16[16,48,128]{2,1,0:T(8,128)(2,1)S(1)}, bf16[16,48,128]{2,1,0:T(8,128)(2,1)S(1)}, u32[]{:S(2)}, u32[]{:S(2)}) %collective-permute-start.1) | collective-permute-done | bytes 196640 | tf_op jit(solution)/shard_map/ppermute | solution.py:231
  42.5 4.7 %all-to-all-done.1.col_ref = bf16[16,48,128]{2,1,0:T(8,128)(2,1)S(1)} async-done(((bf16[16,48,128]{2,1,0:T(8,128)(2,1)}), bf16[16,48,128]{2,1,0:T(8,128)(2,1)S(1)}, u32[]{:S(2)}, u32[]{:S(2)}) %all-to-all-start.1) | async-done | bytes 196640 | tf_op jit(solution)/shard_map/all_to_all | solution.py:232
  47.3 9.5 %pairs.1 = f32[32,1,1280]{2,1,0:T(1,128)S(1)} custom-call(bf16[16,48,128]{2,1,0:T(8,128)(2,1)S(1)} %all-to-all-done.own_ref, bf16[16,48,128]{2,1,0:T(8,128)(2,1)S(1)} %collective-permute-done.1.oth_ref, bf16[16,48,128]{2,1,0:T(8,128)(2,1)S(1)} %all-to-all-done.1.col_ref, bf16[2048,1024]{1,0:T(8,128)(2,1)} %w_hbm.1), custom_call_target="tpu_custom_call" | custom-call | tf_op jit(solution)/shard_map/pairs/pallas_call | solution.py:236
  56.7 16.6 %all_to_all.20.part_ref = f32[32,1,1280]{2,1,0:T(1,128)S(1)} all-to-all(f32[32,1,1280]{2,1,0:T(1,128)S(1)} %pairs.1), channel_id=1, replica_groups=mesh['row'=16,'z'=8,'core'=2,'depth'=2] {'z','core','depth'}, dimensions={0} | all-to-all | bytes 327680 | tf_op jit(solution)/shard_map/all_to_all | solution.py:260
  73.3 0.0 copy-start
  73.4 0.6 broadcast_in_dim.2
  74.0 3.5 %all-to-all-start.3 = ((f32[16,1,128]{2,1,0:T(1,128)}), f32[16,1,128]{2,1,0:T(1,128)S(1)}, u32[]{:S(2)}, u32[]{:S(2)}) async-start(f32[16,1,128]{2,1,0:T(1,128)} %broadcast_in_dim.2), calls=%async_computation.3 | async-start | bytes 16384 | tf_op jit(solution)/shard_map/all_to_all | solution.py:262
  77.5 0.0 copy-done
  77.5 1.7 %finish.1 = f32[16,64]{1,0:T(8,128)} custom-call(f32[32,1,1280]{2,1,0:T(1,128)} %copy-done, f32[16,64]{1,0:T(8,128)} %crd_ref.3), custom_call_target="tpu_custom_call" | custom-call | flops 100000 | bytes 200000 | tf_op jit(solution)/shard_map/finish/pallas_call | solution.py:263
  79.2 7.1 %all-to-all-done.3.part_ref = f32[16,1,128]{2,1,0:T(1,128)S(1)} async-done(((f32[16,1,128]{2,1,0:T(1,128)}), f32[16,1,128]{2,1,0:T(1,128)S(1)}, u32[]{:S(2)}, u32[]{:S(2)}) %all-to-all-start.3) | async-done | bytes 8224 | tf_op jit(solution)/shard_map/all_to_all | solution.py:262
  86.3 0.0 copy-start.1
  86.3 0.6 copy-done.1
  86.9 1.3 %stress.1 = f32[1,1]{1,0:T(1,128)} custom-call(f32[16,1,128]{2,1,0:T(1,128)} %copy-done.1), custom_call_target="tpu_custom_call" | custom-call | tf_op jit(solution)/shard_map/stress/pallas_call | solution.py:269
  (1 shorter events, 0.0 us)
Async XLA Ops:
  2.1 15.4 %collective-permute-start = (bf16[48,128]{1,0:T(8,128)(2,1)}, bf16[48,128]{1,0:T(8,128)(2,1)S(1)}, u32[]{:S(2)}, u32[]{:S(2)}) collective-permute-start(bf16[48,128]{1,0:T(8,128)(2,1)} %get-tuple-element.6), channel_id=1, source_target_pairs={{0,0},{1,32},{2,64},{3,96},{4,128},{5,160},{6,192},{7,224},{8,256}... | collective-permute-start | bytes 36872 | tf_op jit(solution)/shard_map/ppermute | solution.py:222
  10.9 17.2 %all-to-all-start = ((bf16[16,48,128]{2,1,0:T(8,128)(2,1)}), bf16[16,48,128]{2,1,0:T(8,128)(2,1)S(1)}, u32[]{:S(2)}, u32[]{:S(2)}) async-start(bf16[16,48,128]{2,1,0:T(8,128)(2,1)} %get-tuple-element.7), calls=%async_computation | async-start | bytes 393216 | tf_op jit(solution)/shard_map/all_to_all | solution.py:223
  17.5 0.6 copy-start.2
  28.1 19.2 %all-to-all-start.1 = ((bf16[16,48,128]{2,1,0:T(8,128)(2,1)}), bf16[16,48,128]{2,1,0:T(8,128)(2,1)S(1)}, u32[]{:S(2)}, u32[]{:S(2)}) async-start(bf16[16,48,128]{2,1,0:T(8,128)(2,1)} %spread.1), calls=%async_computation.1 | async-start | bytes 393216 | tf_op jit(solution)/shard_map/all_to_all | solution.py:232
  36.7 5.8 %collective-permute-start.1 = (bf16[16,48,128]{2,1,0:T(8,128)(2,1)S(1)}, bf16[16,48,128]{2,1,0:T(8,128)(2,1)S(1)}, u32[]{:S(2)}, u32[]{:S(2)}) collective-permute-start(bf16[16,48,128]{2,1,0:T(8,128)(2,1)S(1)} %all-to-all-done.own_ref), channel_id=1, source_target_pairs={{0,2},{2,0},{1,3},{3,1},{4,6},{6,4},{5,7},{7,5},{8,10},{10,8},{9,1... | collective-permute-start | bytes 589832 | tf_op jit(solution)/shard_map/ppermute | solution.py:231
  73.3 4.2 %copy-start = (f32[32,1,1280]{2,1,0:T(1,128)}, f32[32,1,1280]{2,1,0:T(1,128)S(1)}, u32[]{:S(2)}) copy-start(f32[32,1,1280]{2,1,0:T(1,128)S(1)} %all_to_all.20.part_ref) | copy-start | bytes 491524
  74.0 12.3 %all-to-all-start.3 = ((f32[16,1,128]{2,1,0:T(1,128)}), f32[16,1,128]{2,1,0:T(1,128)S(1)}, u32[]{:S(2)}, u32[]{:S(2)}) async-start(f32[16,1,128]{2,1,0:T(1,128)} %broadcast_in_dim.2), calls=%async_computation.3 | async-start | bytes 16384 | tf_op jit(solution)/shard_map/all_to_all | solution.py:262
  86.3 0.6 copy-start.1

commit v13 on v11

--- a/solution.py
+++ b/solution.py
@@ -72,12 +72,21 @@
         out_ref[k] = own
 
 
-def pairs_kernel(own_ref, oth_ref, col_ref, w_hbm, out_ref, w_ref, f_scr, x_scr, flat_scr, rows_scr, c_scr, f_tiles, x_tiles, sems):
+def rows_kernel(own_ref, oth_ref, out_ref):
+    first = lax.axis_index("core") == 0
+    for z in range(own_ref.shape[0] // 2):
+        own = [own_ref[2 * z], own_ref[2 * z + 1]]
+        oth = [oth_ref[2 * z], oth_ref[2 * z + 1]]
+        shards = [jnp.where(first, a, b) for a, b in zip(own, oth)]
+        shards += [jnp.where(first, b, a) for a, b in zip(own, oth)]
+        out_ref[256 * z : 256 * z + 256, :] = unpack(shards).T.astype(BF16)
+
+
+def pairs_kernel(row_ref, col_ref, w_hbm, out_ref, w_ref, f_scr, x_scr, flat_scr, c_scr, f_tiles, x_tiles, sems):
     total_rows, total = w_ref.shape
     tm = c_scr.shape[0]
     tn = min(256, total)
     steps = total_rows // tm
-    first = lax.axis_index("core") == 0
 
     def fetch(i):
         at = pl.ds(i * tm, tm)
@@ -95,17 +104,8 @@
         f_scr[:, cut] = jnp.dot(form_f, some, preferred_element_type=F32).astype(BF16)
         x_scr[:, cut] = jnp.dot(form_x, some, preferred_element_type=F32).astype(BF16)
 
-    def row_block(i, slot):
-        shards = []
-        for k in range(tm // 256):
-            at = i * (tm // 128) + 2 * k
-            own = [own_ref[at], own_ref[at + 1]]
-            oth = [oth_ref[at], oth_ref[at + 1]]
-            shards += [jnp.where(first, a, b) for a, b in zip(own, oth)]
-            shards += [jnp.where(first, b, a) for a, b in zip(own, oth)]
-        feats = unpack(shards)
-        rows_scr[slot] = feats.astype(BF16)
-        return feats.T.astype(BF16)
+    def row_block(i):
+        return row_ref[pl.ds(pl.multiple_of(i * tm, tm), tm), :]
 
     def squares(rows, slot, cut):
         f_tiles[slot, :, cut] = jnp.dot(rows, f_scr[:, cut], preferred_element_type=F32)
@@ -129,8 +129,8 @@
     def block(i, slot, mis, scl, more=True):
         fetch(i).wait()
         if more:
-            rows = row_block(i + 1, 1 - slot)
-        bent = jnp.dot(form_f, rows_scr[slot], preferred_element_type=F32)
+            rows = row_block(i + 1)
+        bent = lax.dot_general(form_f, row_block(i), last, preferred_element_type=F32)
         base = i * tm
         acc = jnp.zeros((48, tm), F32)
         wacc = jnp.zeros((LANES, tm), F32)
@@ -165,7 +165,7 @@
         carry = block(2 * k, 0, *carry)
         return block(2 * k + 1, 1, *carry)
 
-    squares(row_block(0, 0), 0, slice(0, total))
+    squares(row_block(0), 0, slice(0, total))
     pairs = (steps - 1) // 2
     sums = lax.fori_loop(0, pairs, two, (jnp.zeros((8, tn), F32), jnp.zeros((8, tm), F32)))
     for i in range(2 * pairs, steps):
@@ -230,13 +230,18 @@
     moved, own = lax.optimization_barrier((moved, own))
     oth = lax.ppermute(own, "core", [(0, 1), (1, 0)])
     t_cols = lax.all_to_all(moved, "row", 0, 0, tiled=True)
+    t_rows = pl.pallas_call(
+        rows_kernel,
+        out_shape=jax.ShapeDtypeStruct((rows, LANES), BF16),
+        cost_estimate=pl.CostEstimate(flops=10**10, bytes_accessed=10**8, transcendentals=0),
+        name="rows",
+    )(own, oth)
 
     vmem = pl.BlockSpec(memory_space=pltpu.VMEM)
     tm = 256
     parts = pl.pallas_call(
         pairs_kernel,
         in_specs=[
-            vmem,
             vmem,
             vmem,
             pl.BlockSpec(memory_space=pltpu.HBM),
@@ -248,7 +253,6 @@
             pltpu.VMEM((LANES, cols), BF16),
             pltpu.VMEM((LANES, cols), BF16),
             pltpu.VMEM((LANES, cols), BF16),
-            pltpu.VMEM((2, LANES, tm), BF16),
             pltpu.VMEM((tm, cols), BF16),
             pltpu.VMEM((2, tm, cols), F32),
             pltpu.VMEM((2, tm, cols), F32),
@@ -256,7 +260,7 @@
         ],
         compiler_params=pltpu.CompilerParams(vmem_limit_bytes=52 * 1024 * 1024),
         name="pairs",
-    )(own, oth, t_cols, pair_weight)
+    )(t_rows, t_cols, pair_weight)
     parts = lax.all_to_all(parts, ("z", "core", "depth"), 0, 0, tiled=True)
     shares = jnp.sum(parts[:, :, 1152:], axis=0, keepdims=True)
     shares = lax.all_to_all(jnp.broadcast_to(shares, (n_row, 1, 128)), "row", 0, 0, tiled=True)

time: 89 us -> 91.6 us (1.029)
  blocking collectives: 16.6 us -> 13.6 us
  waiting for transfers between devices: 21.4 us -> 24.3 us
  local copies, waits for them, and re-layouts: 1.79 us -> 3.53 us
  Pallas kernels: 15.2 us -> 16.4 us
    all_to_all x1, waiting for transfers between devices: 4.73 us -> 8.7 us  [shards(): t_cols = lax.all_to_all(moved, 'row', 0, 0, tiled=True)]
    all_to_all x1, blocking collectives: 16.6 us -> 13.6 us  [shards(): parts = lax.all_to_all(parts, ('z', 'core', 'depth'), 0, 0, tiled=True)]
    ppermute x1, starting transfers between devices: 4.73 us -> 2.29 us  [shards(): oth = lax.ppermute(own, 'core', [(0, 1), (1, 0)])]
    all_to_all x1, starting transfers between devices: 8.63 us -> 10.8 us  [shards(): t_cols = lax.all_to_all(moved, 'row', 0, 0, tiled=True)]
    unnamed x6 -> x12, local copies, waits for them, and re-layouts: 1.19 us -> 2.9 us
    pallas_call x1 -> x2, Pallas kernels: 9.38 us -> 10.5 us  [the longest x1 8.34 us: shards(): pl.pallas_call(pairs_kernel, in_specs=[vmem, vmem, pl.BlockSpec(memory_sp...]
    ppermute x1, waiting for transfers between devices: 1.05 us -> 0.01 us  [shards(): oth = lax.ppermute(own, 'core', [(0, 1), (1, 0)])]
  transfers between devices with their start and end apart: 5 -> 5, of which waited for: 4 -> 3; matrix products, arithmetic and copies ran while one was open for 0% -> 0% of each run, Pallas kernels for 4% -> 6%
where the time goes in v13:
time: 91.6 us; the launch traced here: 90.6 us
  starting transfers between devices  31.9 us (35%)
  waiting for transfers between devices  24.3 us (27%)
  Pallas kernels  16.4 us (18%)
  blocking collectives  13.6 us (15%)
  local copies, waits for them, and re-layouts  3.53 us (4%)
    all_to_all x1, blocking collectives, shards(): parts = lax.all_to_all(parts, ('z', 'core', 'depth'), 0, 0, tiled=True)  13.6 us
    all_to_all x1, starting transfers between devices, shards(): t_cols = lax.all_to_all(moved, 'row', 0, 0, tiled=True)  10.8 us
    ppermute x1, starting transfers between devices, shards(): moved = lax.ppermute(packed[0], ('row', 'z', 'core', 'depth'), moves)  8.83 us
    all_to_all x1, waiting for transfers between devices, shards(): t_cols = lax.all_to_all(moved, 'row', 0, 0, tiled=True)  8.7 us
    all_to_all x1, waiting for transfers between devices, shards(): own = lax.all_to_all(packed[1], ('z', 'depth'), 0, 0, tiled=True)  8.56 us
    pallas_call x1, Pallas kernels, shards(): pl.pallas_call(pairs_kernel, in_specs=[vmem, vmem, pl.BlockSpec(memory_sp...  8.34 us
    all_to_all x1, waiting for transfers between devices, shards(): lax.all_to_all(jnp.broadcast_to(shares, (n_row, 1, 128)), 'row', 0, 0, ti...  7.06 us
    all_to_all x1, starting transfers between devices, shards(): own = lax.all_to_all(packed[1], ('z', 'depth'), 0, 0, tiled=True)  6.57 us
  transfers between devices with their start and end apart: 5, of which 3 were waited for; matrix products, arithmetic and copies ran while one was open for 0% of the time, Pallas kernels for 6%

profile of v13, /device:TPU:1, one launch (start us, length us, event | category | flops | bytes accessed | tf_op | source)
XLA Modules:
  0.0 90.6 jit_solution(7057496711919068216)
XLA Ops:
  0.6 1.5 %pack.1 = (bf16[48,128]{1,0:T(8,128)(2,1)}, bf16[16,48,128]{2,1,0:T(8,128)(2,1)}) custom-call(bf16[64,64]{1,0:T(8,128)(2,1)} %emb_ref.1, f32[16,64]{1,0:T(8,128)} %crd_ref.3), custom_call_target="tpu_custom_call" | custom-call | tf_op jit(solution)/shard_map/pack/pallas_call | solution.py:213
  2.1 8.8 %collective-permute-start = (bf16[48,128]{1,0:T(8,128)(2,1)}, bf16[48,128]{1,0:T(8,128)(2,1)S(1)}, u32[]{:S(2)}, u32[]{:S(2)}) collective-permute-start(bf16[48,128]{1,0:T(8,128)(2,1)} %get-tuple-element.6), channel_id=1, source_target_pairs={{0,0},{1,32},{2,64},{3,96},{4,128},{5,160},{6,192},{7,224},{8,256}... | collective-permute-start | bytes 36872 | tf_op jit(solution)/shard_map/ppermute | solution.py:222
  11.0 6.6 %all-to-all-start = ((bf16[16,48,128]{2,1,0:T(8,128)(2,1)}), bf16[16,48,128]{2,1,0:T(8,128)(2,1)S(1)}, u32[]{:S(2)}, u32[]{:S(2)}) async-start(bf16[16,48,128]{2,1,0:T(8,128)(2,1)} %get-tuple-element.7), calls=%async_computation | async-start | bytes 393216 | tf_op jit(solution)/shard_map/all_to_all | solution.py:223
  17.5 0.0 collective-permute-done.own_ref
  17.5 0.0 copy-start.5
  17.6 0.6 copy-done.5
  18.1 1.4 %spread.1 = bf16[16,48,128]{2,1,0:T(8,128)(2,1)} custom-call(bf16[48,128]{1,0:T(8,128)(2,1)} %copy-done.5), custom_call_target="tpu_custom_call" | custom-call | flops 10000000000 | bytes 100000000 | tf_op jit(solution)/shard_map/spread/pallas_call | solution.py:224
  19.6 8.6 %all-to-all-done.own_ref = bf16[16,48,128]{2,1,0:T(8,128)(2,1)S(1)} async-done(((bf16[16,48,128]{2,1,0:T(8,128)(2,1)}), bf16[16,48,128]{2,1,0:T(8,128)(2,1)S(1)}, u32[]{:S(2)}, u32[]{:S(2)}) %all-to-all-start) | async-done | bytes 196640 | tf_op jit(solution)/shard_map/all_to_all | solution.py:223
  28.1 0.0 copy-start.2
  28.1 2.3 %collective-permute-start.1 = (bf16[16,48,128]{2,1,0:T(8,128)(2,1)S(1)}, bf16[16,48,128]{2,1,0:T(8,128)(2,1)S(1)}, u32[]{:S(2)}, u32[]{:S(2)}) collective-permute-start(bf16[16,48,128]{2,1,0:T(8,128)(2,1)S(1)} %all-to-all-done.own_ref), channel_id=1, source_target_pairs={{0,2},{2,0},{1,3},{3,1},{4,6},{6,4},{5,7},{7,5},{8,10},{10,8},{9,1... | collective-permute-start | bytes 589832 | tf_op jit(solution)/shard_map/ppermute | solution.py:231
  30.4 10.8 %all-to-all-start.1 = ((bf16[16,48,128]{2,1,0:T(8,128)(2,1)}), bf16[16,48,128]{2,1,0:T(8,128)(2,1)S(1)}, u32[]{:S(2)}, u32[]{:S(2)}) async-start(bf16[16,48,128]{2,1,0:T(8,128)(2,1)} %spread.1), calls=%async_computation.1 | async-start | bytes 393216 | tf_op jit(solution)/shard_map/all_to_all | solution.py:232
  41.2 0.0 collective-permute-done.1.oth_ref
  41.2 0.0 copy-done.2
  41.2 0.0 copy-start.4
  41.3 0.7 copy-done.4
  41.9 2.2 %rows.1.row_ref = bf16[2048,128]{1,0:T(8,128)(2,1)} custom-call(bf16[16,48,128]{2,1,0:T(8,128)(2,1)} %copy-done.2, bf16[16,48,128]{2,1,0:T(8,128)(2,1)} %copy-done.4), custom_call_target="tpu_custom_call" | custom-call | flops 10000000000 | bytes 100000000 | tf_op jit(solution)/shard_map/rows/pallas_call | solution.py:233
  44.1 8.7 %all-to-all-done.1.col_ref = bf16[16,48,128]{2,1,0:T(8,128)(2,1)S(1)} async-done(((bf16[16,48,128]{2,1,0:T(8,128)(2,1)}), bf16[16,48,128]{2,1,0:T(8,128)(2,1)S(1)}, u32[]{:S(2)}, u32[]{:S(2)}) %all-to-all-start.1) | async-done | bytes 196640 | tf_op jit(solution)/shard_map/all_to_all | solution.py:232
  52.8 0.0 copy-start
  52.8 1.0 %copy-done = bf16[2048,128]{1,0:T(8,128)(2,1)S(1)} copy-done((bf16[2048,128]{1,0:T(8,128)(2,1)S(1)}, bf16[2048,128]{1,0:T(8,128)(2,1)}, u32[]{:S(2)}) %copy-start) | copy-done | bytes 524312
  53.9 8.3 %pairs.1 = f32[32,1,1280]{2,1,0:T(1,128)S(1)} custom-call(bf16[2048,128]{1,0:T(8,128)(2,1)S(1)} %copy-done, bf16[16,48,128]{2,1,0:T(8,128)(2,1)S(1)} %all-to-all-done.1.col_ref, bf16[2048,1024]{1,0:T(8,128)(2,1)} %w_hbm.1), custom_call_target="tpu_custom_call" | custom-call | tf_op jit(solution)/shard_map/pairs/pallas_call | solution.py:242
  62.2 13.6 %all_to_all.20.part_ref = f32[32,1,1280]{2,1,0:T(1,128)S(1)} all-to-all(f32[32,1,1280]{2,1,0:T(1,128)S(1)} %pairs.1), channel_id=1, replica_groups=mesh['row'=16,'z'=8,'core'=2,'depth'=2] {'z','core','depth'}, dimensions={0} | all-to-all | bytes 327680 | tf_op jit(solution)/shard_map/all_to_all | solution.py:264
  75.8 0.0 copy-start.1
  75.9 0.6 broadcast_in_dim.2
  76.5 3.4 %all-to-all-start.3 = ((f32[16,1,128]{2,1,0:T(1,128)}), f32[16,1,128]{2,1,0:T(1,128)S(1)}, u32[]{:S(2)}, u32[]{:S(2)}) async-start(f32[16,1,128]{2,1,0:T(1,128)} %broadcast_in_dim.2), calls=%async_computation.3 | async-start | bytes 16384 | tf_op jit(solution)/shard_map/all_to_all | solution.py:266
  80.0 0.0 copy-done.1
  80.0 1.7 %finish.1 = f32[16,64]{1,0:T(8,128)} custom-call(f32[32,1,1280]{2,1,0:T(1,128)} %copy-done.1, f32[16,64]{1,0:T(8,128)} %crd_ref.3), custom_call_target="tpu_custom_call" | custom-call | flops 100000 | bytes 200000 | tf_op jit(solution)/shard_map/finish/pallas_call | solution.py:267
  81.7 7.1 %all-to-all-done.3.part_ref = f32[16,1,128]{2,1,0:T(1,128)S(1)} async-done(((f32[16,1,128]{2,1,0:T(1,128)}), f32[16,1,128]{2,1,0:T(1,128)S(1)}, u32[]{:S(2)}, u32[]{:S(2)}) %all-to-all-start.3) | async-done | bytes 8224 | tf_op jit(solution)/shard_map/all_to_all | solution.py:266
  88.7 0.0 copy-start.3
  88.7 0.6 copy-done.3
  89.3 1.3 %stress.1 = f32[1,1]{1,0:T(1,128)} custom-call(f32[16,1,128]{2,1,0:T(1,128)} %copy-done.3), custom_call_target="tpu_custom_call" | custom-call | tf_op jit(solution)/shard_map/stress/pallas_call | solution.py:273
  (1 shorter events, 0.0 us)
Async XLA Ops:
  2.1 15.4 %collective-permute-start = (bf16[48,128]{1,0:T(8,128)(2,1)}, bf16[48,128]{1,0:T(8,128)(2,1)S(1)}, u32[]{:S(2)}, u32[]{:S(2)}) collective-permute-start(bf16[48,128]{1,0:T(8,128)(2,1)} %get-tuple-element.6), channel_id=1, source_target_pairs={{0,0},{1,32},{2,64},{3,96},{4,128},{5,160},{6,192},{7,224},{8,256}... | collective-permute-start | bytes 36872 | tf_op jit(solution)/shard_map/ppermute | solution.py:222
  11.0 17.2 %all-to-all-start = ((bf16[16,48,128]{2,1,0:T(8,128)(2,1)}), bf16[16,48,128]{2,1,0:T(8,128)(2,1)S(1)}, u32[]{:S(2)}, u32[]{:S(2)}) async-start(bf16[16,48,128]{2,1,0:T(8,128)(2,1)} %get-tuple-element.7), calls=%async_computation | async-start | bytes 393216 | tf_op jit(solution)/shard_map/all_to_all | solution.py:223
  17.5 0.6 copy-start.5
  28.1 13.1 %copy-start.2 = (bf16[16,48,128]{2,1,0:T(8,128)(2,1)}, bf16[16,48,128]{2,1,0:T(8,128)(2,1)S(1)}, u32[]{:S(2)}) copy-start(bf16[16,48,128]{2,1,0:T(8,128)(2,1)S(1)} %all-to-all-done.own_ref) | copy-start | bytes 589828
  28.1 13.1 %collective-permute-start.1 = (bf16[16,48,128]{2,1,0:T(8,128)(2,1)S(1)}, bf16[16,48,128]{2,1,0:T(8,128)(2,1)S(1)}, u32[]{:S(2)}, u32[]{:S(2)}) collective-permute-start(bf16[16,48,128]{2,1,0:T(8,128)(2,1)S(1)} %all-to-all-done.own_ref), channel_id=1, source_target_pairs={{0,2},{2,0},{1,3},{3,1},{4,6},{6,4},{5,7},{7,5},{8,10},{10,8},{9,1... | collective-permute-start | bytes 589832 | tf_op jit(solution)/shard_map/ppermute | solution.py:231
  30.4 22.4 %all-to-all-start.1 = ((bf16[16,48,128]{2,1,0:T(8,128)(2,1)}), bf16[16,48,128]{2,1,0:T(8,128)(2,1)S(1)}, u32[]{:S(2)}, u32[]{:S(2)}) async-start(bf16[16,48,128]{2,1,0:T(8,128)(2,1)} %spread.1), calls=%async_computation.1 | async-start | bytes 393216 | tf_op jit(solution)/shard_map/all_to_all | solution.py:232
  41.2 0.7 copy-start.4
  52.8 1.0 %copy-start = (bf16[2048,128]{1,0:T(8,128)(2,1)S(1)}, bf16[2048,128]{1,0:T(8,128)(2,1)}, u32[]{:S(2)}) copy-start(bf16[2048,128]{1,0:T(8,128)(2,1)} %rows.1.row_ref) | copy-start | bytes 1572868
  75.8 4.1 %copy-start.1 = (f32[32,1,1280]{2,1,0:T(1,128)}, f32[32,1,1280]{2,1,0:T(1,128)S(1)}, u32[]{:S(2)}) copy-start(f32[32,1,1280]{2,1,0:T(1,128)S(1)} %all_to_all.20.part_ref) | copy-start | bytes 491524
  76.5 12.2 %all-to-all-start.3 = ((f32[16,1,128]{2,1,0:T(1,128)}), f32[16,1,128]{2,1,0:T(1,128)S(1)}, u32[]{:S(2)}, u32[]{:S(2)}) async-start(f32[16,1,128]{2,1,0:T(1,128)} %broadcast_in_dim.2), calls=%async_computation.3 | async-start | bytes 16384 | tf_op jit(solution)/shard_map/all_to_all | solution.py:266
  88.7 0.6 copy-start.3

commit v14 on v11

--- a/solution.py
+++ b/solution.py
@@ -36,14 +36,25 @@
     return hi, mid, low
 
 
+def norm_rows(emb, crd):
+    squares = split3(jnp.sum(emb * emb, axis=0, keepdims=True))
+    squares += split3(jnp.sum(crd * crd, axis=0, keepdims=True))
+    at = lax.broadcasted_iota(jnp.int32, (16, emb.shape[1]), 0)
+    tail = jnp.where((at >= ONE - QF) & (at < ONE - QF + 3), 1.0, 0.0)
+    for k, sq in enumerate(squares):
+        tail = jnp.where(at == k, sq, tail)
+    return tail
+
+
 def pack_kernel(emb_ref, crd_ref, own_ref, out_ref):
     emb = emb_ref[...].astype(F32)
     crd = crd_ref[...]
     hi = crd.astype(BF16).astype(F32)
-    feats = jnp.concatenate([emb, hi, crd - hi], axis=0)
+    low = (crd - hi).astype(BF16).astype(F32)
+    feats = jnp.concatenate([emb, hi, low], axis=0)
     half = feats.shape[0] // 2
-    mine = jnp.concatenate([feats[:half], feats[half:]], axis=1).astype(BF16)
-    own_ref[...] = mine
+    own_ref[...] = jnp.concatenate([feats[:half], feats[half:]], axis=1).astype(BF16)
+    mine = jnp.concatenate([feats, hi, norm_rows(emb, hi + low)], axis=0).T.astype(BF16)
     for k in range(out_ref.shape[0]):
         out_ref[k] = mine
 
@@ -55,15 +66,8 @@
         top.append(sh[:, 0:64])
         low.append(sh[:, 64:128])
     feats = jnp.concatenate([jnp.concatenate(top, axis=1), jnp.concatenate(low, axis=1)], axis=0)
-    emb, hi, low = feats[0:64], feats[XH : XH + 16], feats[XL : XL + 16]
-    crd = hi + low
-    squares = split3(jnp.sum(emb * emb, axis=0, keepdims=True))
-    squares += split3(jnp.sum(crd * crd, axis=0, keepdims=True))
-    at = lax.broadcasted_iota(jnp.int32, (16, feats.shape[1]), 0)
-    tail = jnp.where((at >= ONE - QF) & (at < ONE - QF + 3), 1.0, 0.0)
-    for k, sq in enumerate(squares):
-        tail = jnp.where(at == k, sq, tail)
-    return jnp.concatenate([feats, hi, tail], axis=0)
+    hi, low = feats[XH : XH + 16], feats[XL : XL + 16]
+    return jnp.concatenate([feats, hi, norm_rows(feats[0:64], hi + low)], axis=0)
 
 
 def spread_kernel(own_ref, out_ref):
@@ -72,7 +76,7 @@
         out_ref[k] = own
 
 
-def pairs_kernel(own_ref, oth_ref, col_ref, w_hbm, out_ref, w_ref, f_scr, x_scr, flat_scr, rows_scr, c_scr, f_tiles, x_tiles, sems):
+def pairs_kernel(own_ref, oth_ref, col_ref, w_hbm, out_ref, w_ref, f_scr, x_scr, flat_scr, c_scr, f_tiles, x_tiles, sems):
     total_rows, total = w_ref.shape
     tm = c_scr.shape[0]
     tn = min(256, total)
@@ -88,24 +92,14 @@
     last = (((1,), (1,)), ((), ()))
     form_f = bilinear_form(0)
     form_x = bilinear_form(1)
-    for s in range(0, col_ref.shape[0], 4):
-        some = unpack([col_ref[k] for k in range(s, min(s + 4, col_ref.shape[0]))]).astype(BF16)
-        cut = slice(64 * s, 64 * s + some.shape[1])
-        flat_scr[:, cut] = some
-        f_scr[:, cut] = jnp.dot(form_f, some, preferred_element_type=F32).astype(BF16)
-        x_scr[:, cut] = jnp.dot(form_x, some, preferred_element_type=F32).astype(BF16)
-
-    def row_block(i, slot):
-        shards = []
+
+    def row_block(i):
+        pieces = []
         for k in range(tm // 256):
-            at = i * (tm // 128) + 2 * k
-            own = [own_ref[at], own_ref[at + 1]]
-            oth = [oth_ref[at], oth_ref[at + 1]]
-            shards += [jnp.where(first, a, b) for a, b in zip(own, oth)]
-            shards += [jnp.where(first, b, a) for a, b in zip(own, oth)]
-        feats = unpack(shards)
-        rows_scr[slot] = feats.astype(BF16)
-        return feats.T.astype(BF16)
+            cut = pl.ds(pl.multiple_of(i * (tm // 2) + k * 128, 128), 128)
+            own, oth = own_ref[cut, :], oth_ref[cut, :]
+            pieces += [jnp.where(first, own, oth), jnp.where(first, oth, own)]
+        return jnp.concatenate(pieces, axis=0)
 
     def squares(rows, slot, cut):
         f_tiles[slot, :, cut] = jnp.dot(rows, f_scr[:, cut], preferred_element_type=F32)
@@ -129,8 +123,8 @@
     def block(i, slot, mis, scl, more=True):
         fetch(i).wait()
         if more:
-            rows = row_block(i + 1, 1 - slot)
-        bent = jnp.dot(form_f, rows_scr[slot], preferred_element_type=F32)
+            rows = row_block(i + 1)
+        bent = lax.dot_general(form_f, row_block(i), last, preferred_element_type=F32)
         base = i * tm
         acc = jnp.zeros((48, tm), F32)
         wacc = jnp.zeros((LANES, tm), F32)
@@ -162,15 +156,24 @@
         return mis, scl
 
     def two(k, carry):
-        carry = block(2 * k, 0, *carry)
-        return block(2 * k + 1, 1, *carry)
-
-    squares(row_block(0, 0), 0, slice(0, total))
-    pairs = (steps - 1) // 2
-    sums = lax.fori_loop(0, pairs, two, (jnp.zeros((8, tn), F32), jnp.zeros((8, tm), F32)))
-    for i in range(2 * pairs, steps):
-        sums = block(i, i % 2, *sums, more=i + 1 < steps)
-    mis, scl = sums
+        carry = block(2 * k + 1, 1, *carry)
+        return block(2 * k + 2, 0, *carry)
+
+    rows = row_block(0)
+    per = tn // 64
+    for n, cut in enumerate(tiles):
+        some = unpack([col_ref[k] for k in range(n * per, n * per + per)]).astype(BF16)
+        flat_scr[:, cut] = some
+        f_scr[:, cut] = jnp.dot(form_f, some, preferred_element_type=F32).astype(BF16)
+        x_scr[:, cut] = jnp.dot(form_x, some, preferred_element_type=F32).astype(BF16)
+        squares(rows, 0, cut)
+    carry = (jnp.zeros((8, tn), F32), jnp.zeros((8, tm), F32))
+    carry = block(0, 0, *carry, more=steps > 1)
+    loops = max(0, (steps - 2) // 2)
+    carry = lax.fori_loop(0, loops, two, carry)
+    for i in range(2 * loops + 1, steps):
+        carry = block(i, i % 2, *carry, more=i + 1 < steps)
+    mis, scl = carry
     mis = jnp.sum(jnp.sum(mis, axis=0, keepdims=True), axis=1, keepdims=True)
     scl = jnp.sum(jnp.sum(scl, axis=0, keepdims=True), axis=1, keepdims=True)
     at = lax.broadcasted_iota(jnp.int32, (1, 128), 1)
@@ -214,7 +217,7 @@
         pack_kernel,
         out_shape=(
             jax.ShapeDtypeStruct(shard, BF16),
-            jax.ShapeDtypeStruct((likes,) + shard, BF16),
+            jax.ShapeDtypeStruct((likes, points, LANES), BF16),
         ),
         name="pack",
     )(embeddings, coords)
@@ -228,6 +231,7 @@
         name="spread",
     )(moved)
     moved, own = lax.optimization_barrier((moved, own))
+    own = own.reshape(rows // n_core, LANES)
     oth = lax.ppermute(own, "core", [(0, 1), (1, 0)])
     t_cols = lax.all_to_all(moved, "row", 0, 0, tiled=True)
 
@@ -248,7 +252,6 @@
             pltpu.VMEM((LANES, cols), BF16),
             pltpu.VMEM((LANES, cols), BF16),
             pltpu.VMEM((LANES, cols), BF16),
-            pltpu.VMEM((2, LANES, tm), BF16),
             pltpu.VMEM((tm, cols), BF16),
             pltpu.VMEM((2, tm, cols), F32),
             pltpu.VMEM((2, tm, cols), F32),

time: 89 us -> 90.1 us (1.012)
  waiting for transfers between devices: 21.4 us -> 22.8 us
    all_to_all x1, waiting for transfers between devices: 8.58 us -> 9.67 us  [shards(): own = lax.all_to_all(packed[1], ('z', 'depth'), 0, 0, tiled=True)]
  transfers between devices with their start and end apart: 5 -> 5, of which waited for: 4 -> 4; matrix products, arithmetic and copies ran while one was open for 0% -> 0% of each run, Pallas kernels for 4% -> 3%
where the time goes in v14:
time: 90.1 us; the launch traced here: 89.1 us
  starting transfers between devices  32.4 us (36%)
  waiting for transfers between devices  22.8 us (25%)
  blocking collectives  16.6 us (18%)
  Pallas kernels  14.8 us (16%)
  local copies, waits for them, and re-layouts  1.79 us (2%)
    all_to_all x1, blocking collectives, shards(): parts = lax.all_to_all(parts, ('z', 'core', 'depth'), 0, 0, tiled=True)  16.6 us
    all_to_all x1, waiting for transfers between devices, shards(): own = lax.all_to_all(packed[1], ('z', 'depth'), 0, 0, tiled=True)  9.67 us
    all_to_all x1, starting transfers between devices, shards(): t_cols = lax.all_to_all(moved, 'row', 0, 0, tiled=True)  9.1 us
    pallas_call x1, Pallas kernels, shards(): pl.pallas_call(pairs_kernel, in_specs=[vmem, vmem, vmem, pl.BlockSpec(mem...  8.86 us
    ppermute x1, starting transfers between devices, shards(): moved = lax.ppermute(packed[0], ('row', 'z', 'core', 'depth'), moves)  8.83 us
    all_to_all x1, waiting for transfers between devices, shards(): lax.all_to_all(jnp.broadcast_to(shares, (n_row, 1, 128)), 'row', 0, 0, ti...  7.06 us
    all_to_all x1, starting transfers between devices, shards(): own = lax.all_to_all(packed[1], ('z', 'depth'), 0, 0, tiled=True)  6.57 us
    all_to_all x1, waiting for transfers between devices, shards(): t_cols = lax.all_to_all(moved, 'row', 0, 0, tiled=True)  4.93 us
  transfers between devices with their start and end apart: 5, of which 4 were waited for; matrix products, arithmetic and copies ran while one was open for 0% of the time, Pallas kernels for 3%

profile of v14, /device:TPU:1, one launch (start us, length us, event | category | flops | bytes accessed | tf_op | source)
XLA Modules:
  0.0 89.1 jit_solution(7829842022219394535)
XLA Ops:
  0.6 1.5 %pack.1 = (bf16[48,128]{1,0:T(8,128)(2,1)}, bf16[16,64,128]{2,1,0:T(8,128)(2,1)}) custom-call(bf16[64,64]{1,0:T(8,128)(2,1)} %emb_ref.1, f32[16,64]{1,0:T(8,128)} %crd_ref.3), custom_call_target="tpu_custom_call" | custom-call | tf_op jit(solution)/shard_map/pack/pallas_call | solution.py:216
  2.2 8.8 %collective-permute-start = (bf16[48,128]{1,0:T(8,128)(2,1)}, bf16[48,128]{1,0:T(8,128)(2,1)S(1)}, u32[]{:S(2)}, u32[]{:S(2)}) collective-permute-start(bf16[48,128]{1,0:T(8,128)(2,1)} %get-tuple-element.6), channel_id=1, source_target_pairs={{0,0},{1,32},{2,64},{3,96},{4,128},{5,160},{6,192},{7,224},{8,256}... | collective-permute-start | bytes 36872 | tf_op jit(solution)/shard_map/ppermute | solution.py:225
  11.0 6.6 %all-to-all-start = ((bf16[16,64,128]{2,1,0:T(8,128)(2,1)}), bf16[16,64,128]{2,1,0:T(8,128)(2,1)S(1)}, u32[]{:S(2)}, u32[]{:S(2)}) async-start(bf16[16,64,128]{2,1,0:T(8,128)(2,1)} %get-tuple-element.7), calls=%async_computation | async-start | bytes 524288 | tf_op jit(solution)/shard_map/all_to_all | solution.py:226
  17.6 0.0 collective-permute-done.own_ref
  17.6 0.0 copy-start.2
  17.6 0.6 copy-done.2
  18.2 1.4 %spread.1 = bf16[16,48,128]{2,1,0:T(8,128)(2,1)} custom-call(bf16[48,128]{1,0:T(8,128)(2,1)} %copy-done.2), custom_call_target="tpu_custom_call" | custom-call | flops 10000000000 | bytes 100000000 | tf_op jit(solution)/shard_map/spread/pallas_call | solution.py:227
  19.6 9.7 %all-to-all-done = bf16[16,64,128]{2,1,0:T(8,128)(2,1)S(1)} async-done(((bf16[16,64,128]{2,1,0:T(8,128)(2,1)}), bf16[16,64,128]{2,1,0:T(8,128)(2,1)S(1)}, u32[]{:S(2)}, u32[]{:S(2)}) %all-to-all-start) | async-done | bytes 262176 | tf_op jit(solution)/shard_map/all_to_all | solution.py:226
  29.3 9.1 %all-to-all-start.1 = ((bf16[16,48,128]{2,1,0:T(8,128)(2,1)}), bf16[16,48,128]{2,1,0:T(8,128)(2,1)S(1)}, u32[]{:S(2)}, u32[]{:S(2)}) async-start(bf16[16,48,128]{2,1,0:T(8,128)(2,1)} %spread.1), calls=%async_computation.1 | async-start | bytes 393216 | tf_op jit(solution)/shard_map/all_to_all | solution.py:236
  38.4 4.4 %collective-permute-start.1 = (bf16[1024,128]{1,0:T(8,128)(2,1)S(1)}, bf16[1024,128]{1,0:T(8,128)(2,1)S(1)}, u32[]{:S(2)}, u32[]{:S(2)}) collective-permute-start(bf16[1024,128]{1,0:T(8,128)(2,1)S(1)} %bitcast.2), channel_id=1, source_target_pairs={{0,2},{2,0},{1,3},{3,1},{4,6},{6,4},{5,7},{7,5},{8,10},{10,8},{9,1... | collective-permute-start | bytes 786440 | tf_op jit(solution)/shard_map/ppermute | solution.py:235
  42.8 1.1 %collective-permute-done.1.oth_ref = bf16[1024,128]{1,0:T(8,128)(2,1)S(1)} collective-permute-done((bf16[1024,128]{1,0:T(8,128)(2,1)S(1)}, bf16[1024,128]{1,0:T(8,128)(2,1)S(1)}, u32[]{:S(2)}, u32[]{:S(2)}) %collective-permute-start.1) | collective-permute-done | bytes 262176 | tf_op jit(solution)/shard_map/ppermute | solution.py:235
  44.0 4.9 %all-to-all-done.1.col_ref = bf16[16,48,128]{2,1,0:T(8,128)(2,1)S(1)} async-done(((bf16[16,48,128]{2,1,0:T(8,128)(2,1)}), bf16[16,48,128]{2,1,0:T(8,128)(2,1)S(1)}, u32[]{:S(2)}, u32[]{:S(2)}) %all-to-all-start.1) | async-done | bytes 196640 | tf_op jit(solution)/shard_map/all_to_all | solution.py:236
  48.9 8.9 %pairs.1 = f32[32,1,1280]{2,1,0:T(1,128)S(1)} custom-call(bf16[1024,128]{1,0:T(8,128)(2,1)S(1)} %bitcast.3, bf16[1024,128]{1,0:T(8,128)(2,1)S(1)} %collective-permute-done.1.oth_ref, bf16[16,48,128]{2,1,0:T(8,128)(2,1)S(1)} %all-to-all-done.1.col_ref, bf16[2048,1024]{1,0:T(8,128)(2,1)} %w_hbm.1), custom_call_target="tpu_custom_call" | custom-call | tf_op jit(solution)/shard_map/pairs/pallas_call | solution.py:240
  57.8 16.6 %all_to_all.20.part_ref = f32[32,1,1280]{2,1,0:T(1,128)S(1)} all-to-all(f32[32,1,1280]{2,1,0:T(1,128)S(1)} %pairs.1), channel_id=1, replica_groups=mesh['row'=16,'z'=8,'core'=2,'depth'=2] {'z','core','depth'}, dimensions={0} | all-to-all | bytes 327680 | tf_op jit(solution)/shard_map/all_to_all | solution.py:263
  74.3 0.0 copy-start
  74.4 0.6 broadcast_in_dim.2
  75.0 3.5 %all-to-all-start.3 = ((f32[16,1,128]{2,1,0:T(1,128)}), f32[16,1,128]{2,1,0:T(1,128)S(1)}, u32[]{:S(2)}, u32[]{:S(2)}) async-start(f32[16,1,128]{2,1,0:T(1,128)} %broadcast_in_dim.2), calls=%async_computation.3 | async-start | bytes 16384 | tf_op jit(solution)/shard_map/all_to_all | solution.py:265
  78.5 0.0 copy-done
  78.5 1.7 %finish.1 = f32[16,64]{1,0:T(8,128)} custom-call(f32[32,1,1280]{2,1,0:T(1,128)} %copy-done, f32[16,64]{1,0:T(8,128)} %crd_ref.3), custom_call_target="tpu_custom_call" | custom-call | flops 100000 | bytes 200000 | tf_op jit(solution)/shard_map/finish/pallas_call | solution.py:266
  80.2 7.1 %all-to-all-done.3.part_ref = f32[16,1,128]{2,1,0:T(1,128)S(1)} async-done(((f32[16,1,128]{2,1,0:T(1,128)}), f32[16,1,128]{2,1,0:T(1,128)S(1)}, u32[]{:S(2)}, u32[]{:S(2)}) %all-to-all-start.3) | async-done | bytes 8224 | tf_op jit(solution)/shard_map/all_to_all | solution.py:265
  87.2 0.0 copy-start.1
  87.2 0.6 copy-done.1
  87.8 1.3 %stress.1 = f32[1,1]{1,0:T(1,128)} custom-call(f32[16,1,128]{2,1,0:T(1,128)} %copy-done.1), custom_call_target="tpu_custom_call" | custom-call | tf_op jit(solution)/shard_map/stress/pallas_call | solution.py:272
  (1 shorter events, 0.0 us)
Async XLA Ops:
  2.2 15.4 %collective-permute-start = (bf16[48,128]{1,0:T(8,128)(2,1)}, bf16[48,128]{1,0:T(8,128)(2,1)S(1)}, u32[]{:S(2)}, u32[]{:S(2)}) collective-permute-start(bf16[48,128]{1,0:T(8,128)(2,1)} %get-tuple-element.6), channel_id=1, source_target_pairs={{0,0},{1,32},{2,64},{3,96},{4,128},{5,160},{6,192},{7,224},{8,256}... | collective-permute-start | bytes 36872 | tf_op jit(solution)/shard_map/ppermute | solution.py:225
  11.0 18.3 %all-to-all-start = ((bf16[16,64,128]{2,1,0:T(8,128)(2,1)}), bf16[16,64,128]{2,1,0:T(8,128)(2,1)S(1)}, u32[]{:S(2)}, u32[]{:S(2)}) async-start(bf16[16,64,128]{2,1,0:T(8,128)(2,1)} %get-tuple-element.7), calls=%async_computation | async-start | bytes 524288 | tf_op jit(solution)/shard_map/all_to_all | solution.py:226
  17.6 0.6 copy-start.2
  29.3 19.6 %all-to-all-start.1 = ((bf16[16,48,128]{2,1,0:T(8,128)(2,1)}), bf16[16,48,128]{2,1,0:T(8,128)(2,1)S(1)}, u32[]{:S(2)}, u32[]{:S(2)}) async-start(bf16[16,48,128]{2,1,0:T(8,128)(2,1)} %spread.1), calls=%async_computation.1 | async-start | bytes 393216 | tf_op jit(solution)/shard_map/all_to_all | solution.py:236
  38.4 5.6 %collective-permute-start.1 = (bf16[1024,128]{1,0:T(8,128)(2,1)S(1)}, bf16[1024,128]{1,0:T(8,128)(2,1)S(1)}, u32[]{:S(2)}, u32[]{:S(2)}) collective-permute-start(bf16[1024,128]{1,0:T(8,128)(2,1)S(1)} %bitcast.2), channel_id=1, source_target_pairs={{0,2},{2,0},{1,3},{3,1},{4,6},{6,4},{5,7},{7,5},{8,10},{10,8},{9,1... | collective-permute-start | bytes 786440 | tf_op jit(solution)/shard_map/ppermute | solution.py:235
  74.3 4.2 %copy-start = (f32[32,1,1280]{2,1,0:T(1,128)}, f32[32,1,1280]{2,1,0:T(1,128)S(1)}, u32[]{:S(2)}) copy-start(f32[32,1,1280]{2,1,0:T(1,128)S(1)} %all_to_all.20.part_ref) | copy-start | bytes 491524
  75.0 12.3 %all-to-all-start.3 = ((f32[16,1,128]{2,1,0:T(1,128)}), f32[16,1,128]{2,1,0:T(1,128)S(1)}, u32[]{:S(2)}, u32[]{:S(2)}) async-start(f32[16,1,128]{2,1,0:T(1,128)} %broadcast_in_dim.2), calls=%async_computation.3 | async-start | bytes 16384 | tf_op jit(solution)/shard_map/all_to_all | solution.py:265
  87.2 0.6 copy-start.1

commit v15 on v11

--- a/solution.py
+++ b/solution.py
@@ -72,7 +72,7 @@
         out_ref[k] = own
 
 
-def pairs_kernel(own_ref, oth_ref, col_ref, w_hbm, out_ref, w_ref, f_scr, x_scr, flat_scr, rows_scr, c_scr, f_tiles, x_tiles, sems):
+def pairs_kernel(own_ref, oth_ref, col_ref, w_hbm, out_ref, w_ref, f_scr, x_scr, flat_scr, rows_scr, feat_scr, c_scr, f_tiles, x_tiles, sems):
     total_rows, total = w_ref.shape
     tm = c_scr.shape[0]
     tn = min(256, total)
@@ -104,10 +104,11 @@
             shards += [jnp.where(first, a, b) for a, b in zip(own, oth)]
             shards += [jnp.where(first, b, a) for a, b in zip(own, oth)]
         feats = unpack(shards)
-        rows_scr[slot] = feats.astype(BF16)
-        return feats.T.astype(BF16)
-
-    def squares(rows, slot, cut):
+        feat_scr[slot] = feats.astype(BF16)
+        rows_scr[slot] = feats.T.astype(BF16)
+
+    def squares(slot, cut):
+        rows = rows_scr[slot]
         f_tiles[slot, :, cut] = jnp.dot(rows, f_scr[:, cut], preferred_element_type=F32)
         x_tiles[slot, :, cut] = jnp.dot(rows, x_scr[:, cut], preferred_element_type=F32)
 
@@ -126,19 +127,17 @@
 
     tiles = [slice(start, start + tn) for start in range(0, total, tn)]
 
-    def block(i, slot, mis, scl, more=True):
+    def block(i, slot, mis, scl, ahead=2):
         fetch(i).wait()
-        if more:
-            rows = row_block(i + 1, 1 - slot)
-        bent = jnp.dot(form_f, rows_scr[slot], preferred_element_type=F32)
+        bent = jnp.dot(form_f, feat_scr[slot], preferred_element_type=F32)
         base = i * tm
         acc = jnp.zeros((48, tm), F32)
         wacc = jnp.zeros((LANES, tm), F32)
         for n in range(len(tiles) + 1):
             if n < len(tiles):
                 cut = tiles[n]
-                if more:
-                    squares(rows, 1 - slot, cut)
+                if ahead > 0:
+                    squares(1 - slot, cut)
                 wb = w_ref[pl.ds(pl.multiple_of(base, tm), tm), cut]
                 wacc += lax.dot_general(flat_scr[:, cut], wb, last, preferred_element_type=F32)
             if n > 0:
@@ -147,6 +146,8 @@
                 acc += lax.dot_general(picked, c_scr[:, old], last, preferred_element_type=F32)
             if n < len(tiles):
                 mis = chain(base, slot, cut, mis)
+            if n == 0 and ahead > 1:
+                row_block(i + 2, slot)
         scl += jnp.sum((bent * wacc).reshape(LANES // 8, 8, tm), axis=0)
         less = acc[0:32] - wacc[XH : XH + 32]
         pull = less[0:16] + less[16:32]
@@ -165,12 +166,16 @@
         carry = block(2 * k, 0, *carry)
         return block(2 * k + 1, 1, *carry)
 
-    squares(row_block(0, 0), 0, slice(0, total))
-    pairs = (steps - 1) // 2
-    sums = lax.fori_loop(0, pairs, two, (jnp.zeros((8, tn), F32), jnp.zeros((8, tm), F32)))
-    for i in range(2 * pairs, steps):
-        sums = block(i, i % 2, *sums, more=i + 1 < steps)
-    mis, scl = sums
+    row_block(0, 0)
+    if steps > 1:
+        row_block(1, 1)
+    squares(0, slice(0, total))
+    loops = max(0, (steps - 2) // 2)
+    carry = (jnp.zeros((8, tn), F32), jnp.zeros((8, tm), F32))
+    carry = lax.fori_loop(0, loops, two, carry)
+    for i in range(2 * loops, steps):
+        carry = block(i, i % 2, *carry, ahead=steps - 1 - i)
+    mis, scl = carry
     mis = jnp.sum(jnp.sum(mis, axis=0, keepdims=True), axis=1, keepdims=True)
     scl = jnp.sum(jnp.sum(scl, axis=0, keepdims=True), axis=1, keepdims=True)
     at = lax.broadcasted_iota(jnp.int32, (1, 128), 1)
@@ -248,6 +253,7 @@
             pltpu.VMEM((LANES, cols), BF16),
             pltpu.VMEM((LANES, cols), BF16),
             pltpu.VMEM((LANES, cols), BF16),
+            pltpu.VMEM((2, tm, LANES), BF16),
             pltpu.VMEM((2, LANES, tm), BF16),
             pltpu.VMEM((tm, cols), BF16),
             pltpu.VMEM((2, tm, cols), F32),

time: 89 us -> 88.1 us (0.990)
  Pallas kernels: 15.2 us -> 14.3 us
    pallas_call x1, Pallas kernels: 9.38 us -> 8.47 us  [shards(): pl.pallas_call(pairs_kernel, in_specs=[vmem, vmem, vmem, pl.BlockSpec(mem...]
where the time goes in v15:
time: 88.1 us; the launch traced here: 87.1 us
  starting transfers between devices  32.2 us (37%)
  waiting for transfers between devices  21.4 us (24%)
  blocking collectives  16.6 us (19%)
  Pallas kernels  14.3 us (16%)
  local copies, waits for them, and re-layouts  1.79 us (2%)
    all_to_all x1, blocking collectives, shards(): parts = lax.all_to_all(parts, ('z', 'core', 'depth'), 0, 0, tiled=True)  16.6 us
    ppermute x1, starting transfers between devices, shards(): moved = lax.ppermute(packed[0], ('row', 'z', 'core', 'depth'), moves)  8.83 us
    all_to_all x1, starting transfers between devices, shards(): t_cols = lax.all_to_all(moved, 'row', 0, 0, tiled=True)  8.63 us
    all_to_all x1, waiting for transfers between devices, shards(): own = lax.all_to_all(packed[1], ('z', 'depth'), 0, 0, tiled=True)  8.58 us
    pallas_call x1, Pallas kernels, shards(): pl.pallas_call(pairs_kernel, in_specs=[vmem, vmem, vmem, pl.BlockSpec(mem...  8.47 us
    all_to_all x1, waiting for transfers between devices, shards(): lax.all_to_all(jnp.broadcast_to(shares, (n_row, 1, 128)), 'row', 0, 0, ti...  7.06 us
    all_to_all x1, starting transfers between devices, shards(): own = lax.all_to_all(packed[1], ('z', 'depth'), 0, 0, tiled=True)  6.57 us
    ppermute x1, starting transfers between devices, shards(): oth = lax.ppermute(own, 'core', [(0, 1), (1, 0)])  4.73 us
  transfers between devices with their start and end apart: 5, of which 4 were waited for; matrix products, arithmetic and copies ran while one was open for 0% of the time, Pallas kernels for 4%

profile of v15, /device:TPU:1, one launch (start us, length us, event | category | flops | bytes accessed | tf_op | source)
XLA Modules:
  0.0 87.1 jit_solution(5554690017997071930)
XLA Ops:
  0.6 1.5 %pack.1 = (bf16[48,128]{1,0:T(8,128)(2,1)}, bf16[16,48,128]{2,1,0:T(8,128)(2,1)}) custom-call(bf16[64,64]{1,0:T(8,128)(2,1)} %emb_ref.1, f32[16,64]{1,0:T(8,128)} %crd_ref.3), custom_call_target="tpu_custom_call" | custom-call | tf_op jit(solution)/shard_map/pack/pallas_call | solution.py:218
  2.1 8.8 %collective-permute-start = (bf16[48,128]{1,0:T(8,128)(2,1)}, bf16[48,128]{1,0:T(8,128)(2,1)S(1)}, u32[]{:S(2)}, u32[]{:S(2)}) collective-permute-start(bf16[48,128]{1,0:T(8,128)(2,1)} %get-tuple-element.6), channel_id=1, source_target_pairs={{0,0},{1,32},{2,64},{3,96},{4,128},{5,160},{6,192},{7,224},{8,256}... | collective-permute-start | bytes 36872 | tf_op jit(solution)/shard_map/ppermute | solution.py:227
  10.9 6.6 %all-to-all-start = ((bf16[16,48,128]{2,1,0:T(8,128)(2,1)}), bf16[16,48,128]{2,1,0:T(8,128)(2,1)S(1)}, u32[]{:S(2)}, u32[]{:S(2)}) async-start(bf16[16,48,128]{2,1,0:T(8,128)(2,1)} %get-tuple-element.7), calls=%async_computation | async-start | bytes 393216 | tf_op jit(solution)/shard_map/all_to_all | solution.py:228
  17.5 0.0 collective-permute-done.own_ref
  17.5 0.0 copy-start.2
  17.5 0.6 copy-done.2
  18.1 1.4 %spread.1 = bf16[16,48,128]{2,1,0:T(8,128)(2,1)} custom-call(bf16[48,128]{1,0:T(8,128)(2,1)} %copy-done.2), custom_call_target="tpu_custom_call" | custom-call | flops 10000000000 | bytes 100000000 | tf_op jit(solution)/shard_map/spread/pallas_call | solution.py:229
  19.5 8.6 %all-to-all-done.own_ref = bf16[16,48,128]{2,1,0:T(8,128)(2,1)S(1)} async-done(((bf16[16,48,128]{2,1,0:T(8,128)(2,1)}), bf16[16,48,128]{2,1,0:T(8,128)(2,1)S(1)}, u32[]{:S(2)}, u32[]{:S(2)}) %all-to-all-start) | async-done | bytes 196640 | tf_op jit(solution)/shard_map/all_to_all | solution.py:228
  28.1 8.6 %all-to-all-start.1 = ((bf16[16,48,128]{2,1,0:T(8,128)(2,1)}), bf16[16,48,128]{2,1,0:T(8,128)(2,1)S(1)}, u32[]{:S(2)}, u32[]{:S(2)}) async-start(bf16[16,48,128]{2,1,0:T(8,128)(2,1)} %spread.1), calls=%async_computation.1 | async-start | bytes 393216 | tf_op jit(solution)/shard_map/all_to_all | solution.py:237
  36.7 4.7 %collective-permute-start.1 = (bf16[16,48,128]{2,1,0:T(8,128)(2,1)S(1)}, bf16[16,48,128]{2,1,0:T(8,128)(2,1)S(1)}, u32[]{:S(2)}, u32[]{:S(2)}) collective-permute-start(bf16[16,48,128]{2,1,0:T(8,128)(2,1)S(1)} %all-to-all-done.own_ref), channel_id=1, source_target_pairs={{0,2},{2,0},{1,3},{3,1},{4,6},{6,4},{5,7},{7,5},{8,10},{10,8},{9,1... | collective-permute-start | bytes 589832 | tf_op jit(solution)/shard_map/ppermute | solution.py:236
  41.5 1.0 %collective-permute-done.1.oth_ref = bf16[16,48,128]{2,1,0:T(8,128)(2,1)S(1)} collective-permute-done((bf16[16,48,128]{2,1,0:T(8,128)(2,1)S(1)}, bf16[16,48,128]{2,1,0:T(8,128)(2,1)S(1)}, u32[]{:S(2)}, u32[]{:S(2)}) %collective-permute-start.1) | collective-permute-done | bytes 196640 | tf_op jit(solution)/shard_map/ppermute | solution.py:236
  42.5 4.7 %all-to-all-done.1.col_ref = bf16[16,48,128]{2,1,0:T(8,128)(2,1)S(1)} async-done(((bf16[16,48,128]{2,1,0:T(8,128)(2,1)}), bf16[16,48,128]{2,1,0:T(8,128)(2,1)S(1)}, u32[]{:S(2)}, u32[]{:S(2)}) %all-to-all-start.1) | async-done | bytes 196640 | tf_op jit(solution)/shard_map/all_to_all | solution.py:237
  47.3 8.5 %pairs.1 = f32[32,1,1280]{2,1,0:T(1,128)S(1)} custom-call(bf16[16,48,128]{2,1,0:T(8,128)(2,1)S(1)} %all-to-all-done.own_ref, bf16[16,48,128]{2,1,0:T(8,128)(2,1)S(1)} %collective-permute-done.1.oth_ref, bf16[16,48,128]{2,1,0:T(8,128)(2,1)S(1)} %all-to-all-done.1.col_ref, bf16[2048,1024]{1,0:T(8,128)(2,1)} %w_hbm.1), custom_call_target="tpu_custom_call" | custom-call | tf_op jit(solution)/shard_map/pairs/pallas_call | solution.py:241
  55.7 16.6 %all_to_all.20.part_ref = f32[32,1,1280]{2,1,0:T(1,128)S(1)} all-to-all(f32[32,1,1280]{2,1,0:T(1,128)S(1)} %pairs.1), channel_id=1, replica_groups=mesh['row'=16,'z'=8,'core'=2,'depth'=2] {'z','core','depth'}, dimensions={0} | all-to-all | bytes 327680 | tf_op jit(solution)/shard_map/all_to_all | solution.py:266
  72.3 0.0 copy-start
  72.4 0.6 broadcast_in_dim.2
  73.0 3.5 %all-to-all-start.3 = ((f32[16,1,128]{2,1,0:T(1,128)}), f32[16,1,128]{2,1,0:T(1,128)S(1)}, u32[]{:S(2)}, u32[]{:S(2)}) async-start(f32[16,1,128]{2,1,0:T(1,128)} %broadcast_in_dim.2), calls=%async_computation.3 | async-start | bytes 16384 | tf_op jit(solution)/shard_map/all_to_all | solution.py:268
  76.5 0.0 copy-done
  76.5 1.7 %finish.1 = f32[16,64]{1,0:T(8,128)} custom-call(f32[32,1,1280]{2,1,0:T(1,128)} %copy-done, f32[16,64]{1,0:T(8,128)} %crd_ref.3), custom_call_target="tpu_custom_call" | custom-call | flops 100000 | bytes 200000 | tf_op jit(solution)/shard_map/finish/pallas_call | solution.py:269
  78.2 7.1 %all-to-all-done.3.part_ref = f32[16,1,128]{2,1,0:T(1,128)S(1)} async-done(((f32[16,1,128]{2,1,0:T(1,128)}), f32[16,1,128]{2,1,0:T(1,128)S(1)}, u32[]{:S(2)}, u32[]{:S(2)}) %all-to-all-start.3) | async-done | bytes 8224 | tf_op jit(solution)/shard_map/all_to_all | solution.py:268
  85.3 0.0 copy-start.1
  85.3 0.6 copy-done.1
  85.8 1.3 %stress.1 = f32[1,1]{1,0:T(1,128)} custom-call(f32[16,1,128]{2,1,0:T(1,128)} %copy-done.1), custom_call_target="tpu_custom_call" | custom-call | tf_op jit(solution)/shard_map/stress/pallas_call | solution.py:275
  (1 shorter events, 0.0 us)
Async XLA Ops:
  2.1 15.4 %collective-permute-start = (bf16[48,128]{1,0:T(8,128)(2,1)}, bf16[48,128]{1,0:T(8,128)(2,1)S(1)}, u32[]{:S(2)}, u32[]{:S(2)}) collective-permute-start(bf16[48,128]{1,0:T(8,128)(2,1)} %get-tuple-element.6), channel_id=1, source_target_pairs={{0,0},{1,32},{2,64},{3,96},{4,128},{5,160},{6,192},{7,224},{8,256}... | collective-permute-start | bytes 36872 | tf_op jit(solution)/shard_map/ppermute | solution.py:227
  10.9 17.2 %all-to-all-start = ((bf16[16,48,128]{2,1,0:T(8,128)(2,1)}), bf16[16,48,128]{2,1,0:T(8,128)(2,1)S(1)}, u32[]{:S(2)}, u32[]{:S(2)}) async-start(bf16[16,48,128]{2,1,0:T(8,128)(2,1)} %get-tuple-element.7), calls=%async_computation | async-start | bytes 393216 | tf_op jit(solution)/shard_map/all_to_all | solution.py:228
  17.5 0.6 copy-start.2
  28.1 19.2 %all-to-all-start.1 = ((bf16[16,48,128]{2,1,0:T(8,128)(2,1)}), bf16[16,48,128]{2,1,0:T(8,128)(2,1)S(1)}, u32[]{:S(2)}, u32[]{:S(2)}) async-start(bf16[16,48,128]{2,1,0:T(8,128)(2,1)} %spread.1), calls=%async_computation.1 | async-start | bytes 393216 | tf_op jit(solution)/shard_map/all_to_all | solution.py:237
  36.7 5.8 %collective-permute-start.1 = (bf16[16,48,128]{2,1,0:T(8,128)(2,1)S(1)}, bf16[16,48,128]{2,1,0:T(8,128)(2,1)S(1)}, u32[]{:S(2)}, u32[]{:S(2)}) collective-permute-start(bf16[16,48,128]{2,1,0:T(8,128)(2,1)S(1)} %all-to-all-done.own_ref), channel_id=1, source_target_pairs={{0,2},{2,0},{1,3},{3,1},{4,6},{6,4},{5,7},{7,5},{8,10},{10,8},{9,1... | collective-permute-start | bytes 589832 | tf_op jit(solution)/shard_map/ppermute | solution.py:236
  72.3 4.2 %copy-start = (f32[32,1,1280]{2,1,0:T(1,128)}, f32[32,1,1280]{2,1,0:T(1,128)S(1)}, u32[]{:S(2)}) copy-start(f32[32,1,1280]{2,1,0:T(1,128)S(1)} %all_to_all.20.part_ref) | copy-start | bytes 491524
  73.0 12.3 %all-to-all-start.3 = ((f32[16,1,128]{2,1,0:T(1,128)}), f32[16,1,128]{2,1,0:T(1,128)S(1)}, u32[]{:S(2)}, u32[]{:S(2)}) async-start(f32[16,1,128]{2,1,0:T(1,128)} %broadcast_in_dim.2), calls=%async_computation.3 | async-start | bytes 16384 | tf_op jit(solution)/shard_map/all_to_all | solution.py:268
  85.3 0.6 copy-start.1

commit v16 on v15

--- a/solution.py
+++ b/solution.py
@@ -72,7 +72,7 @@
         out_ref[k] = own
 
 
-def pairs_kernel(own_ref, oth_ref, col_ref, w_hbm, out_ref, w_ref, f_scr, x_scr, flat_scr, rows_scr, feat_scr, c_scr, f_tiles, x_tiles, sems):
+def pairs_kernel(own_ref, oth_ref, col_ref, w_hbm, out_ref, w_ref, f_scr, x_scr, flat_scr, rows_scr, feat_scr, acc_scr, sum_scr, c_scr, f_tiles, x_tiles, sems):
     total_rows, total = w_ref.shape
     tm = c_scr.shape[0]
     tn = min(256, total)
@@ -127,32 +127,15 @@
 
     tiles = [slice(start, start + tn) for start in range(0, total, tn)]
 
-    def block(i, slot, mis, scl, ahead=2):
-        fetch(i).wait()
-        bent = jnp.dot(form_f, feat_scr[slot], preferred_element_type=F32)
-        base = i * tm
-        acc = jnp.zeros((48, tm), F32)
-        wacc = jnp.zeros((LANES, tm), F32)
-        for n in range(len(tiles) + 1):
-            if n < len(tiles):
-                cut = tiles[n]
-                if ahead > 0:
-                    squares(1 - slot, cut)
-                wb = w_ref[pl.ds(pl.multiple_of(base, tm), tm), cut]
-                wacc += lax.dot_general(flat_scr[:, cut], wb, last, preferred_element_type=F32)
-            if n > 0:
-                old = tiles[n - 1]
-                picked = jnp.concatenate([flat_scr[XH : XH + 32, old], flat_scr[QF:, old]], axis=0)
-                acc += lax.dot_general(picked, c_scr[:, old], last, preferred_element_type=F32)
-            if n < len(tiles):
-                mis = chain(base, slot, cut, mis)
-            if n == 0 and ahead > 1:
-                row_block(i + 2, slot)
-        scl += jnp.sum((bent * wacc).reshape(LANES // 8, 8, tm), axis=0)
-        less = acc[0:32] - wacc[XH : XH + 32]
-        pull = less[0:16] + less[16:32]
-        wsum = wacc[ONE : ONE + 1]
-        rate = acc[32 + ONE - QF : 33 + ONE - QF] - wsum
+    def product(cut):
+        picked = jnp.concatenate([flat_scr[XH : XH + 32, cut], flat_scr[QF:, cut]], axis=0)
+        return lax.dot_general(picked, c_scr[:, cut], last, preferred_element_type=F32)
+
+    def finish(i, slot):
+        acc = acc_scr[slot] + product(tiles[-1])
+        pull = acc[0:16] + acc[16:32]
+        rate = acc[32 + ONE - QF : 33 + ONE - QF]
+        wsum = sum_scr[slot, 0:1]
         for k in range(tm // 64):
             cut = slice(64 * k, 64 * k + 64)
             to = i * (tm // 64) + k
@@ -160,12 +143,40 @@
                 line = jnp.concatenate([pull[j : j + 1, cut], pull[j + 8 : j + 9, cut]], axis=1)
                 out_ref[to, :, 128 * j : 128 * j + 128] = line
             out_ref[to, :, 1024:1152] = jnp.concatenate([rate[:, cut], wsum[:, cut]], axis=1)
+
+    def block(i, slot, mis, scl, ahead=2):
+        fetch(i).wait()
+        bent = jnp.dot(form_f, feat_scr[slot], preferred_element_type=F32)
+        base = i * tm
+        acc = jnp.zeros((48, tm), F32)
+        wacc = jnp.zeros((LANES, tm), F32)
+        for n, cut in enumerate(tiles):
+            if ahead > 0:
+                squares(1 - slot, cut)
+            wb = w_ref[pl.ds(pl.multiple_of(base, tm), tm), cut]
+            wacc += lax.dot_general(flat_scr[:, cut], wb, last, preferred_element_type=F32)
+            if n > 0:
+                acc += product(tiles[n - 1])
+            if n == len(tiles) - 1:
+                scl += jnp.sum((bent * wacc).reshape(LANES // 8, 8, tm), axis=0)
+                acc_scr[slot] = acc - jnp.concatenate([wacc[XH : XH + 32], wacc[QF:]], axis=0)
+                sum_scr[slot] = jnp.broadcast_to(wacc[ONE : ONE + 1], (8, tm))
+            if n == 0 and len(tiles) > 1:
+                finish(jnp.maximum(i - 1, 0), 1 - slot)
+            mis = chain(base, slot, cut, mis)
+            if n == 0 and ahead > 1:
+                row_block(i + 2, slot)
+        if len(tiles) == 1:
+            finish(i, slot)
         return mis, scl
 
     def two(k, carry):
         carry = block(2 * k, 0, *carry)
         return block(2 * k + 1, 1, *carry)
 
+    acc_scr[...] = jnp.zeros_like(acc_scr)
+    sum_scr[...] = jnp.zeros_like(sum_scr)
+    c_scr[:, tiles[-1]] = jnp.zeros((tm, tn), BF16)
     row_block(0, 0)
     if steps > 1:
         row_block(1, 1)
@@ -176,6 +187,8 @@
     for i in range(2 * loops, steps):
         carry = block(i, i % 2, *carry, ahead=steps - 1 - i)
     mis, scl = carry
+    if len(tiles) > 1:
+        finish(steps - 1, (steps - 1) % 2)
     mis = jnp.sum(jnp.sum(mis, axis=0, keepdims=True), axis=1, keepdims=True)
     scl = jnp.sum(jnp.sum(scl, axis=0, keepdims=True), axis=1, keepdims=True)
     at = lax.broadcasted_iota(jnp.int32, (1, 128), 1)
@@ -255,6 +268,8 @@
             pltpu.VMEM((LANES, cols), BF16),
             pltpu.VMEM((2, tm, LANES), BF16),
             pltpu.VMEM((2, LANES, tm), BF16),
+            pltpu.VMEM((2, 48, tm), F32),
+            pltpu.VMEM((2, 8, tm), F32),
             pltpu.VMEM((tm, cols), BF16),
             pltpu.VMEM((2, tm, cols), F32),
             pltpu.VMEM((2, tm, cols), F32),

time: 88.1 us -> 88.4 us (level)
  no operation moved by 1% of the time
where the time goes in v16:
time: 88.4 us; the launch traced here: 87.4 us
  starting transfers between devices  32.2 us (36%)
  waiting for transfers between devices  21.4 us (24%)
  blocking collectives  16.6 us (19%)
  Pallas kernels  14.6 us (17%)
  local copies, waits for them, and re-layouts  1.79 us (2%)
    all_to_all x1, blocking collectives, shards(): parts = lax.all_to_all(parts, ('z', 'core', 'depth'), 0, 0, tiled=True)  16.6 us
    ppermute x1, starting transfers between devices, shards(): moved = lax.ppermute(packed[0], ('row', 'z', 'core', 'depth'), moves)  8.83 us
    pallas_call x1, Pallas kernels, shards(): pl.pallas_call(pairs_kernel, in_specs=[vmem, vmem, vmem, pl.BlockSpec(mem...  8.76 us
    all_to_all x1, starting transfers between devices, shards(): t_cols = lax.all_to_all(moved, 'row', 0, 0, tiled=True)  8.63 us
    all_to_all x1, waiting for transfers between devices, shards(): own = lax.all_to_all(packed[1], ('z', 'depth'), 0, 0, tiled=True)  8.58 us
    all_to_all x1, waiting for transfers between devices, shards(): lax.all_to_all(jnp.broadcast_to(shares, (n_row, 1, 128)), 'row', 0, 0, ti...  7.06 us
    all_to_all x1, starting transfers between devices, shards(): own = lax.all_to_all(packed[1], ('z', 'depth'), 0, 0, tiled=True)  6.57 us
    ppermute x1, starting transfers between devices, shards(): oth = lax.ppermute(own, 'core', [(0, 1), (1, 0)])  4.73 us
  transfers between devices with their start and end apart: 5, of which 4 were waited for; matrix products, arithmetic and copies ran while one was open for 0% of the time, Pallas kernels for 4%

profile of v16, /device:TPU:1, one launch (start us, length us, event | category | flops | bytes accessed | tf_op | source)
XLA Modules:
  0.0 87.4 jit_solution(11299771563537346750)
XLA Ops:
  0.6 1.5 %pack.1 = (bf16[48,128]{1,0:T(8,128)(2,1)}, bf16[16,48,128]{2,1,0:T(8,128)(2,1)}) custom-call(bf16[64,64]{1,0:T(8,128)(2,1)} %emb_ref.1, f32[16,64]{1,0:T(8,128)} %crd_ref.3), custom_call_target="tpu_custom_call" | custom-call | tf_op jit(solution)/shard_map/pack/pallas_call | solution.py:231
  2.1 8.8 %collective-permute-start = (bf16[48,128]{1,0:T(8,128)(2,1)}, bf16[48,128]{1,0:T(8,128)(2,1)S(1)}, u32[]{:S(2)}, u32[]{:S(2)}) collective-permute-start(bf16[48,128]{1,0:T(8,128)(2,1)} %get-tuple-element.6), channel_id=1, source_target_pairs={{0,0},{1,32},{2,64},{3,96},{4,128},{5,160},{6,192},{7,224},{8,256}... | collective-permute-start | bytes 36872 | tf_op jit(solution)/shard_map/ppermute | solution.py:240
  10.9 6.6 %all-to-all-start = ((bf16[16,48,128]{2,1,0:T(8,128)(2,1)}), bf16[16,48,128]{2,1,0:T(8,128)(2,1)S(1)}, u32[]{:S(2)}, u32[]{:S(2)}) async-start(bf16[16,48,128]{2,1,0:T(8,128)(2,1)} %get-tuple-element.7), calls=%async_computation | async-start | bytes 393216 | tf_op jit(solution)/shard_map/all_to_all | solution.py:241
  17.5 0.0 collective-permute-done.own_ref
  17.5 0.0 copy-start.2
  17.5 0.6 copy-done.2
  18.1 1.4 %spread.1 = bf16[16,48,128]{2,1,0:T(8,128)(2,1)} custom-call(bf16[48,128]{1,0:T(8,128)(2,1)} %copy-done.2), custom_call_target="tpu_custom_call" | custom-call | flops 10000000000 | bytes 100000000 | tf_op jit(solution)/shard_map/spread/pallas_call | solution.py:242
  19.5 8.6 %all-to-all-done.own_ref = bf16[16,48,128]{2,1,0:T(8,128)(2,1)S(1)} async-done(((bf16[16,48,128]{2,1,0:T(8,128)(2,1)}), bf16[16,48,128]{2,1,0:T(8,128)(2,1)S(1)}, u32[]{:S(2)}, u32[]{:S(2)}) %all-to-all-start) | async-done | bytes 196640 | tf_op jit(solution)/shard_map/all_to_all | solution.py:241
  28.1 8.6 %all-to-all-start.1 = ((bf16[16,48,128]{2,1,0:T(8,128)(2,1)}), bf16[16,48,128]{2,1,0:T(8,128)(2,1)S(1)}, u32[]{:S(2)}, u32[]{:S(2)}) async-start(bf16[16,48,128]{2,1,0:T(8,128)(2,1)} %spread.1), calls=%async_computation.1 | async-start | bytes 393216 | tf_op jit(solution)/shard_map/all_to_all | solution.py:250
  36.7 4.7 %collective-permute-start.1 = (bf16[16,48,128]{2,1,0:T(8,128)(2,1)S(1)}, bf16[16,48,128]{2,1,0:T(8,128)(2,1)S(1)}, u32[]{:S(2)}, u32[]{:S(2)}) collective-permute-start(bf16[16,48,128]{2,1,0:T(8,128)(2,1)S(1)} %all-to-all-done.own_ref), channel_id=1, source_target_pairs={{0,2},{2,0},{1,3},{3,1},{4,6},{6,4},{5,7},{7,5},{8,10},{10,8},{9,1... | collective-permute-start | bytes 589832 | tf_op jit(solution)/shard_map/ppermute | solution.py:249
  41.5 1.0 %collective-permute-done.1.oth_ref = bf16[16,48,128]{2,1,0:T(8,128)(2,1)S(1)} collective-permute-done((bf16[16,48,128]{2,1,0:T(8,128)(2,1)S(1)}, bf16[16,48,128]{2,1,0:T(8,128)(2,1)S(1)}, u32[]{:S(2)}, u32[]{:S(2)}) %collective-permute-start.1) | collective-permute-done | bytes 196640 | tf_op jit(solution)/shard_map/ppermute | solution.py:249
  42.5 4.7 %all-to-all-done.1.col_ref = bf16[16,48,128]{2,1,0:T(8,128)(2,1)S(1)} async-done(((bf16[16,48,128]{2,1,0:T(8,128)(2,1)}), bf16[16,48,128]{2,1,0:T(8,128)(2,1)S(1)}, u32[]{:S(2)}, u32[]{:S(2)}) %all-to-all-start.1) | async-done | bytes 196640 | tf_op jit(solution)/shard_map/all_to_all | solution.py:250
  47.3 8.8 %pairs.1 = f32[32,1,1280]{2,1,0:T(1,128)S(1)} custom-call(bf16[16,48,128]{2,1,0:T(8,128)(2,1)S(1)} %all-to-all-done.own_ref, bf16[16,48,128]{2,1,0:T(8,128)(2,1)S(1)} %collective-permute-done.1.oth_ref, bf16[16,48,128]{2,1,0:T(8,128)(2,1)S(1)} %all-to-all-done.1.col_ref, bf16[2048,1024]{1,0:T(8,128)(2,1)} %w_hbm.1), custom_call_target="tpu_custom_call" | custom-call | tf_op jit(solution)/shard_map/pairs/pallas_call | solution.py:254
  56.0 16.6 %all_to_all.20.part_ref = f32[32,1,1280]{2,1,0:T(1,128)S(1)} all-to-all(f32[32,1,1280]{2,1,0:T(1,128)S(1)} %pairs.1), channel_id=1, replica_groups=mesh['row'=16,'z'=8,'core'=2,'depth'=2] {'z','core','depth'}, dimensions={0} | all-to-all | bytes 327680 | tf_op jit(solution)/shard_map/all_to_all | solution.py:281
  72.6 0.0 copy-start
  72.7 0.6 broadcast_in_dim.2
  73.3 3.5 %all-to-all-start.3 = ((f32[16,1,128]{2,1,0:T(1,128)}), f32[16,1,128]{2,1,0:T(1,128)S(1)}, u32[]{:S(2)}, u32[]{:S(2)}) async-start(f32[16,1,128]{2,1,0:T(1,128)} %broadcast_in_dim.2), calls=%async_computation.3 | async-start | bytes 16384 | tf_op jit(solution)/shard_map/all_to_all | solution.py:283
  76.8 0.0 copy-done
  76.8 1.7 %finish.1 = f32[16,64]{1,0:T(8,128)} custom-call(f32[32,1,1280]{2,1,0:T(1,128)} %copy-done, f32[16,64]{1,0:T(8,128)} %crd_ref.3), custom_call_target="tpu_custom_call" | custom-call | flops 100000 | bytes 200000 | tf_op jit(solution)/shard_map/finish/pallas_call | solution.py:284
  78.5 7.1 %all-to-all-done.3.part_ref = f32[16,1,128]{2,1,0:T(1,128)S(1)} async-done(((f32[16,1,128]{2,1,0:T(1,128)}), f32[16,1,128]{2,1,0:T(1,128)S(1)}, u32[]{:S(2)}, u32[]{:S(2)}) %all-to-all-start.3) | async-done | bytes 8224 | tf_op jit(solution)/shard_map/all_to_all | solution.py:283
  85.5 0.0 copy-start.1
  85.5 0.6 copy-done.1
  86.1 1.3 %stress.1 = f32[1,1]{1,0:T(1,128)} custom-call(f32[16,1,128]{2,1,0:T(1,128)} %copy-done.1), custom_call_target="tpu_custom_call" | custom-call | tf_op jit(solution)/shard_map/stress/pallas_call | solution.py:290
  (1 shorter events, 0.0 us)
Async XLA Ops:
  2.1 15.4 %collective-permute-start = (bf16[48,128]{1,0:T(8,128)(2,1)}, bf16[48,128]{1,0:T(8,128)(2,1)S(1)}, u32[]{:S(2)}, u32[]{:S(2)}) collective-permute-start(bf16[48,128]{1,0:T(8,128)(2,1)} %get-tuple-element.6), channel_id=1, source_target_pairs={{0,0},{1,32},{2,64},{3,96},{4,128},{5,160},{6,192},{7,224},{8,256}... | collective-permute-start | bytes 36872 | tf_op jit(solution)/shard_map/ppermute | solution.py:240
  10.9 17.2 %all-to-all-start = ((bf16[16,48,128]{2,1,0:T(8,128)(2,1)}), bf16[16,48,128]{2,1,0:T(8,128)(2,1)S(1)}, u32[]{:S(2)}, u32[]{:S(2)}) async-start(bf16[16,48,128]{2,1,0:T(8,128)(2,1)} %get-tuple-element.7), calls=%async_computation | async-start | bytes 393216 | tf_op jit(solution)/shard_map/all_to_all | solution.py:241
  17.5 0.6 copy-start.2
  28.1 19.2 %all-to-all-start.1 = ((bf16[16,48,128]{2,1,0:T(8,128)(2,1)}), bf16[16,48,128]{2,1,0:T(8,128)(2,1)S(1)}, u32[]{:S(2)}, u32[]{:S(2)}) async-start(bf16[16,48,128]{2,1,0:T(8,128)(2,1)} %spread.1), calls=%async_computation.1 | async-start | bytes 393216 | tf_op jit(solution)/shard_map/all_to_all | solution.py:250
  36.7 5.8 %collective-permute-start.1 = (bf16[16,48,128]{2,1,0:T(8,128)(2,1)S(1)}, bf16[16,48,128]{2,1,0:T(8,128)(2,1)S(1)}, u32[]{:S(2)}, u32[]{:S(2)}) collective-permute-start(bf16[16,48,128]{2,1,0:T(8,128)(2,1)S(1)} %all-to-all-done.own_ref), channel_id=1, source_target_pairs={{0,2},{2,0},{1,3},{3,1},{4,6},{6,4},{5,7},{7,5},{8,10},{10,8},{9,1... | collective-permute-start | bytes 589832 | tf_op jit(solution)/shard_map/ppermute | solution.py:249
  72.6 4.2 %copy-start = (f32[32,1,1280]{2,1,0:T(1,128)}, f32[32,1,1280]{2,1,0:T(1,128)S(1)}, u32[]{:S(2)}) copy-start(f32[32,1,1280]{2,1,0:T(1,128)S(1)} %all_to_all.20.part_ref) | copy-start | bytes 491524
  73.3 12.3 %all-to-all-start.3 = ((f32[16,1,128]{2,1,0:T(1,128)}), f32[16,1,128]{2,1,0:T(1,128)S(1)}, u32[]{:S(2)}, u32[]{:S(2)}) async-start(f32[16,1,128]{2,1,0:T(1,128)} %broadcast_in_dim.2), calls=%async_computation.3 | async-start | bytes 16384 | tf_op jit(solution)/shard_map/all_to_all | solution.py:283
  85.5 0.6 copy-start.1
